TPU v7x, 32 devices: a whole 2x2x4 slice. The times are simulated.
32 devices in a mesh: grp: 2 (over core), dom: 16 (over z, y, x).
Axes of the slice: x: 2, y: 2, z: 4, core: 2. Of those that a mesh axis runs over, the one named last changes fastest.
Arguments:
- flow_temp: float32 [128, 512, 256], P(None, ('grp', 'dom')), may hold values from -6 to 6
- velocity: bfloat16 [3, 128, 512, 256], P(None, None, ('grp', 'dom')), may hold values from -2.5 to 2.5
- heat_release: bfloat16 [128, 512, 256], P(None, ('grp', 'dom')), may hold values from 0.049804688 to 2
- solid_temp: float32 [32, 512, 256], P(None, ('grp', 'dom')), may hold values from -6 to 6
- conductivity: float32 [32, 512, 256], P(None, ('grp', 'dom')), may hold values from 0.5 to 2
- interp_table: float32 [16, 16, 1024], replicated, may hold values from -0.375 to 0.375
- flow_patch: int32 [131072], P(('grp', 'dom')), may hold values from 0 to 255
- solid_device: int32 [131072, 1], P(('grp', 'dom')), may hold values from 0 to 31; in each aligned block of 4096 rows (0 to 4095, 4096 to 8191, ...) at most 256 rows name the same one
- solid_patch: int32 [131072], P(('grp', 'dom')), may hold values from 0 to 255
- block_index: int32 [131072], P(('grp', 'dom')), may hold values from 0 to 1023
Outputs:
- flow_out: float32 [128, 512, 256], P(None, ('grp', 'dom'))
- solid_out: float32 [32, 512, 256], P(None, ('grp', 'dom'))
Inputs may be any that keep to these rules, and one draw needn't show every extreme that they name: `solid_device`: within the 4096 rows of one device no liner device is named more than 256 times, and some liner device is named exactly 256 times.
All inputs are finite; a program needn't handle non-finite values.
Results may differ from a plain program's by a relative error of at most 0.00115.
Values may be sent and summed in bfloat16 or wider, within the bound.
No kernel may reach another device: no remote copies, remote signals or barrier semaphores. Data moves between devices by JAX's collectives and lax.ppermute only.
A program may use at most 128 MiB of HBM per device.

v0:
```python
import jax
import jax.numpy as jnp
from jax import lax
from jax.sharding import PartitionSpec as P

SUBCYCLES = 4


DIFFUSION = 0.8
TIMESTEP = 0.12
FILM_COEFF = 1.0
CONDUCT_RATE = 0.08
FLUX_GAIN = 0.25


def with_halo(shard, sides, width):
    for axis, dim in sides:
        peers, length = (lax.axis_size(axis), shard.shape[dim])
        up = [(i, (i + 1) % peers) for i in range(peers)]
        down = [(j, i) for i, j in up]
        last = lax.slice_in_dim(shard, length - width, length, axis=dim)
        leading = lax.slice_in_dim(shard, 0, width, axis=dim)
        before = lax.ppermute(last, axis, up)
        after = lax.ppermute(leading, axis, down)
        shard = jnp.concatenate([before, shard, after], axis=dim)
    return shard


def upwind(component, centre, lower_side, upper_side):
    return jnp.maximum(component, 0.0) * (centre - lower_side) + jnp.minimum(component, 0.0) * (
        upper_side - centre
    )


def tendency(centre, zbelow, zabove, xbelow, xabove, velocity, source):
    ybelow = jnp.roll(centre, 1, axis=2)
    yabove = jnp.roll(centre, -1, axis=2)
    advect = upwind(velocity[0], centre, zbelow, zabove) + upwind(
        velocity[1], centre, xbelow, xabove
    )
    advect = advect + upwind(velocity[2], centre, ybelow, yabove)
    spread = zbelow + zabove + xbelow + xabove + ybelow + yabove - 6.0 * centre
    return source - advect + DIFFUSION * spread


def flow_tendency(current, wall_face, speeds, source):
    padded = with_halo(current.astype(jnp.bfloat16), ((("grp", "dom"), 1),), 1).astype(
        current.dtype
    )
    zbelow = jnp.concatenate([jnp.zeros_like(current[:1]), current[:-1]], 0)
    zabove = jnp.concatenate([current[1:], wall_face[None]], 0)
    return tendency(current, zbelow, zabove, padded[:, :-2], padded[:, 2:], speeds, source)


def solid_update(current, xbelow, xabove, conduct, flux_face):
    zbelow = jnp.concatenate([current[:1], current[:-1]], 0)
    zabove = jnp.concatenate([current[1:], jnp.zeros_like(current[:1])], 0)
    ybelow = jnp.roll(current, 1, axis=2)
    yabove = jnp.roll(current, -1, axis=2)
    spread = zbelow + zabove + xbelow + xabove + ybelow + yabove - 6.0 * current
    updated = current + CONDUCT_RATE * conduct * spread
    return updated + jnp.concatenate(
        [(FLUX_GAIN * flux_face)[None], jnp.zeros_like(current[1:])], 0
    )


def route_ids(request):
    return lax.all_to_all(request, ("grp", "dom"), split_axis=0, concat_axis=0, tiled=True)


def route_values(values):
    return lax.all_to_all(values, ("grp", "dom"), split_axis=0, concat_axis=0, tiled=True)


def body(
    flow_temp,
    velocity,
    heat_release,
    solid_temp,
    conductivity,
    interp_table,
    flow_patch,
    solid_device,
    solid_patch,
    block_index,
):
    rows_x = flow_temp.shape[1]
    devices = lax.axis_size(("grp", "dom"))
    patch_count = rows_x * flow_temp.shape[2] // 16
    solid_rows = solid_temp[0].reshape(patch_count, 16)
    table_rows = interp_table.reshape(256, -1).T
    weights = jnp.take(table_rows, block_index, axis=0).reshape(-1, 16, 16)
    destination = solid_device[:, 0]
    capacity = max(2, 2 * block_index.shape[0] // devices)
    member = (destination[:, None] == jnp.arange(devices, dtype=jnp.int32)[None, :]).astype(
        jnp.int32
    )
    before = jnp.cumsum(member, axis=0) - member
    ranking = jnp.sum(before * member, axis=1)
    slot_index = destination * capacity + ranking
    request = jnp.zeros((devices * capacity,), jnp.int32).at[slot_index].set(solid_patch)
    asked_ids = route_ids(request)
    answer = jnp.take(solid_rows, asked_ids, axis=0)
    returned = route_values(answer.reshape(-1)).reshape(-1, 16)
    fetched = jnp.take(returned, slot_index, axis=0)
    forward = jnp.sum(weights * fetched[:, None, :], axis=2)
    wall_rows = jnp.zeros((patch_count, 16), jnp.float32).at[flow_patch].add(forward)
    wall_face = wall_rows.reshape(rows_x, -1)
    speeds = velocity.astype(jnp.float32)
    source = heat_release.astype(jnp.float32)
    predictor = flow_temp + TIMESTEP * flow_tendency(flow_temp, wall_face, speeds, source)
    flow_out = 0.5 * flow_temp + 0.5 * (
        predictor + TIMESTEP * flow_tendency(predictor, wall_face, speeds, source)
    )
    flux_rows = (FILM_COEFF * (flow_out[-1] - wall_face)).reshape(patch_count, 16)
    gathered_flux = jnp.take(flux_rows, flow_patch, axis=0)
    backward = jnp.sum(weights * gathered_flux[:, :, None], axis=1)
    sending = jnp.zeros((devices * capacity, 16), jnp.float32).at[slot_index].set(backward)
    arrived = route_values(sending.reshape(-1)).reshape(-1, 16)
    solid_flux = jnp.zeros((patch_count, 16), jnp.float32).at[asked_ids].add(arrived)
    flux_face = solid_flux.reshape(rows_x, -1)
    current = solid_temp
    for substep in range(SUBCYCLES):
        padded = with_halo(current.astype(jnp.bfloat16), ((("grp", "dom"), 1),), 1).astype(
            current.dtype
        )
        current = solid_update(current, padded[:, :-2], padded[:, 2:], conductivity, flux_face)
    return (flow_out, current)


def solution(mesh):
    placed = (
        P(None, ("grp", "dom"), None),
        P(None, None, ("grp", "dom"), None),
        P(None, ("grp", "dom"), None),
        P(None, ("grp", "dom"), None),
        P(None, ("grp", "dom"), None),
        P(),
        P(("grp", "dom")),
        P(("grp", "dom"), None),
        P(("grp", "dom")),
        P(("grp", "dom")),
    )
    return jax.shard_map(
        body,
        mesh=mesh,
        in_specs=placed,
        out_specs=(P(None, ("grp", "dom"), None), P(None, ("grp", "dom"), None)),
        check_vma=False,
    )
```

profile of v0, /device:TPU:1, one launch (start us, length us, event | category | flops | bytes accessed | tf_op | source)
XLA Modules:
  0.0 362.2 jit_solution(1273704490232834242)
XLA Ops:
  0.6 0.9 fusion.43
  1.6 9.2 %reduce-window.6 = s32[32,32,128]{2,1,0:T(8,128)S(1)} reduce-window(s32[32,32,128]{2,1,0:T(8,128)S(1)} %fusion.43, s32[]{:T(128)} %constant.35.clone.1), window={size=1x1x128 pad=0_0x0_0x127_0}, to_apply=%region_0.1 | reduce-window | flops 16646144 | bytes 1048580 | tf_op jit(solution)/shard_map/reduce-window
  10.8 0.8 slice_reduce_fusion
  12.4 0.7 and_reduce_fusion
  13.1 16.3 %scatter_custom_fusion = s32[8192]{0:T(1024)} fusion(s32[4096]{0:T(1024)S(1)} %bitcast.116, s32[4096]{0:T(1024)} %param.18, s32[]{:T(128)} %constant.35.clone.1), kind=kCustom, calls=%fused_computation.123 | custom fusion | bytes 33280 | tf_op jit(solution)/shard_map/scatter | solution.py:101
  29.3 7.1 %all-to-all-start = ((s32[32,256,1]{1,2,0:T(1,128)}), s32[32,256,1]{1,2,0:T(1,128)S(1)}, u32[]{:S(2)}, u32[]{:S(2)}) async-start(s32[32,256,1]{1,2,0:T(1,128)} %bitcast.10), calls=%async_computation | async-start | bytes 65536 | tf_op jit(solution)/shard_map/all_to_all | solution.py:68
  36.6 1.0 copy-done.4
  37.6 0.9 fusion.63
  38.5 1.4 collective-permute-start
  39.9 4.0 %collective-permute-start.1 = (bf16[128,1,256]{2,1,0:T(2,128)(2,1)}, bf16[128,1,256]{2,1,0:T(2,128)(2,1)}, u32[]{:S(2)}, u32[]{:S(2)}) collective-permute-start(bf16[128,1,256]{2,1,0:T(2,128)(2,1)} %get-tuple-element.27), channel_id=1, source_target_pairs={{1,0},{2,1},{3,2},{4,3},{5,4},{6,5},{7,6},{8,7},{9,8},{10,9},{11,1... | collective-permute-start | bytes 196616 | tf_op jit(solution)/shard_map/ppermute | solution.py:24
  44.4 2.6 fusion.59
  47.0 1.6 fusion.60
  49.9 27.7 %gather_fusion.1 = f32[8192,16]{1,0:T(8,128)} fusion(f32[256,16]{1,0:T(8,128)S(1)} %reshape_squeeze.3, s32[8192]{0:T(1024)S(1)} %broadcast_clamp_fusion), kind=kCustom, calls=%fused_computation.1 | custom fusion | bytes 1081344 | tf_op jit(solution)/shard_map/jit(_take)/gather | solution.py:103
  77.6 4.7 %gather.23 = f32[32,4096,1]{1,0,2:T(8,128)S(1)} reshape(f32[8192,16]{1,0:T(8,128)} %gather_fusion.1) | data formatting | bytes 1048576 | tf_op jit(solution)/shard_map/jit(_take)/gather | solution.py:103
  82.3 1.9 copy.40
  84.4 3.1 bitcast_select_fusion
  87.5 2.6 copy.41
  90.1 3.5 all-to-all-start.1
  94.1 2.8 fusion.61
  97.5 1.7 copy.36
  99.2 16.1 %gather_fusion = f32[4096,256]{1,0:T(8,128)} fusion(f32[1024,256]{1,0:T(8,128)S(1)} %bitcast.103, s32[4096]{0:T(1024)S(1)} %fusion.50), kind=kCustom, calls=%fused_computation | custom fusion | bytes 8404992 | tf_op jit(solution)/shard_map/jit(_take)/gather | solution.py:92
  115.3 5.6 %copy.37 = f32[4096,256]{0,1:T(8,128)} copy(f32[4096,256]{1,0:T(8,128)} %gather_fusion) | data formatting | bytes 8388608 | tf_op jit(solution)/shard_map/jit(_take)/gather | solution.py:92
  120.9 5.5 %convert_element_type.50 = f32[3,128,16,256]{3,2,1,0:T(8,128)} convert(bf16[3,128,16,256]{3,2,1,0:T(8,128)(2,1)} %param.11) | non-fusion elementwise | flops 1572864 | bytes 9437184 | tf_op jit(solution)/shard_map/convert_element_type | solution.py:109
  126.4 3.4 maximum_convert_fusion
  129.8 2.3 reduce.2
  132.1 2.8 reshape.183
  134.9 16.3 %gather_fusion.2 = f32[4096,16]{1,0:T(8,128)} fusion(f32[8192,16]{1,0:T(8,128)} %reshape.183, s32[4096]{0:T(1024)S(1)} %copy-done.17), kind=kCustom, calls=%fused_computation.2 | custom fusion | bytes 540672 | tf_op jit(solution)/shard_map/jit(_take)/gather | solution.py:105
  151.2 4.7 %broadcast_select_fusion.1 = f32[4096,16]{1,0:T(8,128)} fusion(f32[4096,16]{1,0:T(8,128)} %gather_fusion.2, pred[4096]{0:T(1024)(128)(4,1)S(1)} %copy-done.21), kind=kLoop, calls=%fused_computation.64 | loop fusion | flops 65536 | bytes 528384 | tf_op jit(solution)/shard_map/jit(_take)/select_n | solution.py:105
  155.9 2.2 copy.42
  158.1 3.8 %multiply_reduce_fusion.1 = f32[4096,16]{0,1:T(8,128)} fusion(f32[4096,16]{0,1:T(8,128)S(1)} %copy.42, pred[4096]{0:T(1024)(128)(4,1)S(1)} %copy-done.18, f32[4096,256]{0,1:T(8,128)} %copy.37), kind=kLoop, calls=%fused_computation.9 | loop fusion | flops 3080192 | bytes 4722688 | tf_op jit(solution)/shard_map/reduce_sum | solution.py:106
  161.9 3.0 copy.43
  164.9 22.9 %scatter_custom_fusion.1 = f32[256,16]{1,0:T(8,128)S(1)} fusion(s32[4096]{0:T(1024)} %get-tuple-element.61, f32[4096,16]{1,0:T(8,128)} %copy.43, f32[]{:T(128)} %constant.34.clone.1), kind=kCustom, calls=%fused_computation.116 | custom fusion | flops 65536 | bytes 16896 | tf_op jit(solution)/shard_map/scatter-add | solution.py:107
  187.9 9.1 %fusion.54 = (bf16[128,16,256]{2,1,0:T(8,128)(2,1)S(1)}, f32[128,16,256]{2,1,0:T(8,128)S(1)}) fusion(f32[128,16,256]{2,1,0:T(8,128)S(1)} %copy-done, f32[128,16,1]{2,1,0:T(8,128)} %get-tuple-element.21, f32[128,16,255]{2,1,0:T(8,128)} %get-tuple-element.23, f32[128,16,255]{2,1,0:T(8,128)} %get-tuple-element.22, f32[128,16,1]{2,1,0:T(8,128)S(1)} %copy-done.6, ...), kind=kLoop, calls=%fused_computation.133 | loop fusion | flops 20971520 | bytes 25149440 | tf_op jit(solution)/shard_map/convert_element_type | solution.py:47
  197.1 0.7 fusion.58
  197.8 0.7 fusion.56
  198.7 1.4 collective-permute-start.2
  200.2 4.1 %collective-permute-start.3 = (bf16[128,1,256]{2,1,0:T(2,128)(2,1)S(1)}, bf16[128,1,256]{2,1,0:T(2,128)(2,1)S(1)}, u32[]{:S(2)}, u32[]{:S(2)}) collective-permute-start(bf16[128,1,256]{2,1,0:T(2,128)(2,1)S(1)} %get-tuple-element.25), channel_id=1, source_target_pairs={{1,0},{2,1},{3,2},{4,3},{5,4},{6,5},{7,6},{8,7},{9,8},{10,9},{11,1... | collective-permute-start | bytes 196616 | tf_op jit(solution)/shard_map/ppermute | solution.py:24
  204.7 3.2 collective-permute-done.2
  207.9 0.8 maximum_convert_fusion.1
  208.7 4.7 %fusion.7 = f32[128,16,256]{2,1,0:T(8,128)} fusion(f32[128,16,256]{2,1,0:T(8,128)S(1)} %copy-done, f32[128,16,256]{2,1,0:T(8,128)S(1)} %get-tuple-element.9, bf16[128,16,256]{2,1,0:T(8,128)(2,1)S(1)} %copy-done.7, f32[128,16,1]{2,1,0:T(8,128)S(1)} %get-tuple-element.15, f32[128,16,255]{2,1,0:T(8,128)S(1)} %get-tuple-element.17, ...), kind=kLoop, calls=%fused_computation.21 | loop fusion | flops 21495808 | bytes 26198016 | tf_op jit(solution)/shard_map/add | solution.py:112
  213.4 0.7 slice.323
  214.2 15.4 %gather_fusion.3 = f32[4096,16]{1,0:T(8,128)} fusion(f32[256,16]{1,0:T(8,128)S(1)} %sub.85, s32[4096]{0:T(1024)} %get-tuple-element.60), kind=kCustom, calls=%fused_computation.3 | custom fusion | bytes 540672 | tf_op jit(solution)/shard_map/jit(_take)/gather | solution.py:116
  229.7 3.6 broadcast_select_fusion
  234.0 2.7 multiply_reduce_fusion
  237.3 12.9 %scatter_custom_fusion.2 = f32[8192,16]{1,0:T(8,128)} fusion(s32[4096]{0:T(1024)} %bitcast.118, f32[4096,16]{1,0:T(8,128)S(1)} %copy.45, f32[]{:T(128)} %constant.34.clone.1), kind=kCustom, calls=%fused_computation.48 | custom fusion | bytes 524800 | tf_op jit(solution)/shard_map/scatter | solution.py:118
  250.2 4.3 %all_to_all.27 = f32[32,4096,1]{1,2,0:T(1,128)} reshape(f32[8192,16]{1,0:T(8,128)} %scatter_custom_fusion.2) | data formatting | bytes 1048576 | tf_op jit(solution)/shard_map/all_to_all | solution.py:72
  254.5 6.0 %all-to-all-start.2 = ((f32[32,4096,1]{1,2,0:T(1,128)}), f32[32,4096,1]{1,2,0:T(1,128)S(1)}, u32[]{:S(2)}, u32[]{:S(2)}) async-start(f32[32,4096,1]{1,2,0:T(1,128)} %all_to_all.27), calls=%async_computation.2 | async-start | bytes 1048576 | tf_op jit(solution)/shard_map/all_to_all | solution.py:72
  260.5 1.4 collective-permute-start.4
  262.0 4.3 %collective-permute-start.5 = (bf16[32,1,256]{2,1,0:T(2,128)(2,1)S(1)}, bf16[32,1,256]{2,1,0:T(2,128)(2,1)S(1)}, u32[]{:S(2)}, u32[]{:S(2)}) collective-permute-start(bf16[32,1,256]{2,1,0:T(2,128)(2,1)S(1)} %get-tuple-element.59), channel_id=1, source_target_pairs={{1,0},{2,1},{3,2},{4,3},{5,4},{6,5},{7,6},{8,7},{9,8},{10,9},{11,1... | collective-permute-start | bytes 49160 | tf_op jit(solution)/shard_map/ppermute | solution.py:24
  266.3 1.1 fusion.73
  267.6 0.9 fusion.74
  268.5 7.2 %collective-permute-done.4 = bf16[32,1,256]{2,1,0:T(2,128)(2,1)S(1)} collective-permute-done((bf16[32,1,256]{2,1,0:T(2,128)(2,1)S(1)}, bf16[32,1,256]{2,1,0:T(2,128)(2,1)S(1)}, u32[]{:S(2)}, u32[]{:S(2)}) %collective-permute-start.4) | collective-permute-done | bytes 16416 | tf_op jit(solution)/shard_map/ppermute | solution.py:23
  275.9 1.2 all-to-all-done.2
  277.1 1.2 reduce.3
  278.4 2.8 reshape.245
  281.2 53.4 %scatter_custom_fusion.3 = f32[256,16]{1,0:T(8,128)S(1)} fusion(s32[8192]{0:T(1024)} %bitcast.113, f32[8192,16]{1,0:T(8,128)} %reshape.245, f32[]{:T(128)} %constant.34.clone.1), kind=kCustom, calls=%fused_computation.114 | custom fusion | flops 131072 | bytes 16896 | tf_op jit(solution)/shard_map/scatter-add | solution.py:120
  334.7 1.8 fusion.53
  337.1 5.3 %collective-permute-start.7 = (bf16[32,1,256]{2,1,0:T(2,128)(2,1)S(1)}, bf16[32,1,256]{2,1,0:T(2,128)(2,1)S(1)}, u32[]{:S(2)}, u32[]{:S(2)}) collective-permute-start(bf16[32,1,256]{2,1,0:T(2,128)(2,1)S(1)} %get-tuple-element.57), channel_id=1, source_target_pairs={{1,0},{2,1},{3,2},{4,3},{5,4},{6,5},{7,6},{8,7},{9,8},{10,9},{11,1... | collective-permute-start | bytes 49160 | tf_op jit(solution)/shard_map/ppermute | solution.py:24
  342.5 1.5 collective-permute-done.6
  345.2 5.4 %collective-permute-start.9 = (bf16[32,1,256]{2,1,0:T(2,128)(2,1)S(1)}, bf16[32,1,256]{2,1,0:T(2,128)(2,1)S(1)}, u32[]{:S(2)}, u32[]{:S(2)}) collective-permute-start(bf16[32,1,256]{2,1,0:T(2,128)(2,1)S(1)} %get-tuple-element.55), channel_id=1, source_target_pairs={{1,0},{2,1},{3,2},{4,3},{5,4},{6,5},{7,6},{8,7},{9,8},{10,9},{11,1... | collective-permute-start | bytes 49160 | tf_op jit(solution)/shard_map/ppermute | solution.py:24
  350.7 1.4 collective-permute-done.8
  353.3 5.5 %collective-permute-start.11 = (bf16[32,1,256]{2,1,0:T(2,128)(2,1)S(1)}, bf16[32,1,256]{2,1,0:T(2,128)(2,1)S(1)}, u32[]{:S(2)}, u32[]{:S(2)}) collective-permute-start(bf16[32,1,256]{2,1,0:T(2,128)(2,1)S(1)} %get-tuple-element.53), channel_id=1, source_target_pairs={{1,0},{2,1},{3,2},{4,3},{5,4},{6,5},{7,6},{8,7},{9,8},{10,9},{11,1... | collective-permute-start | bytes 49160 | tf_op jit(solution)/shard_map/ppermute | solution.py:24
  358.9 1.4 collective-permute-done.10
  360.5 1.3 pad_add_fusion
  (108 shorter events, 10.1 us)
Async XLA Ops:
  0.6 11.4 %copy-start.12 = (s32[4096,1]{0,1:T(1,128)S(1)}, s32[4096,1]{0,1:T(1,128)}, u32[]{:S(2)}) copy-start(s32[4096,1]{0,1:T(1,128)} %param.17) | copy-start | bytes 49156
  0.6 35.8 %copy-start = (f32[128,16,256]{2,1,0:T(8,128)S(1)}, f32[128,16,256]{2,1,0:T(8,128)}, u32[]{:S(2)}) copy-start(f32[128,16,256]{2,1,0:T(8,128)} %param.10) | copy-start | bytes 6291460
  13.1 33.9 %copy-start.16 = (s32[4096,1]{0,1:T(1,128)}, s32[4096,1]{0,1:T(1,128)S(1)}, u32[]{:S(2)}) copy-start(s32[4096,1]{0,1:T(1,128)S(1)} %get-tuple-element.11) | copy-start | bytes 49156
  29.3 20.1 %all-to-all-start = ((s32[32,256,1]{1,2,0:T(1,128)}), s32[32,256,1]{1,2,0:T(1,128)S(1)}, u32[]{:S(2)}, u32[]{:S(2)}) async-start(s32[32,256,1]{1,2,0:T(1,128)} %bitcast.10), calls=%async_computation | async-start | bytes 65536 | tf_op jit(solution)/shard_map/all_to_all | solution.py:68
  36.6 1.0 copy-start.4
  38.5 87.9 %collective-permute-start = (bf16[128,1,256]{2,1,0:T(2,128)(2,1)}, bf16[128,1,256]{2,1,0:T(2,128)(2,1)S(1)}, u32[]{:S(2)}, u32[]{:S(2)}) collective-permute-start(bf16[128,1,256]{2,1,0:T(2,128)(2,1)} %get-tuple-element.26), channel_id=1, source_target_pairs={{0,1},{1,2},{2,3},{3,4},{4,5},{5,6},{6,7},{7,8},{8,9},{9,10},{10,1... | collective-permute-start | bytes 196616 | tf_op jit(solution)/shard_map/ppermute | solution.py:23
  39.9 86.6 %collective-permute-start.1 = (bf16[128,1,256]{2,1,0:T(2,128)(2,1)}, bf16[128,1,256]{2,1,0:T(2,128)(2,1)}, u32[]{:S(2)}, u32[]{:S(2)}) collective-permute-start(bf16[128,1,256]{2,1,0:T(2,128)(2,1)} %get-tuple-element.27), channel_id=1, source_target_pairs={{1,0},{2,1},{3,2},{4,3},{5,4},{6,5},{7,6},{8,7},{9,8},{10,9},{11,1... | collective-permute-start | bytes 196616 | tf_op jit(solution)/shard_map/ppermute | solution.py:24
  47.0 1.7 copy-start.14
  47.0 2.3 copy-start.15
  47.0 2.3 copy-start.1
  49.3 0.6 copy-start.10
  49.5 28.1 %copy-start.13 = (s32[8192,1]{0,1:T(1,128)}, s32[8192,1]{0,1:T(1,128)S(1)}, u32[]{:S(2)}) copy-start(s32[8192,1]{0,1:T(1,128)S(1)} %compare_select_fusion) | copy-start | bytes 98308
  90.1 39.8 %all-to-all-start.1 = ((f32[32,4096,1]{1,2,0:T(1,128)}), f32[32,4096,1]{1,2,0:T(1,128)}, u32[]{:S(2)}, u32[]{:S(2)}) async-start(f32[32,4096,1]{1,2,0:T(1,128)} %copy.41), calls=%async_computation.1 | async-start | bytes 1048576 | tf_op jit(solution)/shard_map/all_to_all | solution.py:72
  97.5 162.9 %copy-start.8 = (bf16[32,16,256]{2,1,0:T(8,128)(2,1)}, bf16[32,16,256]{2,1,0:T(8,128)(2,1)S(1)}, u32[]{:S(2)}) copy-start(bf16[32,16,256]{2,1,0:T(8,128)(2,1)S(1)} %convert_element_type.57) | copy-start | bytes 786436
  120.9 5.5 %copy-start.5 = (bf16[128,16,256]{2,1,0:T(8,128)(2,1)S(1)}, bf16[128,16,256]{2,1,0:T(8,128)(2,1)}, u32[]{:S(2)}) copy-start(bf16[128,16,256]{2,1,0:T(8,128)(2,1)} %copy-done.4) | copy-start | bytes 3145732
  132.1 2.8 copy-start.17
  134.9 16.3 %copy-start.21 = (pred[4096]{0:T(1024)(128)(4,1)S(1)}, pred[4096]{0:T(1024)(128)(4,1)}, u32[]{:S(2)}) copy-start(pred[4096]{0:T(1024)(128)(4,1)} %get-tuple-element.10) | copy-start | bytes 12292
  155.9 2.2 copy-start.18
  161.9 26.0 %copy-start.6 = (f32[128,16,1]{2,1,0:T(8,128)S(1)}, f32[128,16,1]{2,1,0:T(8,128)}, u32[]{:S(2)}) copy-start(f32[128,16,1]{2,1,0:T(8,128)} %get-tuple-element.20) | copy-start | bytes 24580
  197.8 10.9 %slice-start = ((s8[6291456]{0:T(1024)(128)(4,1)}), s8[4194304]{0:T(1024)(128)(4,1)S(1)}, s32[]{:S(2)}) async-start(s8[6291456]{0:T(1024)(128)(4,1)} %bitcast.104), calls=%async_computation.3 | async-start | bytes 8388608
  198.5 10.2 %slice-start.1 = ((s8[6291456]{0:T(1024)(128)(4,1)}), s8[2097152]{0:T(1024)(128)(4,1)S(1)}, s32[]{:S(2)}) async-start(s8[6291456]{0:T(1024)(128)(4,1)} %bitcast.104), calls=%async_computation.4 | async-start | bytes 4194304
  198.7 9.2 %collective-permute-start.2 = (bf16[128,1,256]{2,1,0:T(2,128)(2,1)S(1)}, bf16[128,1,256]{2,1,0:T(2,128)(2,1)S(1)}, u32[]{:S(2)}, u32[]{:S(2)}) collective-permute-start(bf16[128,1,256]{2,1,0:T(2,128)(2,1)S(1)} %get-tuple-element.24), channel_id=1, source_target_pairs={{0,1},{1,2},{2,3},{3,4},{4,5},{5,6},{6,7},{7,8},{8,9},{9,10},{10,1... | collective-permute-start | bytes 196616 | tf_op jit(solution)/shard_map/ppermute | solution.py:23
  200.2 7.7 %collective-permute-start.3 = (bf16[128,1,256]{2,1,0:T(2,128)(2,1)S(1)}, bf16[128,1,256]{2,1,0:T(2,128)(2,1)S(1)}, u32[]{:S(2)}, u32[]{:S(2)}) collective-permute-start(bf16[128,1,256]{2,1,0:T(2,128)(2,1)S(1)} %get-tuple-element.25), channel_id=1, source_target_pairs={{1,0},{2,1},{3,2},{4,3},{5,4},{6,5},{7,6},{8,7},{9,8},{10,9},{11,1... | collective-permute-start | bytes 196616 | tf_op jit(solution)/shard_map/ppermute | solution.py:24
  204.7 4.1 %copy-start.7 = (bf16[128,16,256]{2,1,0:T(8,128)(2,1)S(1)}, bf16[128,16,256]{2,1,0:T(8,128)(2,1)}, u32[]{:S(2)}) copy-start(bf16[128,16,256]{2,1,0:T(8,128)(2,1)} %param.12) | copy-start | bytes 3145732
  214.2 15.4 %copy-start.20 = (pred[4096]{0:T(1024)(128)(4,1)S(1)}, pred[4096]{0:T(1024)(128)(4,1)}, u32[]{:S(2)}) copy-start(pred[4096]{0:T(1024)(128)(4,1)} %compare_and_fusion.1) | copy-start | bytes 12292
  233.3 0.7 copy-start.19
  250.2 16.1 %copy-start.2 = (f32[32,16,256]{2,1,0:T(8,128)S(1)}, f32[32,16,256]{2,1,0:T(8,128)}, u32[]{:S(2)}) copy-start(f32[32,16,256]{2,1,0:T(8,128)} %param.13) | copy-start | bytes 1572868
  254.5 22.6 %all-to-all-start.2 = ((f32[32,4096,1]{1,2,0:T(1,128)}), f32[32,4096,1]{1,2,0:T(1,128)S(1)}, u32[]{:S(2)}, u32[]{:S(2)}) async-start(f32[32,4096,1]{1,2,0:T(1,128)} %all_to_all.27), calls=%async_computation.2 | async-start | bytes 1048576 | tf_op jit(solution)/shard_map/all_to_all | solution.py:72
  260.5 15.2 %collective-permute-start.4 = (bf16[32,1,256]{2,1,0:T(2,128)(2,1)S(1)}, bf16[32,1,256]{2,1,0:T(2,128)(2,1)S(1)}, u32[]{:S(2)}, u32[]{:S(2)}) collective-permute-start(bf16[32,1,256]{2,1,0:T(2,128)(2,1)S(1)} %get-tuple-element.58), channel_id=1, source_target_pairs={{0,1},{1,2},{2,3},{3,4},{4,5},{5,6},{6,7},{7,8},{8,9},{9,10},{10,1... | collective-permute-start | bytes 49160 | tf_op jit(solution)/shard_map/ppermute | solution.py:23
  262.0 13.8 %copy-start.9 = (bf16[32,16,256]{2,1,0:T(8,128)(2,1)S(1)}, bf16[32,16,256]{2,1,0:T(8,128)(2,1)}, u32[]{:S(2)}) copy-start(bf16[32,16,256]{2,1,0:T(8,128)(2,1)} %copy-done.8) | copy-start | bytes 786436
  262.0 13.8 %collective-permute-start.5 = (bf16[32,1,256]{2,1,0:T(2,128)(2,1)S(1)}, bf16[32,1,256]{2,1,0:T(2,128)(2,1)S(1)}, u32[]{:S(2)}, u32[]{:S(2)}) collective-permute-start(bf16[32,1,256]{2,1,0:T(2,128)(2,1)S(1)} %get-tuple-element.59), channel_id=1, source_target_pairs={{1,0},{2,1},{3,2},{4,3},{5,4},{6,5},{7,6},{8,7},{9,8},{10,9},{11,1... | collective-permute-start | bytes 49160 | tf_op jit(solution)/shard_map/ppermute | solution.py:24
  278.4 56.4 %copy-start.3 = (f32[32,16,256]{2,1,0:T(8,128)S(1)}, f32[32,16,256]{2,1,0:T(8,128)}, u32[]{:S(2)}) copy-start(f32[32,16,256]{2,1,0:T(8,128)} %param.14) | copy-start | bytes 1572868
  278.4 56.4 %copy-start.11 = (f32[1,16,256]{2,1,0:T(8,128)S(1)}, f32[1,16,256]{2,1,0:T(8,128)}, u32[]{:S(2)}) copy-start(f32[1,16,256]{2,1,0:T(8,128)} %copy-done.10) | copy-start | bytes 49156
  337.0 7.0 %collective-permute-start.6 = (bf16[32,1,256]{2,1,0:T(2,128)(2,1)S(1)}, bf16[32,1,256]{2,1,0:T(2,128)(2,1)S(1)}, u32[]{:S(2)}, u32[]{:S(2)}) collective-permute-start(bf16[32,1,256]{2,1,0:T(2,128)(2,1)S(1)} %get-tuple-element.56), channel_id=1, source_target_pairs={{0,1},{1,2},{2,3},{3,4},{4,5},{5,6},{6,7},{7,8},{8,9},{9,10},{10,1... | collective-permute-start | bytes 49160 | tf_op jit(solution)/shard_map/ppermute | solution.py:23
  337.1 6.9 %collective-permute-start.7 = (bf16[32,1,256]{2,1,0:T(2,128)(2,1)S(1)}, bf16[32,1,256]{2,1,0:T(2,128)(2,1)S(1)}, u32[]{:S(2)}, u32[]{:S(2)}) collective-permute-start(bf16[32,1,256]{2,1,0:T(2,128)(2,1)S(1)} %get-tuple-element.57), channel_id=1, source_target_pairs={{1,0},{2,1},{3,2},{4,3},{5,4},{6,5},{7,6},{8,7},{9,8},{10,9},{11,1... | collective-permute-start | bytes 49160 | tf_op jit(solution)/shard_map/ppermute | solution.py:24
  345.1 7.0 %collective-permute-start.8 = (bf16[32,1,256]{2,1,0:T(2,128)(2,1)S(1)}, bf16[32,1,256]{2,1,0:T(2,128)(2,1)S(1)}, u32[]{:S(2)}, u32[]{:S(2)}) collective-permute-start(bf16[32,1,256]{2,1,0:T(2,128)(2,1)S(1)} %get-tuple-element.54), channel_id=1, source_target_pairs={{0,1},{1,2},{2,3},{3,4},{4,5},{5,6},{6,7},{7,8},{8,9},{9,10},{10,1... | collective-permute-start | bytes 49160 | tf_op jit(solution)/shard_map/ppermute | solution.py:23
  345.2 6.9 %collective-permute-start.9 = (bf16[32,1,256]{2,1,0:T(2,128)(2,1)S(1)}, bf16[32,1,256]{2,1,0:T(2,128)(2,1)S(1)}, u32[]{:S(2)}, u32[]{:S(2)}) collective-permute-start(bf16[32,1,256]{2,1,0:T(2,128)(2,1)S(1)} %get-tuple-element.55), channel_id=1, source_target_pairs={{1,0},{2,1},{3,2},{4,3},{5,4},{6,5},{7,6},{8,7},{9,8},{10,9},{11,1... | collective-permute-start | bytes 49160 | tf_op jit(solution)/shard_map/ppermute | solution.py:24
  353.2 7.1 %collective-permute-start.10 = (bf16[32,1,256]{2,1,0:T(2,128)(2,1)S(1)}, bf16[32,1,256]{2,1,0:T(2,128)(2,1)S(1)}, u32[]{:S(2)}, u32[]{:S(2)}) collective-permute-start(bf16[32,1,256]{2,1,0:T(2,128)(2,1)S(1)} %get-tuple-element.52), channel_id=1, source_target_pairs={{0,1},{1,2},{2,3},{3,4},{4,5},{5,6},{6,7},{7,8},{8,9},{9,10},{10,1... | collective-permute-start | bytes 49160 | tf_op jit(solution)/shard_map/ppermute | solution.py:23
  353.3 7.0 %collective-permute-start.11 = (bf16[32,1,256]{2,1,0:T(2,128)(2,1)S(1)}, bf16[32,1,256]{2,1,0:T(2,128)(2,1)S(1)}, u32[]{:S(2)}, u32[]{:S(2)}) collective-permute-start(bf16[32,1,256]{2,1,0:T(2,128)(2,1)S(1)} %get-tuple-element.53), channel_id=1, source_target_pairs={{1,0},{2,1},{3,2},{4,3},{5,4},{6,5},{7,6},{8,7},{9,8},{10,9},{11,1... | collective-permute-start | bytes 49160 | tf_op jit(solution)/shard_map/ppermute | solution.py:24
where the time goes:
time: 367 us; the launch traced here: 362 us
  local copies, waits for them, and re-layouts  155 us (42%)
  other arithmetic  140 us (38%)
  starting transfers between devices  49.6 us (14%)
  waiting for transfers between devices  15.9 us (4%)
    scatter-add x1, other arithmetic, body(): jnp.zeros((patch_count, 16), jnp.float32).at[asked_ids].add(arrived)  53.4 us
    gather x3, local copies, waits for them, and re-layouts, body(): answer = jnp.take(solid_rows, asked_ids, axis=0)  34.3 us
    ppermute x6, starting transfers between devices, with_halo(): after = lax.ppermute(leading, axis, down)  28.5 us
    scatter-add x1, other arithmetic, body(): jnp.zeros((patch_count, 16), jnp.float32).at[flow_patch].add(forward)  22.9 us
    gather x2, local copies, waits for them, and re-layouts, body(): weights = jnp.take(table_rows, block_index, axis=0).reshape(-1, 16, 16)  21.7 us
    gather x1, local copies, waits for them, and re-layouts, body(): fetched = jnp.take(returned, slot_index, axis=0)  16.3 us
    scatter x1, local copies, waits for them, and re-layouts, body(): jnp.zeros((devices * capacity,), jnp.int32).at[slot_index].set(solid_patch)  16.3 us
    gather x1, local copies, waits for them, and re-layouts, body(): gathered_flux = jnp.take(flux_rows, flow_patch, axis=0)  15.4 us
  transfers between devices with their start and end apart: 15, of which 6 were waited for; matrix products, arithmetic and copies ran while one was open for 24% of the time, Pallas kernels for 0%

commit v1 on v0

v1 whole, which is shorter than its diff:
```python
import functools

import jax
import jax.numpy as jnp
from jax import lax
from jax.experimental import pallas as pl
from jax.experimental.pallas import tpu as pltpu
from jax.sharding import PartitionSpec as P

SUBCYCLES = 4
DIFFUSION = 0.8
TIMESTEP = 0.12
FILM_COEFF = 1.0
CONDUCT_RATE = 0.08
FLUX_GAIN = 0.25

AXES = ("grp", "dom")
NODES = 16
CHUNK = 512
LANES = 128
LAYERS = 16
HALO = 4
F32 = jnp.float32
BF16 = jnp.bfloat16
VMEM_LIMIT = 58 * 1024 * 1024
STEPS_PER_UNIT = 5461.0
I16 = jnp.int16


def params(**kw):
    return pltpu.CompilerParams(vmem_limit_bytes=VMEM_LIMIT, **kw)


def cost(flops, nbytes):
    return pl.CostEstimate(flops=flops, bytes_accessed=nbytes, transcendentals=0)


def one_hot(index, rows):
    cells = lax.broadcasted_iota(jnp.int32, (rows, index.shape[1]), 0)
    return jnp.where(cells == index, 1.0, 0.0).astype(BF16)


def dot(a, b):
    return lax.dot_general(a, b, (((1,), (0,)), ((), ())), preferred_element_type=F32)


def dot_nt(a, b):
    return lax.dot_general(a, b, (((1,), (1,)), ((), ())), preferred_element_type=F32)


def split(x):
    high = x.astype(BF16)
    return high, (x - high.astype(F32)).astype(BF16)


def weights_kernel(block_ref, table_ref, out_ref, table_high, table_low):
    @pl.when(pl.program_id(0) == 0)
    def _():
        table_high[...], table_low[...] = split(table_ref[...])

    picked = one_hot(block_ref[...], table_ref.shape[1])
    out_ref[...] = dot(table_high[...], picked) + dot(table_low[...], picked)


def weights_of(block_index, table):
    entries, blocks = table.shape
    count = block_index.shape[1]
    return pl.pallas_call(
        weights_kernel,
        grid=(count // CHUNK,),
        in_specs=[
            pl.BlockSpec((1, CHUNK), lambda i: (0, i)),
            pl.BlockSpec((entries, blocks), lambda i: (0, 0)),
        ],
        out_specs=pl.BlockSpec((entries, CHUNK), lambda i: (0, i)),
        out_shape=jax.ShapeDtypeStruct((entries, count), F32),
        scratch_shapes=[pltpu.VMEM((entries, blocks), BF16)] * 2,
        compiler_params=params(),
        cost_estimate=cost(4 * entries * blocks * count, 4 * entries * (blocks + count)),
        name="weights",
    )(block_index, table)


def spread_rows(rows_x):
    p = lax.broadcasted_iota(jnp.int32, (rows_x, rows_x * NODES), 1)
    x = lax.broadcasted_iota(jnp.int32, (rows_x, rows_x * NODES), 0)
    return jnp.where(p // NODES == x, 1.0, 0.0).astype(BF16)


def patches_to_face(patches, rows_x):
    count = patches.shape[1]
    c = lax.broadcasted_iota(jnp.int32, (NODES, count), 1) % NODES
    parts = [jnp.where(c == k, patches, 0.0) for k in range(NODES)]
    high, low = split(jnp.concatenate(parts, axis=0))
    rows = spread_rows(rows_x)
    return dot_nt(rows, high) + dot_nt(rows, low)


def face_to_patches(face, rows_x):
    high, low = split(face)
    rows = spread_rows(rows_x)
    wide = lax.dot_general(
        high, rows, (((0,), (0,)), ((), ())), preferred_element_type=F32
    ) + lax.dot_general(low, rows, (((0,), (0,)), ((), ())), preferred_element_type=F32)
    c = lax.broadcasted_iota(jnp.int32, (NODES, rows.shape[1]), 1) % NODES
    out = jnp.zeros((NODES, rows.shape[1]), F32)
    for k in range(NODES):
        out = jnp.where(c == k, wide[k * NODES : (k + 1) * NODES], out)
    return out


def solid_place(device_ref, patch_ref, rows_x):
    per_row = NODES
    patch = patch_ref[...]
    return device_ref[...] * rows_x + patch // per_row, patch % per_row


def forward_kernel(
    device_ref,
    patch_ref,
    flow_p_ref,
    weights_ref,
    faces_ref,
    wall_ref,
    first_ref,
    last_ref,
    faces_high,
    faces_low,
    fetched,
    product_high,
    product_low,
    total,
):
    step = pl.program_id(0)
    rows_x = wall_ref.shape[0]

    @pl.when(step == 0)
    def _():
        faces_high[...], faces_low[...] = split(faces_ref[...].astype(F32).T)
        total[...] = jnp.zeros_like(total)

    solid_x, solid_c = solid_place(device_ref, patch_ref, rows_x)
    picked = one_hot(solid_x, faces_ref.shape[0])
    fetched[...] = dot(faces_high[...], picked) + dot(faces_low[...], picked)
    for k in range(CHUNK // LANES):
        lanes = slice(k * LANES, (k + 1) * LANES)
        c = jnp.broadcast_to(solid_c[:, lanes], (NODES, LANES))
        values = jnp.zeros((NODES, LANES), F32)
        for j in range(NODES):
            values = jnp.where(c == j, fetched[j * NODES : (j + 1) * NODES, lanes], values)
        values = values * (1.0 / STEPS_PER_UNIT)
        for i in range(NODES):
            rows = slice(i * NODES, (i + 1) * NODES)
            product_high[rows, lanes], product_low[rows, lanes] = split(weights_ref[rows, lanes] * values)
    placed = one_hot(flow_p_ref[...], total.shape[1])
    total[...] += dot_nt(product_high[...], placed) + dot_nt(product_low[...], placed)

    @pl.when(step == pl.num_programs(0) - 1)
    def _():
        patches = jnp.sum(total[...].reshape(NODES, NODES, total.shape[1]), axis=1)
        wall = patches_to_face(patches, rows_x)
        wall_ref[...] = wall
        first_ref[...] = wall[:1]
        last_ref[...] = wall[rows_x - 1 :]


def forward(solid_device, solid_patch, flow_p, weights, faces, rows_x):
    entries, count = weights.shape
    tall, width = faces.shape
    line = pl.BlockSpec((1, CHUNK), lambda i: (0, i))
    fixed = lambda shape: pl.BlockSpec(shape, lambda i: (0,) * len(shape))
    return pl.pallas_call(
        forward_kernel,
        grid=(count // CHUNK,),
        in_specs=[
            line,
            line,
            line,
            pl.BlockSpec((entries, CHUNK), lambda i: (0, i)),
            fixed((tall, width)),
        ],
        out_specs=[fixed((rows_x, width)), fixed((1, width)), fixed((1, width))],
        out_shape=[
            jax.ShapeDtypeStruct((rows_x, width), F32),
            jax.ShapeDtypeStruct((1, width), F32),
            jax.ShapeDtypeStruct((1, width), F32),
        ],
        scratch_shapes=[
            pltpu.VMEM((width, tall), BF16),
            pltpu.VMEM((width, tall), BF16),
            pltpu.VMEM((width, CHUNK), F32),
            pltpu.VMEM((entries, CHUNK), BF16),
            pltpu.VMEM((entries, CHUNK), BF16),
            pltpu.VMEM((entries, rows_x * NODES), F32),
        ],
        compiler_params=params(),
        cost_estimate=cost(4 * width * (tall + entries) * count, 4 * entries * count),
        name="forward",
    )(solid_device, solid_patch, flow_p, weights, faces)


def edges_kernel(
    flow_low_ref, flow_high_ref, speed_ref, solid_ref, rates_ref, up_ref, down_ref
):
    layers = flow_low_ref.shape[0]
    solid_layers, rows, width = solid_ref.shape
    low = lax.broadcasted_iota(jnp.int32, (8, width), 0) < HALO
    for l in range(0, solid_layers, 2):
        ups, downs = [], []
        for m in (l, l + 1):
            ups.append(
                jnp.where(low, pltpu.roll(rates_ref[m, rows - 8 :], HALO, 0), solid_ref[m, rows - 8 :])
            )
            downs.append(jnp.where(low, solid_ref[m, :8], pltpu.roll(rates_ref[m, :8], HALO, 0)))
        up_ref[l * 8 : l * 8 + 16] = jnp.concatenate(ups, axis=0).astype(BF16)
        down_ref[l * 8 : l * 8 + 16] = jnp.concatenate(downs, axis=0).astype(BF16)
    start = solid_layers * 8
    for l in range(0, layers, LAYERS):
        part = slice(start + l, start + l + LAYERS)
        up_ref[part] = jnp.concatenate(
            [flow_high_ref[m, 7:8] for m in range(l, l + LAYERS)], axis=0
        ).astype(BF16)
        down_ref[part] = jnp.concatenate(
            [flow_low_ref[m, 0:1] for m in range(l, l + LAYERS)], axis=0
        ).astype(BF16)
    part = slice(start + layers, start + layers + LAYERS)
    speed = speed_ref[0, 0].astype(F32)
    up_ref[part] = jnp.broadcast_to(speed[rows - 1 :], (LAYERS, width)).astype(BF16)
    down_ref[part] = jnp.broadcast_to(speed[:1], (LAYERS, width)).astype(BF16)


def edges(flow, velocity, solid, rates):
    layers, rows, width = flow.shape
    solid_layers = solid.shape[0]
    shape = (solid_layers * 8 + layers + LAYERS, width)
    whole = pl.BlockSpec(solid.shape, lambda i: (0, 0, 0))
    return pl.pallas_call(
        edges_kernel,
        grid=(1,),
        in_specs=[
            pl.BlockSpec((layers, 8, width), lambda i: (0, 0, 0)),
            pl.BlockSpec((layers, 8, width), lambda i: (0, rows // 8 - 1, 0)),
            pl.BlockSpec((1, 1, rows, width), lambda i: (0, layers - 1, 0, 0)),
            whole,
            whole,
        ],
        out_specs=[pl.BlockSpec(shape, lambda i: (0, 0))] * 2,
        out_shape=[jax.ShapeDtypeStruct(shape, BF16)] * 2,
        compiler_params=params(),
        cost_estimate=cost(8 * shape[0] * width, 12 * shape[0] * width),
        name="edges",
    )(flow, flow, velocity, solid, rates)


def layer_tendency(centre, zlow, zhigh, xlow, xhigh, vz, vx, vy, source):
    width = centre.shape[1]
    total = source
    pairs = (
        (vz, zlow, zhigh),
        (vx, xlow, xhigh),
        (vy, pltpu.roll(centre, 1, 1), pltpu.roll(centre, width - 1, 1)),
    )
    for speed, low, high in pairs:
        a = jnp.maximum(speed, 0.0) + DIFFUSION
        b = a - speed
        total = total + a * (low - centre) + b * (high - centre)
    return total


def x_neighbours(centre, low_row, high_row):
    rows, width = centre.shape
    row = lax.broadcasted_iota(jnp.int32, (rows, width), 0)
    low = jnp.where(row == 0, jnp.broadcast_to(low_row, (rows, width)), pltpu.roll(centre, 1, 0))
    high = jnp.where(
        row == rows - 1, jnp.broadcast_to(high_row, (rows, width)), pltpu.roll(centre, rows - 1, 0)
    )
    return low, high


def predictor_kernel(
    below_ref, flow_ref, above_ref, low_ref, high_ref, velocity_ref, heat_ref, out_ref, first_ref, last_ref
):
    step = pl.program_id(0)
    lows = low_ref[...].astype(F32)
    highs = high_ref[...].astype(F32)
    first, last = [], []
    rows = flow_ref.shape[1]
    for l in range(LAYERS):
        centre = flow_ref[l]
        if l == 0:
            zlow = jnp.where(step == 0, 0.0, below_ref[0])
        else:
            zlow = flow_ref[l - 1]
        if l == LAYERS - 1:
            zhigh = jnp.where(step == pl.num_programs(0) - 1, 0.0, above_ref[0])
        else:
            zhigh = flow_ref[l + 1]
        xlow, xhigh = x_neighbours(centre, lows[l : l + 1], highs[l : l + 1])
        vz, vx, vy = (velocity_ref[d, l].astype(F32) for d in range(3))
        value = centre + TIMESTEP * layer_tendency(
            centre, zlow, zhigh, xlow, xhigh, vz, vx, vy, heat_ref[l].astype(F32)
        )
        out_ref[l] = value
        first.append(value[0:1])
        last.append(value[rows - 1 : rows])
    first_ref[...] = jnp.concatenate(first, axis=0).astype(BF16)
    last_ref[...] = jnp.concatenate(last, axis=0).astype(BF16)


def layer_specs(shape, halo=True):
    layers, rows, width = shape
    block = pl.BlockSpec((LAYERS, rows, width), lambda i: (i, 0, 0))
    below = pl.BlockSpec((1, rows, width), lambda i: (jnp.maximum(i * LAYERS - 1, 0), 0, 0))
    above = pl.BlockSpec((1, rows, width), lambda i: (jnp.minimum((i + 1) * LAYERS, layers - 1), 0, 0))
    speeds = pl.BlockSpec((3, LAYERS, rows, width), lambda i: (0, i, 0, 0))
    edge = pl.BlockSpec((LAYERS, width), lambda i: (i, 0))
    return block, below, above, speeds, edge


def predictor(flow, low, high, velocity, heat):
    layers, rows, width = flow.shape
    block, below, above, speeds, edge = layer_specs(flow.shape)
    cells = layers * rows * width
    first_edge = low.shape[0] // LAYERS - layers // LAYERS - 1
    flow_edge = pl.BlockSpec((LAYERS, width), lambda i: (i + first_edge, 0))
    return pl.pallas_call(
        predictor_kernel,
        grid=(layers // LAYERS,),
        in_specs=[below, block, above, flow_edge, flow_edge, speeds, block],
        out_specs=[block, edge, edge],
        out_shape=[
            jax.ShapeDtypeStruct(flow.shape, F32),
            jax.ShapeDtypeStruct((layers, width), BF16),
            jax.ShapeDtypeStruct((layers, width), BF16),
        ],
        compiler_params=params(),
        cost_estimate=cost(40 * cells, 16 * cells),
        name="predictor",
    )(flow, flow, flow, low, high, velocity, heat)


def corrector_kernel(
    below_ref, mid_ref, above_ref, top_ref, wall_ref, rim_ref, low_ref, high_ref, flow_ref, velocity_ref, heat_ref, out_ref
):
    step = pl.program_id(0)
    final = step == pl.num_programs(0) - 1
    lows = low_ref[...].astype(F32)
    highs = high_ref[...].astype(F32)
    for l in range(LAYERS):
        centre = mid_ref[l]
        low_row, high_row = lows[l : l + 1], highs[l : l + 1]
        zlow = jnp.where(step == 0, 0.0, below_ref[0]) if l == 0 else mid_ref[l - 1]
        if l == LAYERS - 1:
            centre = jnp.where(final, top_ref[...], centre)
            zhigh = jnp.where(final, wall_ref[...], above_ref[0])
            low_row = jnp.where(final, rim_ref[0:1], low_row)
            high_row = jnp.where(final, rim_ref[1:2], high_row)
        elif l == LAYERS - 2:
            zhigh = jnp.where(final, top_ref[...], mid_ref[l + 1])
        else:
            zhigh = mid_ref[l + 1]
        xlow, xhigh = x_neighbours(centre, low_row, high_row)
        vz, vx, vy = (velocity_ref[d, l].astype(F32) for d in range(3))
        slope = layer_tendency(centre, zlow, zhigh, xlow, xhigh, vz, vx, vy, heat_ref[l].astype(F32))
        out_ref[l] = 0.5 * flow_ref[l] + 0.5 * (centre + TIMESTEP * slope)


def corrector(mid, top, wall, rim, low, high, flow, velocity, heat):
    layers, rows, width = flow.shape
    block, below, above, speeds, edge = layer_specs(flow.shape)
    face = pl.BlockSpec((rows, width), lambda i: (0, 0))
    cells = layers * rows * width
    return pl.pallas_call(
        corrector_kernel,
        grid=(layers // LAYERS,),
        in_specs=[below, block, above, face, face, pl.BlockSpec(rim.shape, lambda i: (0, 0)), edge, edge, block, speeds, block],
        out_specs=block,
        out_shape=jax.ShapeDtypeStruct(flow.shape, F32),
        compiler_params=params(),
        cost_estimate=cost(44 * cells, 20 * cells),
        name="corrector",
    )(mid, mid, mid, top, wall, rim, low, high, flow, velocity, heat)


def backward_kernel(
    device_ref,
    patch_ref,
    flow_p_ref,
    weights_ref,
    wall_ref,
    wall_low_ref,
    wall_high_ref,
    vz_low_ref,
    vz_high_ref,
    mid_ref,
    low_ref,
    high_ref,
    flow_ref,
    velocity_ref,
    heat_ref,
    send_ref,
    top_ref,
    rim_ref,
    flux_high,
    flux_low,
    fetched,
    returned_high,
    returned_low,
    total,
):
    step = pl.program_id(0)
    rows, width = wall_ref.shape

    @pl.when(step == 0)
    def _():
        total[...] = jnp.zeros_like(total)
        wall = wall_ref[...]
        vz, vx, vy = (velocity_ref[d, 0].astype(F32) for d in range(3))
        top = mid_ref[1] + TIMESTEP * (DIFFUSION - jnp.minimum(vz, 0.0)) * wall
        edge = low_ref.shape[0]
        low_row = low_ref[edge - 1 : edge].astype(F32) + TIMESTEP * (
            DIFFUSION - jnp.minimum(vz_low_ref[...].astype(F32)[:1], 0.0)
        ) * wall_low_ref[...]
        high_row = high_ref[edge - 1 : edge].astype(F32) + TIMESTEP * (
            DIFFUSION - jnp.minimum(vz_high_ref[...].astype(F32)[:1], 0.0)
        ) * wall_high_ref[...]
        xlow, xhigh = x_neighbours(top, low_row, high_row)
        slope = layer_tendency(top, mid_ref[0], wall, xlow, xhigh, vz, vx, vy, heat_ref[0].astype(F32))
        out = 0.5 * flow_ref[0] + 0.5 * (top + TIMESTEP * slope)
        top_ref[...] = top
        rim_ref[...] = jnp.zeros_like(rim_ref)
        rim_ref[0:1] = low_row
        rim_ref[1:2] = high_row
        patches = face_to_patches(FILM_COEFF * (out - wall), rows)
        wide = jnp.broadcast_to(patches[:, None, :], (NODES, NODES, patches.shape[1]))
        high, low = split(wide.reshape(NODES * NODES, patches.shape[1]))
        flux_high[...] = high
        flux_low[...] = low

    picked = one_hot(flow_p_ref[...], flux_high.shape[1])
    fetched[...] = dot(flux_high[...], picked) + dot(flux_low[...], picked)
    solid_x, solid_c = solid_place(device_ref, patch_ref, rows)
    for k in range(CHUNK // LANES):
        lanes = slice(k * LANES, (k + 1) * LANES)
        value = jnp.zeros((NODES, LANES), F32)
        for i in range(NODES):
            part = slice(i * NODES, (i + 1) * NODES)
            value = value + weights_ref[part, lanes] * fetched[part, lanes]
        c = jnp.broadcast_to(solid_c[:, lanes], (NODES, LANES))
        high, low = split(value)
        high, low = high.astype(F32), low.astype(F32)
        for j in range(NODES):
            part = slice(j * NODES, (j + 1) * NODES)
            returned_high[part, lanes] = jnp.where(c == j, high, 0.0).astype(BF16)
            returned_low[part, lanes] = jnp.where(c == j, low, 0.0).astype(BF16)
    placed = one_hot(solid_x, total.shape[0])
    total[...] += dot_nt(placed, returned_high[...]) + dot_nt(placed, returned_low[...])

    @pl.when(step == pl.num_programs(0) - 1)
    def _():
        devices = send_ref.shape[0]
        tall = total.shape[0]
        peak = jnp.zeros((8, width), F32)
        for r in range(0, tall, 8):
            peak = jnp.maximum(peak, jnp.abs(total[r : r + 8]))
        peak = jnp.maximum(jnp.max(peak, axis=0, keepdims=True), 1e-30)
        power = jnp.floor(jnp.log2(peak)) + 1.0
        factor = jnp.exp2(15.0 - power)
        sub = lax.broadcasted_iota(jnp.int32, (8, width), 0)
        for d in range(devices):
            own = total[d * rows : (d + 1) * rows]
            after = ((d + 1) * rows) % tall
            before = (d * rows - 8) % tall
            rim = jnp.where(sub < HALO, total[after : after + 8], total[before : before + 8])
            scaled = jnp.clip(jnp.round(jnp.concatenate([own, rim], axis=0) * factor), -32767.0, 32767.0)
            place = lax.broadcasted_iota(jnp.int32, scaled.shape, 0) == rows + HALO - 1
            scaled = jnp.where(place, jnp.broadcast_to(power, scaled.shape), scaled)
            send_ref[d] = scaled.astype(jnp.int32).astype(I16)


def backward(solid_device, solid_patch, flow_p, weights, wall, wall_low, wall_high, edge_low, edge_high, mid, low, high, flow, velocity, heat, devices):
    entries, count = weights.shape
    rows, width = wall.shape
    layers = flow.shape[0]
    tall = devices * rows
    line = pl.BlockSpec((1, CHUNK), lambda i: (0, i))
    fixed = lambda shape: pl.BlockSpec(shape, lambda i: (0,) * len(shape))
    edge = pl.BlockSpec((LAYERS, width), lambda i: (layers // LAYERS - 1, 0))
    last = edge_low.shape[0] // LAYERS - 1
    speed = pl.BlockSpec((LAYERS, width), lambda i: (last, 0))
    return pl.pallas_call(
        backward_kernel,
        grid=(count // CHUNK,),
        in_specs=[
            line,
            line,
            line,
            pl.BlockSpec((entries, CHUNK), lambda i: (0, i)),
            fixed((rows, width)),
            fixed((1, width)),
            fixed((1, width)),
            speed,
            speed,
            pl.BlockSpec((2, rows, width), lambda i: (layers // 2 - 1, 0, 0)),
            edge,
            edge,
            pl.BlockSpec((1, rows, width), lambda i: (layers - 1, 0, 0)),
            pl.BlockSpec((3, 1, rows, width), lambda i: (0, layers - 1, 0, 0)),
            pl.BlockSpec((1, rows, width), lambda i: (layers - 1, 0, 0)),
        ],
        out_specs=[fixed((devices, rows + 8, width)), fixed((rows, width)), fixed((8, width))],
        out_shape=[
            jax.ShapeDtypeStruct((devices, rows + 8, width), I16),
            jax.ShapeDtypeStruct((rows, width), F32),
            jax.ShapeDtypeStruct((8, width), F32),
        ],
        scratch_shapes=[
            pltpu.VMEM((entries, rows * NODES), BF16),
            pltpu.VMEM((entries, rows * NODES), BF16),
            pltpu.VMEM((entries, CHUNK), F32),
            pltpu.VMEM((width, CHUNK), BF16),
            pltpu.VMEM((width, CHUNK), BF16),
            pltpu.VMEM((tall, width), F32),
        ],
        compiler_params=params(),
        cost_estimate=cost(4 * width * (tall + entries) * count, 4 * entries * count),
        name="backward",
    )(solid_device, solid_patch, flow_p, weights, wall, wall_low, wall_high, edge_low, edge_high, mid, low, high, flow, velocity, heat)


def conduct(current, layers, rates, flux):
    rows = current[0].shape[0]
    width = current[0].shape[1]
    out = []
    for l in range(layers):
        centre = current[l]
        low = current[l - 1] if l > 0 else centre
        around = low + pltpu.roll(centre, 1, 0) + pltpu.roll(centre, rows - 1, 0)
        around = around + pltpu.roll(centre, 1, 1) + pltpu.roll(centre, width - 1, 1)
        if l + 1 < len(current):
            around = around + current[l + 1]
        value = centre + CONDUCT_RATE * rates[l] * (around - 6.0 * centre)
        if l == 0 and flux is not None:
            value = value + flux
        out.append(value)
    return out


def rims(low_ref, high_ref, l, width):
    low = lax.broadcasted_iota(jnp.int32, (8, width), 0) < HALO
    before = low_ref[l * 8 : l * 8 + 8].astype(F32)
    after = high_ref[l * 8 : l * 8 + 8].astype(F32)
    return jnp.where(low, after, before), pltpu.roll(jnp.where(low, before, after), HALO, 0)


def liner_kernel(solid_ref, rates_ref, low_ref, high_ref, out_ref, first, second, rates):
    layers, rows, width = solid_ref.shape
    for l in range(layers):
        solid_rim, rates_rim = rims(low_ref, high_ref, l, width)
        first[l, :rows] = solid_ref[l]
        first[l, rows:] = solid_rim
        rates[l, :rows] = CONDUCT_RATE * rates_ref[l]
        rates[l, rows:] = CONDUCT_RATE * rates_rim
    tall = first.shape[1]

    for substep in range(SUBCYCLES):
        source, target = (first, second) if substep % 2 == 0 else (second, first)
        for l in range(layers):
            centre = source[l]
            around = source[max(l - 1, 0)] + pltpu.roll(centre, 1, 0) + pltpu.roll(centre, tall - 1, 0)
            around = around + pltpu.roll(centre, 1, 1) + pltpu.roll(centre, width - 1, 1)
            if l < layers - 1:
                around = around + source[l + 1]
            value = centre + rates[l] * (around - 6.0 * centre)
            if substep == SUBCYCLES - 1:
                out_ref[l] = value[:rows]
            else:
                target[l] = value


def liner(solid, rates, edge_low, edge_high):
    layers, rows, width = solid.shape
    tall = rows + 8
    cells = layers * tall * width
    whole = pl.BlockSpec(solid.shape, lambda i: (0, 0, 0))
    edge = pl.BlockSpec((layers * 8, width), lambda i: (0, 0))
    return pl.pallas_call(
        liner_kernel,
        grid=(1,),
        in_specs=[whole, whole, edge, edge],
        out_specs=whole,
        out_shape=jax.ShapeDtypeStruct(solid.shape, F32),
        scratch_shapes=[pltpu.VMEM((layers, tall, width), F32)] * 3,
        compiler_params=params(),
        cost_estimate=cost(14 * SUBCYCLES * cells, 12 * cells),
        name="liner",
    )(solid, rates, edge_low, edge_high)


def liner_top_kernel(arrived_ref, solid_ref, rates_ref, low_ref, high_ref, rest_ref, out_ref):
    del rest_ref
    depth, rows, width = solid_ref.shape
    mark = rows + HALO - 1
    flux = jnp.zeros(arrived_ref.shape[1:], F32)
    for d in range(arrived_ref.shape[0]):
        part = arrived_ref[d].astype(jnp.int32).astype(F32)
        flux = flux + part * jnp.exp2(part[mark : mark + 1] - 15.0)
    flux = FLUX_GAIN * flux
    current, rates = [], []
    for l in range(depth):
        solid_rim, rates_rim = rims(low_ref, high_ref, l, width)
        current.append(jnp.concatenate([solid_ref[l], solid_rim], axis=0))
        rates.append(jnp.concatenate([rates_ref[l], rates_rim], axis=0))
    for substep in range(SUBCYCLES):
        current = conduct(current, depth - 1 - substep, rates, flux)
    for l in range(SUBCYCLES):
        out_ref[l] = current[l][:rows]


def liner_top(arrived, solid, rates, edge_low, edge_high, rest):
    rows, width = solid.shape[1:]
    depth = 2 * SUBCYCLES
    top = pl.BlockSpec((depth, rows, width), lambda i: (0, 0, 0))
    edge = pl.BlockSpec((depth * 8, width), lambda i: (0, 0))
    cells = depth * (rows + 8) * width
    return pl.pallas_call(
        liner_top_kernel,
        grid=(1,),
        in_specs=[
            pl.BlockSpec(arrived.shape, lambda i: (0, 0, 0)),
            top,
            top,
            edge,
            edge,
            pl.BlockSpec(memory_space=pl.ANY),
        ],
        out_specs=pl.BlockSpec((SUBCYCLES, rows, width), lambda i: (0, 0, 0)),
        out_shape=jax.ShapeDtypeStruct(rest.shape, F32),
        input_output_aliases={5: 0},
        compiler_params=params(),
        cost_estimate=cost(60 * cells, 8 * cells),
        name="liner_top",
    )(arrived, solid, rates, edge_low, edge_high, rest)


def body(
    flow_temp,
    velocity,
    heat_release,
    solid_temp,
    conductivity,
    interp_table,
    flow_patch,
    solid_device,
    solid_patch,
    block_index,
):
    layers, rows, width = flow_temp.shape
    devices = lax.axis_size(AXES)
    up = [(i, (i + 1) % devices) for i in range(devices)]
    down = [(j, i) for i, j in up]

    steps = jnp.round(solid_temp[0] * STEPS_PER_UNIT).astype(I16)
    outgoing = jnp.broadcast_to(steps[None], (devices, rows, width))
    faces = lax.all_to_all(outgoing, AXES, split_axis=0, concat_axis=0, tiled=True)
    faces = faces.reshape(devices * rows, width)

    to_up, to_down = edges(flow_temp, velocity, solid_temp, conductivity)
    before = lax.ppermute(to_up, AXES, up)
    after = lax.ppermute(to_down, AXES, down)

    solid_device = solid_device.reshape(1, -1)
    solid_patch = solid_patch[None]
    flow_p = flow_patch[None]
    weights = weights_of(block_index[None], interp_table.reshape(NODES * NODES, -1))

    mid, mid_first, mid_last = predictor(flow_temp, before, after, velocity, heat_release)
    mid_low = lax.ppermute(mid_last, AXES, up)
    mid_high = lax.ppermute(mid_first, AXES, down)

    wall, wall_first, wall_last = forward(solid_device, solid_patch, flow_p, weights, faces, rows)
    wall_low = lax.ppermute(wall_last, AXES, up)
    wall_high = lax.ppermute(wall_first, AXES, down)

    sending, top, rim = backward(
        solid_device,
        solid_patch,
        flow_p,
        weights,
        wall,
        wall_low,
        wall_high,
        before,
        after,
        mid,
        mid_low,
        mid_high,
        flow_temp,
        velocity,
        heat_release,
        devices,
    )
    arrived = lax.all_to_all(sending, AXES, split_axis=0, concat_axis=0, tiled=True)
    flow_out = corrector(mid, top, wall, rim, mid_low, mid_high, flow_temp, velocity, heat_release)
    rest = liner(solid_temp, conductivity, before, after)
    solid_out = liner_top(arrived, solid_temp, conductivity, before, after, rest)
    return (flow_out, solid_out)


def solution(mesh):
    placed = (
        P(None, AXES, None),
        P(None, None, AXES, None),
        P(None, AXES, None),
        P(None, AXES, None),
        P(None, AXES, None),
        P(),
        P(AXES),
        P(AXES, None),
        P(AXES),
        P(AXES),
    )
    return jax.shard_map(
        body,
        mesh=mesh,
        in_specs=placed,
        out_specs=(P(None, AXES, None), P(None, AXES, None)),
        check_vma=False,
    )
```

time: 367 us -> 93.6 us (0.26)
  the two profiles are of different devices: /device:TPU:1 before, /device:TPU:0 now
where the time goes in v1:
time: 93.6 us; the launch traced here: 92.6 us
  Pallas kernels  54.7 us (58%)
  starting transfers between devices  29.2 us (31%)
  local copies, waits for them, and re-layouts  4.08 us (4%)
  waiting for transfers between devices  3.19 us (3%)
    pallas_call x1, Pallas kernels, forward(): pl.pallas_call(forward_kernel, grid=(count // CHUNK,), in_specs=[line, li...  10.4 us
    pallas_call x1, Pallas kernels, backward(): pl.pallas_call(backward_kernel, grid=(count // CHUNK,), in_specs=[line, l...  10.2 us
    pallas_call x1, Pallas kernels, weights_of(): pl.pallas_call(weights_kernel, grid=(count // CHUNK,), in_specs=[pl.Block...  8.72 us
    pallas_call x1, Pallas kernels, corrector(): pl.pallas_call(corrector_kernel, grid=(layers // LAYERS,), in_specs=[belo...  8.51 us
    pallas_call x1, Pallas kernels, predictor(): pl.pallas_call(predictor_kernel, grid=(layers // LAYERS,), in_specs=[belo...  8.07 us
    all_to_all x1, starting transfers between devices, body(): lax.all_to_all(outgoing, AXES, split_axis=0, concat_axis=0, tiled=True)  7.3 us
    all_to_all x1, starting transfers between devices, body(): lax.all_to_all(sending, AXES, split_axis=0, concat_axis=0, tiled=True)  5.84 us
    ppermute x1, starting transfers between devices, body(): wall_high = lax.ppermute(wall_first, AXES, down)  5.34 us
  transfers between devices with their start and end apart: 8, of which 2 were waited for; matrix products, arithmetic and copies ran while one was open for 0% of the time, Pallas kernels for 46%

profile of v1, /device:TPU:0, one launch (start us, length us, event | category | flops | bytes accessed | tf_op | source)
XLA Modules:
  0.0 92.6 jit_solution(12317337703459710785)
XLA Ops:
  0.6 0.7 fusion
  1.4 0.7 broadcast_in_dim.21
  2.1 7.3 %all-to-all-start = ((s16[32,16,256]{2,1,0:T(8,128)(2,1)}), s16[32,16,256]{2,1,0:T(8,128)(2,1)S(1)}, u32[]{:S(2)}, u32[]{:S(2)}) async-start(s16[32,16,256]{2,1,0:T(8,128)(2,1)} %broadcast_in_dim.21), calls=%async_computation | async-start | bytes 524288 | tf_op jit(solution)/shard_map/all_to_all | solution.py:665
  9.4 2.8 %edges.1 = (bf16[400,256]{1,0:T(8,128)(2,1)}, bf16[400,256]{1,0:T(8,128)(2,1)}) custom-call(f32[128,16,256]{2,1,0:T(8,128)} %flow_ref.5, f32[128,16,256]{2,1,0:T(8,128)} %flow_ref.5, bf16[3,128,16,256]{3,2,1,0:T(8,128)(2,1)} %velocity_ref.5, f32[32,16,256]{2,1,0:T(8,128)} %solid_ref.5, f32[32,16,256]{2,1,0:T(8,128)} %rates_ref.5), custom_call_target="tpu_custom_call" | custom-call | flops 819200 | bytes 1228800 | tf_op jit(solution)/shard_map/edges/pallas_call | solution.py:237
  12.1 1.8 %collective-permute-start = (bf16[400,256]{1,0:T(8,128)(2,1)}, bf16[400,256]{1,0:T(8,128)(2,1)S(1)}, u32[]{:S(2)}, u32[]{:S(2)}) collective-permute-start(bf16[400,256]{1,0:T(8,128)(2,1)} %get-tuple-element.13), channel_id=1, source_target_pairs={{0,1},{1,2},{2,3},{3,4},{4,5},{5,6},{6,7},{7,8},{8,9},{9,10},{10,1... | collective-permute-start | bytes 614408 | tf_op jit(solution)/shard_map/ppermute | solution.py:669
  13.9 3.6 %collective-permute-start.1 = (bf16[400,256]{1,0:T(8,128)(2,1)}, bf16[400,256]{1,0:T(8,128)(2,1)S(1)}, u32[]{:S(2)}, u32[]{:S(2)}) collective-permute-start(bf16[400,256]{1,0:T(8,128)(2,1)} %get-tuple-element.14), channel_id=1, source_target_pairs={{1,0},{2,1},{3,2},{4,3},{5,4},{6,5},{7,6},{8,7},{9,8},{10,9},{11,1... | collective-permute-start | bytes 614408 | tf_op jit(solution)/shard_map/ppermute | solution.py:670
  17.5 8.7 %weights.1.weights_ref = f32[256,4096]{1,0:T(8,128)} custom-call(s32[1,4096]{1,0:T(1,128)} %bitcast.16, f32[256,1024]{1,0:T(8,128)} %bitcast.15), custom_call_target="tpu_custom_call" | custom-call | flops 4294967296 | bytes 5242880 | tf_op jit(solution)/shard_map/weights/pallas_call | solution.py:68
  26.2 0.0 collective-permute-done.low_ref.vz_low_ref
  26.2 0.0 copy-start
  26.2 0.0 collective-permute-done.1.high_ref.vz_high_ref
  26.2 0.7 copy-done
  26.9 0.0 copy-start.1
  26.9 0.7 copy-done.1
  27.6 8.1 %predictor.1 = (f32[128,16,256]{2,1,0:T(8,128)}, bf16[128,256]{1,0:T(8,128)(2,1)}, bf16[128,256]{1,0:T(8,128)(2,1)}) custom-call(f32[128,16,256]{2,1,0:T(8,128)} %flow_ref.5, f32[128,16,256]{2,1,0:T(8,128)} %flow_ref.5, f32[128,16,256]{2,1,0:T(8,128)} %flow_ref.5, bf16[400,256]{1,0:T(8,128)(2,1)} %copy-done, bf16[400,256]{1,0:T(8,128)(2,1)} %copy-done.1, ...), custom_call_target="tpu_custom_call" | custom-call | flops 20971520 | bytes 8388608 | tf_op jit(solution)/shard_map/predictor/pallas_call | solution.py:326
  35.6 0.7 collective-permute-start.4
  36.3 4.7 %collective-permute-start.5 = (bf16[128,256]{1,0:T(8,128)(2,1)}, bf16[128,256]{1,0:T(8,128)(2,1)S(1)}, u32[]{:S(2)}, u32[]{:S(2)}) collective-permute-start(bf16[128,256]{1,0:T(8,128)(2,1)} %get-tuple-element.20), channel_id=1, source_target_pairs={{1,0},{2,1},{3,2},{4,3},{5,4},{6,5},{7,6},{8,7},{9,8},{10,9},{11,1... | collective-permute-start | bytes 196616 | tf_op jit(solution)/shard_map/ppermute | solution.py:679
  41.0 0.0 all-to-all-done
  41.0 0.0 copy-start.5
  41.0 0.7 copy-done.5
  41.7 10.4 %forward.1 = (f32[16,256]{1,0:T(8,128)}, f32[1,256]{1,0:T(1,128)}, f32[1,256]{1,0:T(1,128)}) custom-call(s32[1,4096]{1,0:T(1,128)} %bitcast.9, s32[1,4096]{1,0:T(1,128)} %bitcast.11, s32[1,4096]{1,0:T(1,128)} %bitcast.13, f32[256,4096]{1,0:T(8,128)} %weights.1.weights_ref, s16[512,256]{1,0:T(8,128)(2,1)} %bitcast.8), custom_call_target="tpu_custom_call" | custom-call | flops 3221225472 | bytes 4194304 | tf_op jit(solution)/shard_map/forward/pallas_call | solution.py:172
  52.2 0.0 collective-permute-start.2
  52.2 5.3 %collective-permute-start.3 = (f32[1,256]{1,0:T(1,128)}, f32[1,256]{1,0:T(1,128)S(1)}, u32[]{:S(2)}, u32[]{:S(2)}) collective-permute-start(f32[1,256]{1,0:T(1,128)} %get-tuple-element.18), channel_id=1, source_target_pairs={{1,0},{2,1},{3,2},{4,3},{5,4},{6,5},{7,6},{8,7},{9,8},{10,9},{11,1... | collective-permute-start | bytes 3080 | tf_op jit(solution)/shard_map/ppermute | solution.py:683
  57.5 0.0 collective-permute-done.4.low_ref
  57.5 0.0 copy-start.3
  57.5 0.0 collective-permute-done.5.high_ref
  57.5 0.0 copy-start.4
  57.5 1.4 %collective-permute-done.2.wall_low_ref = f32[1,256]{1,0:T(1,128)S(1)} collective-permute-done((f32[1,256]{1,0:T(1,128)}, f32[1,256]{1,0:T(1,128)S(1)}, u32[]{:S(2)}, u32[]{:S(2)}) %collective-permute-start.2) | collective-permute-done | bytes 1056 | tf_op jit(solution)/shard_map/ppermute | solution.py:682
  59.0 0.0 copy-start.6
  59.0 0.0 collective-permute-done.3.wall_high_ref
  59.0 0.0 copy-start.7
  59.0 0.0 copy-done.3
  59.0 0.0 copy-done.4
  59.0 0.5 copy-done.6
  59.5 0.0 copy-done.7
  59.5 10.2 %backward.1 = (s16[32,24,256]{2,1,0:T(8,128)(2,1)}, f32[16,256]{1,0:T(8,128)}, f32[8,256]{1,0:T(8,128)}) custom-call(s32[1,4096]{1,0:T(1,128)} %bitcast.10, s32[1,4096]{1,0:T(1,128)} %bitcast.12, s32[1,4096]{1,0:T(1,128)} %bitcast.14, f32[256,4096]{1,0:T(8,128)} %weights.1.weights_ref, f32[16,256]{1,0:T(8,128)} %get-tuple-element.16.wall_ref, ...), custom_call_target="tpu_custom_call" | custom-call | flops 3221225472 | bytes 4194304 | tf_op jit(solution)/shard_map/backward/pallas_call | solution.py:491
  69.7 5.8 %all-to-all-start.1 = ((s16[32,24,256]{2,1,0:T(8,128)(2,1)}), s16[32,24,256]{2,1,0:T(8,128)(2,1)S(1)}, u32[]{:S(2)}, u32[]{:S(2)}) async-start(s16[32,24,256]{2,1,0:T(8,128)(2,1)} %get-tuple-element.23), calls=%async_computation.1 | async-start | bytes 786432 | tf_op jit(solution)/shard_map/all_to_all | solution.py:703
  75.6 3.8 %liner.1.rest_ref = f32[32,16,256]{2,1,0:T(8,128)} custom-call(f32[32,16,256]{2,1,0:T(8,128)} %solid_ref.5, f32[32,16,256]{2,1,0:T(8,128)} %rates_ref.5, bf16[400,256]{1,0:T(8,128)(2,1)} %copy-done, bf16[400,256]{1,0:T(8,128)(2,1)} %copy-done.1), custom_call_target="tpu_custom_call" | custom-call | flops 11010048 | bytes 2359296 | tf_op jit(solution)/shard_map/liner/pallas_call | solution.py:587
  79.3 8.5 %corrector.1 = f32[128,16,256]{2,1,0:T(8,128)} custom-call(f32[128,16,256]{2,1,0:T(8,128)} %get-tuple-element.15.mid_ref.below_ref.above_ref, f32[128,16,256]{2,1,0:T(8,128)} %get-tuple-element.15.mid_ref.below_ref.above_ref, f32[128,16,256]{2,1,0:T(8,128)} %get-tuple-element.15.mid_ref.below_ref.above_ref, f32[16,256]{1,0:T(8,128)} %get-tuple-element.21.top_ref, ...), custom_call_target="tpu_custom_call" | custom-call | flops 23068672 | bytes 10485760 | tf_op jit(solution)/shard_map/corrector/pallas_call | solution.py:373
  87.9 1.7 %all-to-all-done.1.arrived_ref = s16[32,24,256]{2,1,0:T(8,128)(2,1)S(1)} async-done(((s16[32,24,256]{2,1,0:T(8,128)(2,1)}), s16[32,24,256]{2,1,0:T(8,128)(2,1)S(1)}, u32[]{:S(2)}, u32[]{:S(2)}) %all-to-all-start.1) | async-done | bytes 393248 | tf_op jit(solution)/shard_map/all_to_all | solution.py:703
  89.6 0.0 copy-start.2
  89.6 0.7 copy-done.2
  90.4 2.2 %liner_top.1 = f32[32,16,256]{2,1,0:T(8,128)} custom-call(s16[32,24,256]{2,1,0:T(8,128)(2,1)} %copy-done.2, f32[32,16,256]{2,1,0:T(8,128)} %solid_ref.5, f32[32,16,256]{2,1,0:T(8,128)} %rates_ref.5, bf16[400,256]{1,0:T(8,128)(2,1)} %copy-done, bf16[400,256]{1,0:T(8,128)(2,1)} %copy-done.1, f32[32,16,256]{2,1,0:T(8,128)} %liner.1.rest_ref), custom_call_target="tpu_custom_call", output_to_operand_aliasing={{}: (5, {})} | custom-call | flops 2949120 | bytes 393216 | tf_op jit(solution)/shard_map/liner_top/pallas_call | solution.py:626
Async XLA Ops:
  2.1 38.9 %all-to-all-start = ((s16[32,16,256]{2,1,0:T(8,128)(2,1)}), s16[32,16,256]{2,1,0:T(8,128)(2,1)S(1)}, u32[]{:S(2)}, u32[]{:S(2)}) async-start(s16[32,16,256]{2,1,0:T(8,128)(2,1)} %broadcast_in_dim.21), calls=%async_computation | async-start | bytes 524288 | tf_op jit(solution)/shard_map/all_to_all | solution.py:665
  12.1 14.1 %collective-permute-start = (bf16[400,256]{1,0:T(8,128)(2,1)}, bf16[400,256]{1,0:T(8,128)(2,1)S(1)}, u32[]{:S(2)}, u32[]{:S(2)}) collective-permute-start(bf16[400,256]{1,0:T(8,128)(2,1)} %get-tuple-element.13), channel_id=1, source_target_pairs={{0,1},{1,2},{2,3},{3,4},{4,5},{5,6},{6,7},{7,8},{8,9},{9,10},{10,1... | collective-permute-start | bytes 614408 | tf_op jit(solution)/shard_map/ppermute | solution.py:669
  13.9 12.3 %collective-permute-start.1 = (bf16[400,256]{1,0:T(8,128)(2,1)}, bf16[400,256]{1,0:T(8,128)(2,1)S(1)}, u32[]{:S(2)}, u32[]{:S(2)}) collective-permute-start(bf16[400,256]{1,0:T(8,128)(2,1)} %get-tuple-element.14), channel_id=1, source_target_pairs={{1,0},{2,1},{3,2},{4,3},{5,4},{6,5},{7,6},{8,7},{9,8},{10,9},{11,1... | collective-permute-start | bytes 614408 | tf_op jit(solution)/shard_map/ppermute | solution.py:670
  26.2 0.7 copy-start
  26.9 0.7 copy-start.1
  35.6 21.9 %collective-permute-start.4 = (bf16[128,256]{1,0:T(8,128)(2,1)}, bf16[128,256]{1,0:T(8,128)(2,1)S(1)}, u32[]{:S(2)}, u32[]{:S(2)}) collective-permute-start(bf16[128,256]{1,0:T(8,128)(2,1)} %get-tuple-element.19), channel_id=1, source_target_pairs={{0,1},{1,2},{2,3},{3,4},{4,5},{5,6},{6,7},{7,8},{8,9},{9,10},{10,1... | collective-permute-start | bytes 196616 | tf_op jit(solution)/shard_map/ppermute | solution.py:678
  36.3 21.2 %collective-permute-start.5 = (bf16[128,256]{1,0:T(8,128)(2,1)}, bf16[128,256]{1,0:T(8,128)(2,1)S(1)}, u32[]{:S(2)}, u32[]{:S(2)}) collective-permute-start(bf16[128,256]{1,0:T(8,128)(2,1)} %get-tuple-element.20), channel_id=1, source_target_pairs={{1,0},{2,1},{3,2},{4,3},{5,4},{6,5},{7,6},{8,7},{9,8},{10,9},{11,1... | collective-permute-start | bytes 196616 | tf_op jit(solution)/shard_map/ppermute | solution.py:679
  41.0 0.7 copy-start.5
  52.2 6.8 %collective-permute-start.2 = (f32[1,256]{1,0:T(1,128)}, f32[1,256]{1,0:T(1,128)S(1)}, u32[]{:S(2)}, u32[]{:S(2)}) collective-permute-start(f32[1,256]{1,0:T(1,128)} %get-tuple-element.17), channel_id=1, source_target_pairs={{0,1},{1,2},{2,3},{3,4},{4,5},{5,6},{6,7},{7,8},{8,9},{9,10},{10,1... | collective-permute-start | bytes 3080 | tf_op jit(solution)/shard_map/ppermute | solution.py:682
  52.2 6.8 %collective-permute-start.3 = (f32[1,256]{1,0:T(1,128)}, f32[1,256]{1,0:T(1,128)S(1)}, u32[]{:S(2)}, u32[]{:S(2)}) collective-permute-start(f32[1,256]{1,0:T(1,128)} %get-tuple-element.18), channel_id=1, source_target_pairs={{1,0},{2,1},{3,2},{4,3},{5,4},{6,5},{7,6},{8,7},{9,8},{10,9},{11,1... | collective-permute-start | bytes 3080 | tf_op jit(solution)/shard_map/ppermute | solution.py:683
  57.5 1.5 %copy-start.3 = (bf16[128,256]{1,0:T(8,128)(2,1)}, bf16[128,256]{1,0:T(8,128)(2,1)S(1)}, u32[]{:S(2)}) copy-start(bf16[128,256]{1,0:T(8,128)(2,1)S(1)} %collective-permute-done.4.low_ref) | copy-start | bytes 196612
  57.5 1.5 %copy-start.4 = (bf16[128,256]{1,0:T(8,128)(2,1)}, bf16[128,256]{1,0:T(8,128)(2,1)S(1)}, u32[]{:S(2)}) copy-start(bf16[128,256]{1,0:T(8,128)(2,1)S(1)} %collective-permute-done.5.high_ref) | copy-start | bytes 196612
  59.0 0.6 copy-start.6
  59.0 0.6 copy-start.7
  69.7 19.9 %all-to-all-start.1 = ((s16[32,24,256]{2,1,0:T(8,128)(2,1)}), s16[32,24,256]{2,1,0:T(8,128)(2,1)S(1)}, u32[]{:S(2)}, u32[]{:S(2)}) async-start(s16[32,24,256]{2,1,0:T(8,128)(2,1)} %get-tuple-element.23), calls=%async_computation.1 | async-start | bytes 786432 | tf_op jit(solution)/shard_map/all_to_all | solution.py:703
  89.6 0.8 copy-start.2

commit v2 on v1

--- a/solution.py
+++ b/solution.py
@@ -16,7 +16,9 @@
 
 AXES = ("grp", "dom")
 NODES = 16
-CHUNK = 512
+CHUNK = 2048
+WEIGHT_CHUNK = 1024
+BLOCK = 64
 LANES = 128
 LAYERS = 16
 HALO = 4
@@ -36,8 +38,18 @@
 
 
 def one_hot(index, rows):
-    cells = lax.broadcasted_iota(jnp.int32, (rows, index.shape[1]), 0)
-    return jnp.where(cells == index, 1.0, 0.0).astype(BF16)
+    count = index.shape[1]
+    wide = jnp.broadcast_to(index, (NODES, count))
+    cells = lax.broadcasted_iota(jnp.int32, (NODES, count), 0)
+    inner = min(rows, 128)
+    low = wide % inner
+    high = wide // inner
+    parts = [jnp.where(cells + g == low, 1.0, 0.0).astype(BF16) for g in range(0, inner, NODES)]
+    out = []
+    for h in range(-(-rows // inner)):
+        mask = jnp.where(high == h, 1.0, 0.0).astype(BF16)
+        out.extend([p * mask for p in parts])
+    return jnp.concatenate(out, axis=0)
 
 
 def dot(a, b):
@@ -53,13 +65,22 @@
     return high, (x - high.astype(F32)).astype(BF16)
 
 
-def weights_kernel(block_ref, table_ref, out_ref, table_high, table_low):
+def stack(x):
+    return jnp.concatenate(split(x), axis=0)
+
+
+def fold(x):
+    half = x.shape[0] // 2
+    return x[:half] + x[half:]
+
+
+def weights_kernel(block_ref, table_ref, out_ref, table):
     @pl.when(pl.program_id(0) == 0)
     def _():
-        table_high[...], table_low[...] = split(table_ref[...])
+        table[...] = stack(table_ref[...])
 
     picked = one_hot(block_ref[...], table_ref.shape[1])
-    out_ref[...] = dot(table_high[...], picked) + dot(table_low[...], picked)
+    out_ref[...] = fold(dot(table[...], picked))
 
 
 def weights_of(block_index, table):
@@ -67,14 +88,14 @@
     count = block_index.shape[1]
     return pl.pallas_call(
         weights_kernel,
-        grid=(count // CHUNK,),
+        grid=(count // WEIGHT_CHUNK,),
         in_specs=[
-            pl.BlockSpec((1, CHUNK), lambda i: (0, i)),
+            pl.BlockSpec((1, WEIGHT_CHUNK), lambda i: (0, i)),
             pl.BlockSpec((entries, blocks), lambda i: (0, 0)),
         ],
-        out_specs=pl.BlockSpec((entries, CHUNK), lambda i: (0, i)),
+        out_specs=pl.BlockSpec((entries, WEIGHT_CHUNK), lambda i: (0, i)),
         out_shape=jax.ShapeDtypeStruct((entries, count), F32),
-        scratch_shapes=[pltpu.VMEM((entries, blocks), BF16)] * 2,
+        scratch_shapes=[pltpu.VMEM((2 * entries, blocks), BF16)],
         compiler_params=params(),
         cost_estimate=cost(4 * entries * blocks * count, 4 * entries * (blocks + count)),
         name="weights",
@@ -121,14 +142,19 @@
     flow_p_ref,
     weights_ref,
     faces_ref,
+    edge_low_ref,
+    edge_high_ref,
+    under_ref,
+    flow_ref,
+    velocity_ref,
+    heat_ref,
     wall_ref,
+    top_ref,
     first_ref,
     last_ref,
-    faces_high,
-    faces_low,
+    faces_turned,
     fetched,
-    product_high,
-    product_low,
+    product,
     total,
 ):
     step = pl.program_id(0)
@@ -136,12 +162,12 @@
 
     @pl.when(step == 0)
     def _():
-        faces_high[...], faces_low[...] = split(faces_ref[...].astype(F32).T)
+        faces_turned[...] = stack(faces_ref[...].astype(F32).T)
         total[...] = jnp.zeros_like(total)
 
     solid_x, solid_c = solid_place(device_ref, patch_ref, rows_x)
     picked = one_hot(solid_x, faces_ref.shape[0])
-    fetched[...] = dot(faces_high[...], picked) + dot(faces_low[...], picked)
+    fetched[...] = fold(dot(faces_turned[...], picked))
     for k in range(CHUNK // LANES):
         lanes = slice(k * LANES, (k + 1) * LANES)
         c = jnp.broadcast_to(solid_c[:, lanes], (NODES, LANES))
@@ -151,22 +177,41 @@
         values = values * (1.0 / STEPS_PER_UNIT)
         for i in range(NODES):
             rows = slice(i * NODES, (i + 1) * NODES)
-            product_high[rows, lanes], product_low[rows, lanes] = split(weights_ref[rows, lanes] * values)
+            high, low = split(weights_ref[rows, lanes] * values)
+            product[rows, lanes] = high
+            product[NODES * NODES + i * NODES : NODES * NODES + (i + 1) * NODES, lanes] = low
     placed = one_hot(flow_p_ref[...], total.shape[1])
-    total[...] += dot_nt(product_high[...], placed) + dot_nt(product_low[...], placed)
+    total[...] += dot_nt(product[...], placed)
 
     @pl.when(step == pl.num_programs(0) - 1)
     def _():
-        patches = jnp.sum(total[...].reshape(NODES, NODES, total.shape[1]), axis=1)
+        patches = jnp.sum(fold(total[...]).reshape(NODES, NODES, total.shape[1]), axis=1)
         wall = patches_to_face(patches, rows_x)
         wall_ref[...] = wall
-        first_ref[...] = wall[:1]
-        last_ref[...] = wall[rows_x - 1 :]
-
-
-def forward(solid_device, solid_patch, flow_p, weights, faces, rows_x):
+        edge = edge_low_ref.shape[0]
+        lows = edge_low_ref[...].astype(F32)
+        highs = edge_high_ref[...].astype(F32)
+        for l in range(2):
+            centre = flow_ref[l]
+            zlow = under_ref[1] if l == 0 else flow_ref[0]
+            zhigh = flow_ref[1] if l == 0 else wall
+            row = slice(edge - 2 + l, edge - 1 + l)
+            xlow, xhigh = x_neighbours(centre, lows[row], highs[row])
+            vz, vx, vy = (velocity_ref[d, l].astype(F32) for d in range(3))
+            top_ref[l] = centre + TIMESTEP * layer_tendency(
+                centre, zlow, zhigh, xlow, xhigh, vz, vx, vy, heat_ref[l].astype(F32)
+            )
+        first_ref[...] = top_ref[1, :1]
+        last_ref[...] = top_ref[1, rows_x - 1 :]
+
+
+def forward(solid_device, solid_patch, flow_p, weights, faces, edge_low, edge_high, flow, velocity, heat):
     entries, count = weights.shape
     tall, width = faces.shape
+    layers, rows_x = flow.shape[:2]
+    last = edge_low.shape[0] // LAYERS - 1
+    edge = pl.BlockSpec((LAYERS, width), lambda i: (last, 0))
+    pair = pl.BlockSpec((2, rows_x, width), lambda i: (layers // 2 - 1, 0, 0))
     line = pl.BlockSpec((1, CHUNK), lambda i: (0, i))
     fixed = lambda shape: pl.BlockSpec(shape, lambda i: (0,) * len(shape))
     return pl.pallas_call(
@@ -178,29 +223,34 @@
             line,
             pl.BlockSpec((entries, CHUNK), lambda i: (0, i)),
             fixed((tall, width)),
-        ],
-        out_specs=[fixed((rows_x, width)), fixed((1, width)), fixed((1, width))],
+            edge,
+            edge,
+            pl.BlockSpec((2, rows_x, width), lambda i: (layers // 2 - 2, 0, 0)),
+            pair,
+            pl.BlockSpec((3, 2, rows_x, width), lambda i: (0, layers // 2 - 1, 0, 0)),
+            pair,
+        ],
+        out_specs=[fixed((rows_x, width)), fixed((2, rows_x, width)), fixed((1, width)), fixed((1, width))],
         out_shape=[
             jax.ShapeDtypeStruct((rows_x, width), F32),
+            jax.ShapeDtypeStruct((2, rows_x, width), F32),
             jax.ShapeDtypeStruct((1, width), F32),
             jax.ShapeDtypeStruct((1, width), F32),
         ],
         scratch_shapes=[
-            pltpu.VMEM((width, tall), BF16),
-            pltpu.VMEM((width, tall), BF16),
+            pltpu.VMEM((2 * width, tall), BF16),
             pltpu.VMEM((width, CHUNK), F32),
-            pltpu.VMEM((entries, CHUNK), BF16),
-            pltpu.VMEM((entries, CHUNK), BF16),
-            pltpu.VMEM((entries, rows_x * NODES), F32),
+            pltpu.VMEM((2 * entries, CHUNK), BF16),
+            pltpu.VMEM((2 * entries, rows_x * NODES), F32),
         ],
         compiler_params=params(),
         cost_estimate=cost(4 * width * (tall + entries) * count, 4 * entries * count),
         name="forward",
-    )(solid_device, solid_patch, flow_p, weights, faces)
+    )(solid_device, solid_patch, flow_p, weights, faces, edge_low, edge_high, flow, flow, velocity, heat)
 
 
 def edges_kernel(
-    flow_low_ref, flow_high_ref, speed_ref, solid_ref, rates_ref, up_ref, down_ref
+    flow_low_ref, flow_high_ref, solid_ref, rates_ref, up_ref, down_ref
 ):
     layers = flow_low_ref.shape[0]
     solid_layers, rows, width = solid_ref.shape
@@ -223,16 +273,12 @@
         down_ref[part] = jnp.concatenate(
             [flow_low_ref[m, 0:1] for m in range(l, l + LAYERS)], axis=0
         ).astype(BF16)
-    part = slice(start + layers, start + layers + LAYERS)
-    speed = speed_ref[0, 0].astype(F32)
-    up_ref[part] = jnp.broadcast_to(speed[rows - 1 :], (LAYERS, width)).astype(BF16)
-    down_ref[part] = jnp.broadcast_to(speed[:1], (LAYERS, width)).astype(BF16)
-
-
-def edges(flow, velocity, solid, rates):
+
+
+def edges(flow, solid, rates):
     layers, rows, width = flow.shape
     solid_layers = solid.shape[0]
-    shape = (solid_layers * 8 + layers + LAYERS, width)
+    shape = (solid_layers * 8 + layers, width)
     whole = pl.BlockSpec(solid.shape, lambda i: (0, 0, 0))
     return pl.pallas_call(
         edges_kernel,
@@ -240,7 +286,6 @@
         in_specs=[
             pl.BlockSpec((layers, 8, width), lambda i: (0, 0, 0)),
             pl.BlockSpec((layers, 8, width), lambda i: (0, rows // 8 - 1, 0)),
-            pl.BlockSpec((1, 1, rows, width), lambda i: (0, layers - 1, 0, 0)),
             whole,
             whole,
         ],
@@ -249,7 +294,7 @@
         compiler_params=params(),
         cost_estimate=cost(8 * shape[0] * width, 12 * shape[0] * width),
         name="edges",
-    )(flow, flow, velocity, solid, rates)
+    )(flow, flow, solid, rates)
 
 
 def layer_tendency(centre, zlow, zhigh, xlow, xhigh, vz, vx, vy, source):
@@ -285,13 +330,13 @@
     highs = high_ref[...].astype(F32)
     first, last = [], []
     rows = flow_ref.shape[1]
-    for l in range(LAYERS):
+    for l in range(BLOCK):
         centre = flow_ref[l]
         if l == 0:
             zlow = jnp.where(step == 0, 0.0, below_ref[0])
         else:
             zlow = flow_ref[l - 1]
-        if l == LAYERS - 1:
+        if l == BLOCK - 1:
             zhigh = jnp.where(step == pl.num_programs(0) - 1, 0.0, above_ref[0])
         else:
             zhigh = flow_ref[l + 1]
@@ -309,11 +354,11 @@
 
 def layer_specs(shape, halo=True):
     layers, rows, width = shape
-    block = pl.BlockSpec((LAYERS, rows, width), lambda i: (i, 0, 0))
-    below = pl.BlockSpec((1, rows, width), lambda i: (jnp.maximum(i * LAYERS - 1, 0), 0, 0))
-    above = pl.BlockSpec((1, rows, width), lambda i: (jnp.minimum((i + 1) * LAYERS, layers - 1), 0, 0))
-    speeds = pl.BlockSpec((3, LAYERS, rows, width), lambda i: (0, i, 0, 0))
-    edge = pl.BlockSpec((LAYERS, width), lambda i: (i, 0))
+    block = pl.BlockSpec((BLOCK, rows, width), lambda i: (i, 0, 0))
+    below = pl.BlockSpec((1, rows, width), lambda i: (jnp.maximum(i * BLOCK - 1, 0), 0, 0))
+    above = pl.BlockSpec((1, rows, width), lambda i: (jnp.minimum((i + 1) * BLOCK, layers - 1), 0, 0))
+    speeds = pl.BlockSpec((3, BLOCK, rows, width), lambda i: (0, i, 0, 0))
+    edge = pl.BlockSpec((BLOCK, width), lambda i: (i, 0))
     return block, below, above, speeds, edge
 
 
@@ -321,11 +366,11 @@
     layers, rows, width = flow.shape
     block, below, above, speeds, edge = layer_specs(flow.shape)
     cells = layers * rows * width
-    first_edge = low.shape[0] // LAYERS - layers // LAYERS - 1
-    flow_edge = pl.BlockSpec((LAYERS, width), lambda i: (i + first_edge, 0))
+    first_edge = (low.shape[0] - layers) // BLOCK
+    flow_edge = pl.BlockSpec((BLOCK, width), lambda i: (i + first_edge, 0))
     return pl.pallas_call(
         predictor_kernel,
-        grid=(layers // LAYERS,),
+        grid=(layers // BLOCK,),
         in_specs=[below, block, above, flow_edge, flow_edge, speeds, block],
         out_specs=[block, edge, edge],
         out_shape=[
@@ -340,23 +385,35 @@
 
 
 def corrector_kernel(
-    below_ref, mid_ref, above_ref, top_ref, wall_ref, rim_ref, low_ref, high_ref, flow_ref, velocity_ref, heat_ref, out_ref
+    below_ref,
+    mid_ref,
+    above_ref,
+    top_ref,
+    wall_ref,
+    top_low_ref,
+    top_high_ref,
+    low_ref,
+    high_ref,
+    flow_ref,
+    velocity_ref,
+    heat_ref,
+    out_ref,
 ):
     step = pl.program_id(0)
     final = step == pl.num_programs(0) - 1
     lows = low_ref[...].astype(F32)
     highs = high_ref[...].astype(F32)
-    for l in range(LAYERS):
+    for l in range(BLOCK):
         centre = mid_ref[l]
         low_row, high_row = lows[l : l + 1], highs[l : l + 1]
         zlow = jnp.where(step == 0, 0.0, below_ref[0]) if l == 0 else mid_ref[l - 1]
-        if l == LAYERS - 1:
-            centre = jnp.where(final, top_ref[...], centre)
+        if l == BLOCK - 1:
+            centre = jnp.where(final, top_ref[1], centre)
             zhigh = jnp.where(final, wall_ref[...], above_ref[0])
-            low_row = jnp.where(final, rim_ref[0:1], low_row)
-            high_row = jnp.where(final, rim_ref[1:2], high_row)
-        elif l == LAYERS - 2:
-            zhigh = jnp.where(final, top_ref[...], mid_ref[l + 1])
+            low_row = jnp.where(final, top_low_ref[...], low_row)
+            high_row = jnp.where(final, top_high_ref[...], high_row)
+        elif l == BLOCK - 2:
+            zhigh = jnp.where(final, top_ref[1], mid_ref[l + 1])
         else:
             zhigh = mid_ref[l + 1]
         xlow, xhigh = x_neighbours(centre, low_row, high_row)
@@ -365,21 +422,22 @@
         out_ref[l] = 0.5 * flow_ref[l] + 0.5 * (centre + TIMESTEP * slope)
 
 
-def corrector(mid, top, wall, rim, low, high, flow, velocity, heat):
+def corrector(mid, top, wall, top_low, top_high, low, high, flow, velocity, heat):
     layers, rows, width = flow.shape
     block, below, above, speeds, edge = layer_specs(flow.shape)
     face = pl.BlockSpec((rows, width), lambda i: (0, 0))
+    line = pl.BlockSpec((1, width), lambda i: (0, 0))
     cells = layers * rows * width
     return pl.pallas_call(
         corrector_kernel,
-        grid=(layers // LAYERS,),
-        in_specs=[below, block, above, face, face, pl.BlockSpec(rim.shape, lambda i: (0, 0)), edge, edge, block, speeds, block],
+        grid=(layers // BLOCK,),
+        in_specs=[below, block, above, pl.BlockSpec(top.shape, lambda i: (0, 0, 0)), face, line, line, edge, edge, block, speeds, block],
         out_specs=block,
         out_shape=jax.ShapeDtypeStruct(flow.shape, F32),
         compiler_params=params(),
         cost_estimate=cost(44 * cells, 20 * cells),
         name="corrector",
-    )(mid, mid, mid, top, wall, rim, low, high, flow, velocity, heat)
+    )(mid, mid, mid, top, wall, top_low, top_high, low, high, flow, velocity, heat)
 
 
 def backward_kernel(
@@ -388,19 +446,13 @@
     flow_p_ref,
     weights_ref,
     wall_ref,
-    wall_low_ref,
-    wall_high_ref,
-    vz_low_ref,
-    vz_high_ref,
-    mid_ref,
+    top_ref,
     low_ref,
     high_ref,
     flow_ref,
     velocity_ref,
     heat_ref,
     send_ref,
-    top_ref,
-    rim_ref,
     flux_high,
     flux_low,
     fetched,
@@ -416,21 +468,10 @@
         total[...] = jnp.zeros_like(total)
         wall = wall_ref[...]
         vz, vx, vy = (velocity_ref[d, 0].astype(F32) for d in range(3))
-        top = mid_ref[1] + TIMESTEP * (DIFFUSION - jnp.minimum(vz, 0.0)) * wall
-        edge = low_ref.shape[0]
-        low_row = low_ref[edge - 1 : edge].astype(F32) + TIMESTEP * (
-            DIFFUSION - jnp.minimum(vz_low_ref[...].astype(F32)[:1], 0.0)
-        ) * wall_low_ref[...]
-        high_row = high_ref[edge - 1 : edge].astype(F32) + TIMESTEP * (
-            DIFFUSION - jnp.minimum(vz_high_ref[...].astype(F32)[:1], 0.0)
-        ) * wall_high_ref[...]
-        xlow, xhigh = x_neighbours(top, low_row, high_row)
-        slope = layer_tendency(top, mid_ref[0], wall, xlow, xhigh, vz, vx, vy, heat_ref[0].astype(F32))
+        top = top_ref[1]
+        xlow, xhigh = x_neighbours(top, low_ref[...], high_ref[...])
+        slope = layer_tendency(top, top_ref[0], wall, xlow, xhigh, vz, vx, vy, heat_ref[0].astype(F32))
         out = 0.5 * flow_ref[0] + 0.5 * (top + TIMESTEP * slope)
-        top_ref[...] = top
-        rim_ref[...] = jnp.zeros_like(rim_ref)
-        rim_ref[0:1] = low_row
-        rim_ref[1:2] = high_row
         patches = face_to_patches(FILM_COEFF * (out - wall), rows)
         wide = jnp.broadcast_to(patches[:, None, :], (NODES, NODES, patches.shape[1]))
         high, low = split(wide.reshape(NODES * NODES, patches.shape[1]))
@@ -478,16 +519,13 @@
             send_ref[d] = scaled.astype(jnp.int32).astype(I16)
 
 
-def backward(solid_device, solid_patch, flow_p, weights, wall, wall_low, wall_high, edge_low, edge_high, mid, low, high, flow, velocity, heat, devices):
+def backward(solid_device, solid_patch, flow_p, weights, wall, top, low, high, flow, velocity, heat, devices):
     entries, count = weights.shape
     rows, width = wall.shape
     layers = flow.shape[0]
     tall = devices * rows
     line = pl.BlockSpec((1, CHUNK), lambda i: (0, i))
     fixed = lambda shape: pl.BlockSpec(shape, lambda i: (0,) * len(shape))
-    edge = pl.BlockSpec((LAYERS, width), lambda i: (layers // LAYERS - 1, 0))
-    last = edge_low.shape[0] // LAYERS - 1
-    speed = pl.BlockSpec((LAYERS, width), lambda i: (last, 0))
     return pl.pallas_call(
         backward_kernel,
         grid=(count // CHUNK,),
@@ -497,23 +535,15 @@
             line,
             pl.BlockSpec((entries, CHUNK), lambda i: (0, i)),
             fixed((rows, width)),
+            fixed((2, rows, width)),
             fixed((1, width)),
             fixed((1, width)),
-            speed,
-            speed,
-            pl.BlockSpec((2, rows, width), lambda i: (layers // 2 - 1, 0, 0)),
-            edge,
-            edge,
             pl.BlockSpec((1, rows, width), lambda i: (layers - 1, 0, 0)),
             pl.BlockSpec((3, 1, rows, width), lambda i: (0, layers - 1, 0, 0)),
             pl.BlockSpec((1, rows, width), lambda i: (layers - 1, 0, 0)),
         ],
-        out_specs=[fixed((devices, rows + 8, width)), fixed((rows, width)), fixed((8, width))],
-        out_shape=[
-            jax.ShapeDtypeStruct((devices, rows + 8, width), I16),
-            jax.ShapeDtypeStruct((rows, width), F32),
-            jax.ShapeDtypeStruct((8, width), F32),
-        ],
+        out_specs=fixed((devices, rows + 8, width)),
+        out_shape=jax.ShapeDtypeStruct((devices, rows + 8, width), I16),
         scratch_shapes=[
             pltpu.VMEM((entries, rows * NODES), BF16),
             pltpu.VMEM((entries, rows * NODES), BF16),
@@ -525,7 +555,7 @@
         compiler_params=params(),
         cost_estimate=cost(4 * width * (tall + entries) * count, 4 * entries * count),
         name="backward",
-    )(solid_device, solid_patch, flow_p, weights, wall, wall_low, wall_high, edge_low, edge_high, mid, low, high, flow, velocity, heat)
+    )(solid_device, solid_patch, flow_p, weights, wall, top, low, high, flow, velocity, heat)
 
 
 def conduct(current, layers, rates, flux):
@@ -665,7 +695,7 @@
     faces = lax.all_to_all(outgoing, AXES, split_axis=0, concat_axis=0, tiled=True)
     faces = faces.reshape(devices * rows, width)
 
-    to_up, to_down = edges(flow_temp, velocity, solid_temp, conductivity)
+    to_up, to_down = edges(flow_temp, solid_temp, conductivity)
     before = lax.ppermute(to_up, AXES, up)
     after = lax.ppermute(to_down, AXES, down)
 
@@ -674,34 +704,37 @@
     flow_p = flow_patch[None]
     weights = weights_of(block_index[None], interp_table.reshape(NODES * NODES, -1))
 
+    wall, top, top_first, top_last = forward(
+        solid_device, solid_patch, flow_p, weights, faces, before, after, flow_temp, velocity, heat_release
+    )
+    top_low = lax.ppermute(top_last, AXES, up)
+    top_high = lax.ppermute(top_first, AXES, down)
+
+    before, after, wall = lax.optimization_barrier((before, after, wall))
     mid, mid_first, mid_last = predictor(flow_temp, before, after, velocity, heat_release)
     mid_low = lax.ppermute(mid_last, AXES, up)
     mid_high = lax.ppermute(mid_first, AXES, down)
-
-    wall, wall_first, wall_last = forward(solid_device, solid_patch, flow_p, weights, faces, rows)
-    wall_low = lax.ppermute(wall_last, AXES, up)
-    wall_high = lax.ppermute(wall_first, AXES, down)
-
-    sending, top, rim = backward(
+    top_low, top_high, mid_first = lax.optimization_barrier((top_low, top_high, mid_first))
+
+    sending = backward(
         solid_device,
         solid_patch,
         flow_p,
         weights,
         wall,
-        wall_low,
-        wall_high,
-        before,
-        after,
-        mid,
-        mid_low,
-        mid_high,
+        top,
+        top_low,
+        top_high,
         flow_temp,
         velocity,
         heat_release,
         devices,
     )
+    sending, top, before = lax.optimization_barrier((sending, top, before))
     arrived = lax.all_to_all(sending, AXES, split_axis=0, concat_axis=0, tiled=True)
-    flow_out = corrector(mid, top, wall, rim, mid_low, mid_high, flow_temp, velocity, heat_release)
+    flow_out = corrector(
+        mid, top, wall, top_low, top_high, mid_low, mid_high, flow_temp, velocity, heat_release
+    )
     rest = liner(solid_temp, conductivity, before, after)
     solid_out = liner_top(arrived, solid_temp, conductivity, before, after, rest)
     return (flow_out, solid_out)

time: 93.6 us -> 79.7 us (0.85)
  Pallas kernels: 54.7 us -> 43 us
  starting transfers between devices: 29.2 us -> 26.2 us
  waiting for transfers between devices: 3.19 us -> 5.13 us
    pallas_call x3, Pallas kernels: 25.3 us -> 19.9 us  [the longest x1 7.57 us: weights_of(): pl.pallas_call(weights_kernel, grid=(count // WEIGHT_CHUNK,), in_specs=[p...]
    ppermute x1, waiting for transfers between devices: 0.01 us -> 4.5 us  [body(): mid_low = lax.ppermute(mid_last, AXES, up)]
    all_to_all x1, starting transfers between devices: 5.84 us -> 2.59 us  [body(): lax.all_to_all(sending, AXES, split_axis=0, concat_axis=0, tiled=True)]
    pallas_call x1, Pallas kernels: 10.4 us -> 7.26 us  [forward(): pl.pallas_call(forward_kernel, grid=(count // CHUNK,), in_specs=[line, li...]
    pallas_call x1, Pallas kernels: 10.2 us -> 7.17 us  [backward(): pl.pallas_call(backward_kernel, grid=(count // CHUNK,), in_specs=[line, l...]
    all_to_all x1, waiting for transfers between devices: 1.74 us -> 0.01 us  [body(): lax.all_to_all(sending, AXES, split_axis=0, concat_axis=0, tiled=True)]
    ppermute x2, waiting for transfers between devices: 1.44 us -> 0.01 us  [the longest x1 0.01 us: body(): top_low = lax.ppermute(top_last, AXES, up)]
    ppermute x1, starting transfers between devices: 0.66 us -> 1.69 us  [body(): mid_low = lax.ppermute(mid_last, AXES, up)]
  transfers between devices with their start and end apart: 8 -> 8, of which waited for: 2 -> 2; matrix products, arithmetic and copies ran while one was open for 0% -> 0% of each run, Pallas kernels for 46% -> 33%
where the time goes in v2:
time: 79.7 us; the launch traced here: 79.2 us
  Pallas kernels  43 us (54%)
  starting transfers between devices  26.2 us (33%)
  waiting for transfers between devices  5.13 us (6%)
  local copies, waits for them, and re-layouts  3.44 us (4%)
    pallas_call x1, Pallas kernels, weights_of(): pl.pallas_call(weights_kernel, grid=(count // WEIGHT_CHUNK,), in_specs=[p...  7.57 us
    all_to_all x1, starting transfers between devices, body(): lax.all_to_all(outgoing, AXES, split_axis=0, concat_axis=0, tiled=True)  7.3 us
    pallas_call x1, Pallas kernels, forward(): pl.pallas_call(forward_kernel, grid=(count // CHUNK,), in_specs=[line, li...  7.26 us
    pallas_call x1, Pallas kernels, backward(): pl.pallas_call(backward_kernel, grid=(count // CHUNK,), in_specs=[line, l...  7.17 us
    pallas_call x1, Pallas kernels, corrector(): pl.pallas_call(corrector_kernel, grid=(layers // BLOCK,), in_specs=[below...  6.35 us
    pallas_call x1, Pallas kernels, predictor(): pl.pallas_call(predictor_kernel, grid=(layers // BLOCK,), in_specs=[below...  5.99 us
    ppermute x1, waiting for transfers between devices, body(): mid_low = lax.ppermute(mid_last, AXES, up)  4.5 us
    ppermute x1, starting transfers between devices, body(): top_high = lax.ppermute(top_first, AXES, down)  3.86 us
  transfers between devices with their start and end apart: 8, of which 2 were waited for; matrix products, arithmetic and copies ran while one was open for 0% of the time, Pallas kernels for 33%

profile of v2, /device:TPU:0, one launch (start us, length us, event | category | flops | bytes accessed | tf_op | source)
XLA Modules:
  0.0 79.2 jit_solution(10166169962464223900)
XLA Ops:
  0.6 0.7 fusion
  1.4 0.7 broadcast_in_dim.21
  2.1 7.3 %all-to-all-start = ((s16[32,16,256]{2,1,0:T(8,128)(2,1)}), s16[32,16,256]{2,1,0:T(8,128)(2,1)S(1)}, u32[]{:S(2)}, u32[]{:S(2)}) async-start(s16[32,16,256]{2,1,0:T(8,128)(2,1)} %broadcast_in_dim.21), calls=%async_computation | async-start | bytes 524288 | tf_op jit(solution)/shard_map/all_to_all | solution.py:695
  9.4 2.7 %edges.1 = (bf16[384,256]{1,0:T(8,128)(2,1)}, bf16[384,256]{1,0:T(8,128)(2,1)}) custom-call(f32[128,16,256]{2,1,0:T(8,128)} %flow_ref.7, f32[128,16,256]{2,1,0:T(8,128)} %flow_ref.7, f32[32,16,256]{2,1,0:T(8,128)} %solid_ref.5, f32[32,16,256]{2,1,0:T(8,128)} %rates_ref.5), custom_call_target="tpu_custom_call" | custom-call | flops 786432 | bytes 1179648 | tf_op jit(solution)/shard_map/edges/pallas_call | solution.py:283
  12.1 1.8 %collective-permute-start = (bf16[384,256]{1,0:T(8,128)(2,1)}, bf16[384,256]{1,0:T(8,128)(2,1)S(1)}, u32[]{:S(2)}, u32[]{:S(2)}) collective-permute-start(bf16[384,256]{1,0:T(8,128)(2,1)} %get-tuple-element.19), channel_id=1, source_target_pairs={{0,1},{1,2},{2,3},{3,4},{4,5},{5,6},{6,7},{7,8},{8,9},{9,10},{10,1... | collective-permute-start | bytes 589832 | tf_op jit(solution)/shard_map/ppermute | solution.py:699
  13.9 3.6 %collective-permute-start.1 = (bf16[384,256]{1,0:T(8,128)(2,1)}, bf16[384,256]{1,0:T(8,128)(2,1)S(1)}, u32[]{:S(2)}, u32[]{:S(2)}) collective-permute-start(bf16[384,256]{1,0:T(8,128)(2,1)} %get-tuple-element.20), channel_id=1, source_target_pairs={{1,0},{2,1},{3,2},{4,3},{5,4},{6,5},{7,6},{8,7},{9,8},{10,9},{11,1... | collective-permute-start | bytes 589832 | tf_op jit(solution)/shard_map/ppermute | solution.py:700
  17.5 7.6 %weights.1.weights_ref = f32[256,4096]{1,0:T(8,128)} custom-call(s32[1,4096]{1,0:T(1,128)} %bitcast.16, f32[256,1024]{1,0:T(8,128)} %bitcast.15), custom_call_target="tpu_custom_call" | custom-call | flops 4294967296 | bytes 5242880 | tf_op jit(solution)/shard_map/weights/pallas_call | solution.py:89
  25.0 0.0 collective-permute-done.edge_low_ref.low_ref
  25.0 0.0 copy-start
  25.0 0.6 collective-permute-done.1.edge_high_ref.high_ref
  25.6 0.0 copy-start.1
  25.6 0.0 all-to-all-done
  25.6 0.0 copy-start.3
  25.6 0.1 copy-done
  25.7 0.6 copy-done.1
  26.3 0.1 copy-done.3
  26.4 7.3 %forward.1 = (f32[16,256]{1,0:T(8,128)}, f32[2,16,256]{2,1,0:T(8,128)}, f32[1,256]{1,0:T(1,128)}, f32[1,256]{1,0:T(1,128)}) custom-call(s32[1,4096]{1,0:T(1,128)} %bitcast.9, s32[1,4096]{1,0:T(1,128)} %bitcast.11, s32[1,4096]{1,0:T(1,128)} %bitcast.13, f32[256,4096]{1,0:T(8,128)} %weights.1.weights_ref, s16[512,256]{1,0:T(8,128)(2,1)} %bitcast.8, ...), custom_call_target="tpu_custom_call" | custom-call | flops 3221225472 | bytes 4194304 | tf_op jit(solution)/shard_map/forward/pallas_call | solution.py:217
  33.7 1.5 %collective-permute-start.2 = (f32[1,256]{1,0:T(1,128)}, f32[1,256]{1,0:T(1,128)S(1)}, u32[]{:S(2)}, u32[]{:S(2)}) collective-permute-start(f32[1,256]{1,0:T(1,128)} %get-tuple-element.27), channel_id=1, source_target_pairs={{0,1},{1,2},{2,3},{3,4},{4,5},{5,6},{6,7},{7,8},{8,9},{9,10},{10,1... | collective-permute-start | bytes 3080 | tf_op jit(solution)/shard_map/ppermute | solution.py:710
  35.2 3.9 %collective-permute-start.3 = (f32[1,256]{1,0:T(1,128)}, f32[1,256]{1,0:T(1,128)S(1)}, u32[]{:S(2)}, u32[]{:S(2)}) collective-permute-start(f32[1,256]{1,0:T(1,128)} %get-tuple-element.28), channel_id=1, source_target_pairs={{1,0},{2,1},{3,2},{4,3},{5,4},{6,5},{7,6},{8,7},{9,8},{10,9},{11,1... | collective-permute-start | bytes 3080 | tf_op jit(solution)/shard_map/ppermute | solution.py:711
  39.1 6.0 %predictor.1 = (f32[128,16,256]{2,1,0:T(8,128)}, bf16[128,256]{1,0:T(8,128)(2,1)}, bf16[128,256]{1,0:T(8,128)(2,1)}) custom-call(f32[128,16,256]{2,1,0:T(8,128)} %flow_ref.7, f32[128,16,256]{2,1,0:T(8,128)} %flow_ref.7, f32[128,16,256]{2,1,0:T(8,128)} %flow_ref.7, bf16[384,256]{1,0:T(8,128)(2,1)} %copy-done, bf16[384,256]{1,0:T(8,128)(2,1)} %copy-done.1, ...), custom_call_target="tpu_custom_call" | custom-call | flops 20971520 | bytes 8388608 | tf_op jit(solution)/shard_map/predictor/pallas_call | solution.py:371
  45.1 0.0 collective-permute-done.2.low_ref.top_low_ref
  45.1 0.0 copy-start.6
  45.1 0.0 collective-permute-done.3.high_ref.top_high_ref
  45.1 0.0 copy-start.7
  45.1 0.5 copy-done.6
  45.6 0.0 copy-done.7
  45.6 0.0 copy-start.9
  45.6 0.0 copy-start.8
  45.6 7.2 %backward.1 = s16[32,24,256]{2,1,0:T(8,128)(2,1)} custom-call(s32[1,4096]{1,0:T(1,128)} %bitcast.10, s32[1,4096]{1,0:T(1,128)} %bitcast.12, s32[1,4096]{1,0:T(1,128)} %bitcast.14, f32[256,4096]{1,0:T(8,128)} %weights.1.weights_ref, f32[16,256]{1,0:T(8,128)} %get-tuple-element.25.wall_ref, f32[2,16,256]{2,1,0:T(8,128)} %get-tuple-element.32.top_ref, ...), custom_call_target="tpu_custom_call" | custom-call | flops 3221225472 | bytes 4194304 | tf_op jit(solution)/shard_map/backward/pallas_call | solution.py:529
  52.8 2.6 %all-to-all-start.1 = ((s16[32,24,256]{2,1,0:T(8,128)(2,1)}), s16[32,24,256]{2,1,0:T(8,128)(2,1)S(1)}, u32[]{:S(2)}, u32[]{:S(2)}) async-start(s16[32,24,256]{2,1,0:T(8,128)(2,1)} %backward.1), calls=%async_computation.1 | async-start | bytes 786432 | tf_op jit(solution)/shard_map/all_to_all | solution.py:734
  55.4 0.0 copy-done.9
  55.4 1.7 %collective-permute-start.4 = (bf16[128,256]{1,0:T(8,128)(2,1)S(1)}, bf16[128,256]{1,0:T(8,128)(2,1)S(1)}, u32[]{:S(2)}, u32[]{:S(2)}) collective-permute-start(bf16[128,256]{1,0:T(8,128)(2,1)S(1)} %copy-done.9), channel_id=1, source_target_pairs={{0,1},{1,2},{2,3},{3,4},{4,5},{5,6},{6,7},{7,8},{8,9},{9,10},{10,1... | collective-permute-start | bytes 196616 | tf_op jit(solution)/shard_map/ppermute | solution.py:715
  57.1 0.0 copy-done.8
  57.1 3.8 %collective-permute-start.5 = (bf16[128,256]{1,0:T(8,128)(2,1)S(1)}, bf16[128,256]{1,0:T(8,128)(2,1)S(1)}, u32[]{:S(2)}, u32[]{:S(2)}) collective-permute-start(bf16[128,256]{1,0:T(8,128)(2,1)S(1)} %copy-done.8), channel_id=1, source_target_pairs={{1,0},{2,1},{3,2},{4,3},{5,4},{6,5},{7,6},{8,7},{9,8},{10,9},{11,1... | collective-permute-start | bytes 196616 | tf_op jit(solution)/shard_map/ppermute | solution.py:716
  61.0 3.8 %liner.1.rest_ref = f32[32,16,256]{2,1,0:T(8,128)} custom-call(f32[32,16,256]{2,1,0:T(8,128)} %solid_ref.5, f32[32,16,256]{2,1,0:T(8,128)} %rates_ref.5, bf16[384,256]{1,0:T(8,128)(2,1)} %copy-done, bf16[384,256]{1,0:T(8,128)(2,1)} %copy-done.1), custom_call_target="tpu_custom_call" | custom-call | flops 11010048 | bytes 2359296 | tf_op jit(solution)/shard_map/liner/pallas_call | solution.py:617
  64.7 4.5 %collective-permute-done.4.low_ref = bf16[128,256]{1,0:T(8,128)(2,1)S(1)} collective-permute-done((bf16[128,256]{1,0:T(8,128)(2,1)S(1)}, bf16[128,256]{1,0:T(8,128)(2,1)S(1)}, u32[]{:S(2)}, u32[]{:S(2)}) %collective-permute-start.4) | collective-permute-done | bytes 65568 | tf_op jit(solution)/shard_map/ppermute | solution.py:715
  69.2 0.0 copy-start.4
  69.2 0.0 collective-permute-done.5.high_ref
  69.2 0.0 copy-start.5
  69.2 0.6 copy-done.4
  69.9 0.0 copy-done.5
  69.9 6.4 %corrector.1 = f32[128,16,256]{2,1,0:T(8,128)} custom-call(f32[128,16,256]{2,1,0:T(8,128)} %get-tuple-element.24.below_ref.mid_ref.above_ref, f32[128,16,256]{2,1,0:T(8,128)} %get-tuple-element.24.below_ref.mid_ref.above_ref, f32[128,16,256]{2,1,0:T(8,128)} %get-tuple-element.24.below_ref.mid_ref.above_ref, f32[2,16,256]{2,1,0:T(8,128)} %get-tuple-element.32.top_ref, ...), custom_call_target="tpu_custom_call" | custom-call | flops 23068672 | bytes 10485760 | tf_op jit(solution)/shard_map/corrector/pallas_call | solution.py:431
  76.2 0.0 all-to-all-done.1.arrived_ref
  76.2 0.0 copy-start.2
  76.3 0.7 copy-done.2
  77.0 2.2 %liner_top.1 = f32[32,16,256]{2,1,0:T(8,128)} custom-call(s16[32,24,256]{2,1,0:T(8,128)(2,1)} %copy-done.2, f32[32,16,256]{2,1,0:T(8,128)} %solid_ref.5, f32[32,16,256]{2,1,0:T(8,128)} %rates_ref.5, bf16[384,256]{1,0:T(8,128)(2,1)} %copy-done, bf16[384,256]{1,0:T(8,128)(2,1)} %copy-done.1, f32[32,16,256]{2,1,0:T(8,128)} %liner.1.rest_ref), custom_call_target="tpu_custom_call", output_to_operand_aliasing={{}: (5, {})} | custom-call | flops 2949120 | bytes 393216 | tf_op jit(solution)/shard_map/liner_top/pallas_call | solution.py:656
Async XLA Ops:
  2.1 23.6 %all-to-all-start = ((s16[32,16,256]{2,1,0:T(8,128)(2,1)}), s16[32,16,256]{2,1,0:T(8,128)(2,1)S(1)}, u32[]{:S(2)}, u32[]{:S(2)}) async-start(s16[32,16,256]{2,1,0:T(8,128)(2,1)} %broadcast_in_dim.21), calls=%async_computation | async-start | bytes 524288 | tf_op jit(solution)/shard_map/all_to_all | solution.py:695
  12.1 12.9 %collective-permute-start = (bf16[384,256]{1,0:T(8,128)(2,1)}, bf16[384,256]{1,0:T(8,128)(2,1)S(1)}, u32[]{:S(2)}, u32[]{:S(2)}) collective-permute-start(bf16[384,256]{1,0:T(8,128)(2,1)} %get-tuple-element.19), channel_id=1, source_target_pairs={{0,1},{1,2},{2,3},{3,4},{4,5},{5,6},{6,7},{7,8},{8,9},{9,10},{10,1... | collective-permute-start | bytes 589832 | tf_op jit(solution)/shard_map/ppermute | solution.py:699
  13.9 11.8 %collective-permute-start.1 = (bf16[384,256]{1,0:T(8,128)(2,1)}, bf16[384,256]{1,0:T(8,128)(2,1)S(1)}, u32[]{:S(2)}, u32[]{:S(2)}) collective-permute-start(bf16[384,256]{1,0:T(8,128)(2,1)} %get-tuple-element.20), channel_id=1, source_target_pairs={{1,0},{2,1},{3,2},{4,3},{5,4},{6,5},{7,6},{8,7},{9,8},{10,9},{11,1... | collective-permute-start | bytes 589832 | tf_op jit(solution)/shard_map/ppermute | solution.py:700
  25.0 0.7 copy-start
  25.6 0.7 copy-start.1
  25.6 0.8 copy-start.3
  33.7 11.4 %collective-permute-start.2 = (f32[1,256]{1,0:T(1,128)}, f32[1,256]{1,0:T(1,128)S(1)}, u32[]{:S(2)}, u32[]{:S(2)}) collective-permute-start(f32[1,256]{1,0:T(1,128)} %get-tuple-element.27), channel_id=1, source_target_pairs={{0,1},{1,2},{2,3},{3,4},{4,5},{5,6},{6,7},{7,8},{8,9},{9,10},{10,1... | collective-permute-start | bytes 3080 | tf_op jit(solution)/shard_map/ppermute | solution.py:710
  35.2 9.9 %collective-permute-start.3 = (f32[1,256]{1,0:T(1,128)}, f32[1,256]{1,0:T(1,128)S(1)}, u32[]{:S(2)}, u32[]{:S(2)}) collective-permute-start(f32[1,256]{1,0:T(1,128)} %get-tuple-element.28), channel_id=1, source_target_pairs={{1,0},{2,1},{3,2},{4,3},{5,4},{6,5},{7,6},{8,7},{9,8},{10,9},{11,1... | collective-permute-start | bytes 3080 | tf_op jit(solution)/shard_map/ppermute | solution.py:711
  45.1 0.6 copy-start.6
  45.1 0.6 copy-start.7
  45.6 9.8 %copy-start.9 = (bf16[128,256]{1,0:T(8,128)(2,1)S(1)}, bf16[128,256]{1,0:T(8,128)(2,1)}, u32[]{:S(2)}) copy-start(bf16[128,256]{1,0:T(8,128)(2,1)} %get-tuple-element.33) | copy-start | bytes 196612
  45.6 11.5 %copy-start.8 = (bf16[128,256]{1,0:T(8,128)(2,1)S(1)}, bf16[128,256]{1,0:T(8,128)(2,1)}, u32[]{:S(2)}) copy-start(bf16[128,256]{1,0:T(8,128)(2,1)} %get-tuple-element.29) | copy-start | bytes 196612
  52.8 23.4 %all-to-all-start.1 = ((s16[32,24,256]{2,1,0:T(8,128)(2,1)}), s16[32,24,256]{2,1,0:T(8,128)(2,1)S(1)}, u32[]{:S(2)}, u32[]{:S(2)}) async-start(s16[32,24,256]{2,1,0:T(8,128)(2,1)} %backward.1), calls=%async_computation.1 | async-start | bytes 786432 | tf_op jit(solution)/shard_map/all_to_all | solution.py:734
  55.4 13.8 %collective-permute-start.4 = (bf16[128,256]{1,0:T(8,128)(2,1)S(1)}, bf16[128,256]{1,0:T(8,128)(2,1)S(1)}, u32[]{:S(2)}, u32[]{:S(2)}) collective-permute-start(bf16[128,256]{1,0:T(8,128)(2,1)S(1)} %copy-done.9), channel_id=1, source_target_pairs={{0,1},{1,2},{2,3},{3,4},{4,5},{5,6},{6,7},{7,8},{8,9},{9,10},{10,1... | collective-permute-start | bytes 196616 | tf_op jit(solution)/shard_map/ppermute | solution.py:715
  57.1 12.1 %collective-permute-start.5 = (bf16[128,256]{1,0:T(8,128)(2,1)S(1)}, bf16[128,256]{1,0:T(8,128)(2,1)S(1)}, u32[]{:S(2)}, u32[]{:S(2)}) collective-permute-start(bf16[128,256]{1,0:T(8,128)(2,1)S(1)} %copy-done.8), channel_id=1, source_target_pairs={{1,0},{2,1},{3,2},{4,3},{5,4},{6,5},{7,6},{8,7},{9,8},{10,9},{11,1... | collective-permute-start | bytes 196616 | tf_op jit(solution)/shard_map/ppermute | solution.py:716
  69.2 0.6 copy-start.4
  69.2 0.6 copy-start.5
  76.2 0.8 copy-start.2

commit v3 on v2

--- a/solution.py
+++ b/solution.py
@@ -24,7 +24,7 @@
 HALO = 4
 F32 = jnp.float32
 BF16 = jnp.bfloat16
-VMEM_LIMIT = 58 * 1024 * 1024
+VMEM_LIMIT = 63 * 1000 * 1000
 STEPS_PER_UNIT = 5461.0
 I16 = jnp.int16
 
@@ -38,18 +38,8 @@
 
 
 def one_hot(index, rows):
-    count = index.shape[1]
-    wide = jnp.broadcast_to(index, (NODES, count))
-    cells = lax.broadcasted_iota(jnp.int32, (NODES, count), 0)
-    inner = min(rows, 128)
-    low = wide % inner
-    high = wide // inner
-    parts = [jnp.where(cells + g == low, 1.0, 0.0).astype(BF16) for g in range(0, inner, NODES)]
-    out = []
-    for h in range(-(-rows // inner)):
-        mask = jnp.where(high == h, 1.0, 0.0).astype(BF16)
-        out.extend([p * mask for p in parts])
-    return jnp.concatenate(out, axis=0)
+    cells = lax.broadcasted_iota(jnp.int16, (rows, index.shape[1]), 0)
+    return jnp.where(cells == index.astype(jnp.int16), BF16(1), BF16(0))
 
 
 def dot(a, b):
@@ -58,6 +48,16 @@
 
 def dot_nt(a, b):
     return lax.dot_general(a, b, (((1,), (1,)), ((), ())), preferred_element_type=F32)
+
+
+def sides(pair, cross):
+    even = lax.axis_index(AXES[1]) % 2 == 0
+    return jnp.where(even, cross, pair), jnp.where(even, pair, cross)
+
+
+def lots(to_before, to_after):
+    even = lax.axis_index(AXES[1]) % 2 == 0
+    return jnp.where(even, to_after, to_before), jnp.where(even, to_before, to_after)
 
 
 def split(x):
@@ -142,8 +142,8 @@
     flow_p_ref,
     weights_ref,
     faces_ref,
-    edge_low_ref,
-    edge_high_ref,
+    edge_pair_ref,
+    edge_cross_ref,
     under_ref,
     flow_ref,
     velocity_ref,
@@ -188,9 +188,8 @@
         patches = jnp.sum(fold(total[...]).reshape(NODES, NODES, total.shape[1]), axis=1)
         wall = patches_to_face(patches, rows_x)
         wall_ref[...] = wall
-        edge = edge_low_ref.shape[0]
-        lows = edge_low_ref[...].astype(F32)
-        highs = edge_high_ref[...].astype(F32)
+        edge = edge_pair_ref.shape[0]
+        lows, highs = sides(edge_pair_ref[...].astype(F32), edge_cross_ref[...].astype(F32))
         for l in range(2):
             centre = flow_ref[l]
             zlow = under_ref[1] if l == 0 else flow_ref[0]
@@ -201,15 +200,14 @@
             top_ref[l] = centre + TIMESTEP * layer_tendency(
                 centre, zlow, zhigh, xlow, xhigh, vz, vx, vy, heat_ref[l].astype(F32)
             )
-        first_ref[...] = top_ref[1, :1]
-        last_ref[...] = top_ref[1, rows_x - 1 :]
-
-
-def forward(solid_device, solid_patch, flow_p, weights, faces, edge_low, edge_high, flow, velocity, heat):
+        first_ref[...], last_ref[...] = lots(top_ref[1, :1], top_ref[1, rows_x - 1 :])
+
+
+def forward(solid_device, solid_patch, flow_p, weights, faces, edge_pair, edge_cross, flow, velocity, heat):
     entries, count = weights.shape
     tall, width = faces.shape
     layers, rows_x = flow.shape[:2]
-    last = edge_low.shape[0] // LAYERS - 1
+    last = edge_pair.shape[0] // LAYERS - 1
     edge = pl.BlockSpec((LAYERS, width), lambda i: (last, 0))
     pair = pl.BlockSpec((2, rows_x, width), lambda i: (layers // 2 - 1, 0, 0))
     line = pl.BlockSpec((1, CHUNK), lambda i: (0, i))
@@ -246,11 +244,11 @@
         compiler_params=params(),
         cost_estimate=cost(4 * width * (tall + entries) * count, 4 * entries * count),
         name="forward",
-    )(solid_device, solid_patch, flow_p, weights, faces, edge_low, edge_high, flow, flow, velocity, heat)
+    )(solid_device, solid_patch, flow_p, weights, faces, edge_pair, edge_cross, flow, flow, velocity, heat)
 
 
 def edges_kernel(
-    flow_low_ref, flow_high_ref, solid_ref, rates_ref, up_ref, down_ref
+    flow_low_ref, flow_high_ref, solid_ref, rates_ref, pair_ref, cross_ref
 ):
     layers = flow_low_ref.shape[0]
     solid_layers, rows, width = solid_ref.shape
@@ -262,17 +260,18 @@
                 jnp.where(low, pltpu.roll(rates_ref[m, rows - 8 :], HALO, 0), solid_ref[m, rows - 8 :])
             )
             downs.append(jnp.where(low, solid_ref[m, :8], pltpu.roll(rates_ref[m, :8], HALO, 0)))
-        up_ref[l * 8 : l * 8 + 16] = jnp.concatenate(ups, axis=0).astype(BF16)
-        down_ref[l * 8 : l * 8 + 16] = jnp.concatenate(downs, axis=0).astype(BF16)
+        pair, cross = lots(jnp.concatenate(downs, axis=0), jnp.concatenate(ups, axis=0))
+        pair_ref[l * 8 : l * 8 + 16] = pair.astype(BF16)
+        cross_ref[l * 8 : l * 8 + 16] = cross.astype(BF16)
     start = solid_layers * 8
     for l in range(0, layers, LAYERS):
         part = slice(start + l, start + l + LAYERS)
-        up_ref[part] = jnp.concatenate(
-            [flow_high_ref[m, 7:8] for m in range(l, l + LAYERS)], axis=0
-        ).astype(BF16)
-        down_ref[part] = jnp.concatenate(
-            [flow_low_ref[m, 0:1] for m in range(l, l + LAYERS)], axis=0
-        ).astype(BF16)
+        pair, cross = lots(
+            jnp.concatenate([flow_low_ref[m, 0:1] for m in range(l, l + LAYERS)], axis=0),
+            jnp.concatenate([flow_high_ref[m, 7:8] for m in range(l, l + LAYERS)], axis=0),
+        )
+        pair_ref[part] = pair.astype(BF16)
+        cross_ref[part] = cross.astype(BF16)
 
 
 def edges(flow, solid, rates):
@@ -323,11 +322,10 @@
 
 
 def predictor_kernel(
-    below_ref, flow_ref, above_ref, low_ref, high_ref, velocity_ref, heat_ref, out_ref, first_ref, last_ref
+    below_ref, flow_ref, above_ref, pair_ref, cross_ref, velocity_ref, heat_ref, out_ref, first_ref, last_ref
 ):
     step = pl.program_id(0)
-    lows = low_ref[...].astype(F32)
-    highs = high_ref[...].astype(F32)
+    lows, highs = sides(pair_ref[...].astype(F32), cross_ref[...].astype(F32))
     first, last = [], []
     rows = flow_ref.shape[1]
     for l in range(BLOCK):
@@ -348,8 +346,9 @@
         out_ref[l] = value
         first.append(value[0:1])
         last.append(value[rows - 1 : rows])
-    first_ref[...] = jnp.concatenate(first, axis=0).astype(BF16)
-    last_ref[...] = jnp.concatenate(last, axis=0).astype(BF16)
+    pair, cross = lots(jnp.concatenate(first, axis=0), jnp.concatenate(last, axis=0))
+    first_ref[...] = pair.astype(BF16)
+    last_ref[...] = cross.astype(BF16)
 
 
 def layer_specs(shape, halo=True):
@@ -390,10 +389,10 @@
     above_ref,
     top_ref,
     wall_ref,
-    top_low_ref,
-    top_high_ref,
-    low_ref,
-    high_ref,
+    top_pair_ref,
+    top_cross_ref,
+    pair_ref,
+    cross_ref,
     flow_ref,
     velocity_ref,
     heat_ref,
@@ -401,8 +400,7 @@
 ):
     step = pl.program_id(0)
     final = step == pl.num_programs(0) - 1
-    lows = low_ref[...].astype(F32)
-    highs = high_ref[...].astype(F32)
+    lows, highs = sides(pair_ref[...].astype(F32), cross_ref[...].astype(F32))
     for l in range(BLOCK):
         centre = mid_ref[l]
         low_row, high_row = lows[l : l + 1], highs[l : l + 1]
@@ -410,8 +408,9 @@
         if l == BLOCK - 1:
             centre = jnp.where(final, top_ref[1], centre)
             zhigh = jnp.where(final, wall_ref[...], above_ref[0])
-            low_row = jnp.where(final, top_low_ref[...], low_row)
-            high_row = jnp.where(final, top_high_ref[...], high_row)
+            top_low, top_high = sides(top_pair_ref[...], top_cross_ref[...])
+            low_row = jnp.where(final, top_low, low_row)
+            high_row = jnp.where(final, top_high, high_row)
         elif l == BLOCK - 2:
             zhigh = jnp.where(final, top_ref[1], mid_ref[l + 1])
         else:
@@ -447,8 +446,8 @@
     weights_ref,
     wall_ref,
     top_ref,
-    low_ref,
-    high_ref,
+    pair_ref,
+    cross_ref,
     flow_ref,
     velocity_ref,
     heat_ref,
@@ -469,7 +468,7 @@
         wall = wall_ref[...]
         vz, vx, vy = (velocity_ref[d, 0].astype(F32) for d in range(3))
         top = top_ref[1]
-        xlow, xhigh = x_neighbours(top, low_ref[...], high_ref[...])
+        xlow, xhigh = x_neighbours(top, *sides(pair_ref[...], cross_ref[...]))
         slope = layer_tendency(top, top_ref[0], wall, xlow, xhigh, vz, vx, vy, heat_ref[0].astype(F32))
         out = 0.5 * flow_ref[0] + 0.5 * (top + TIMESTEP * slope)
         patches = face_to_patches(FILM_COEFF * (out - wall), rows)
@@ -576,17 +575,17 @@
     return out
 
 
-def rims(low_ref, high_ref, l, width):
+def rims(pair_ref, cross_ref, l, width):
     low = lax.broadcasted_iota(jnp.int32, (8, width), 0) < HALO
-    before = low_ref[l * 8 : l * 8 + 8].astype(F32)
-    after = high_ref[l * 8 : l * 8 + 8].astype(F32)
+    part = slice(l * 8, l * 8 + 8)
+    before, after = sides(pair_ref[part].astype(F32), cross_ref[part].astype(F32))
     return jnp.where(low, after, before), pltpu.roll(jnp.where(low, before, after), HALO, 0)
 
 
-def liner_kernel(solid_ref, rates_ref, low_ref, high_ref, out_ref, first, second, rates):
+def liner_kernel(solid_ref, rates_ref, pair_ref, cross_ref, out_ref, first, second, rates):
     layers, rows, width = solid_ref.shape
     for l in range(layers):
-        solid_rim, rates_rim = rims(low_ref, high_ref, l, width)
+        solid_rim, rates_rim = rims(pair_ref, cross_ref, l, width)
         first[l, :rows] = solid_ref[l]
         first[l, rows:] = solid_rim
         rates[l, :rows] = CONDUCT_RATE * rates_ref[l]
@@ -608,7 +607,7 @@
                 target[l] = value
 
 
-def liner(solid, rates, edge_low, edge_high):
+def liner(solid, rates, edge_pair, edge_cross):
     layers, rows, width = solid.shape
     tall = rows + 8
     cells = layers * tall * width
@@ -624,10 +623,10 @@
         compiler_params=params(),
         cost_estimate=cost(14 * SUBCYCLES * cells, 12 * cells),
         name="liner",
-    )(solid, rates, edge_low, edge_high)
-
-
-def liner_top_kernel(arrived_ref, solid_ref, rates_ref, low_ref, high_ref, rest_ref, out_ref):
+    )(solid, rates, edge_pair, edge_cross)
+
+
+def liner_top_kernel(arrived_ref, solid_ref, rates_ref, pair_ref, cross_ref, rest_ref, out_ref):
     del rest_ref
     depth, rows, width = solid_ref.shape
     mark = rows + HALO - 1
@@ -638,7 +637,7 @@
     flux = FLUX_GAIN * flux
     current, rates = [], []
     for l in range(depth):
-        solid_rim, rates_rim = rims(low_ref, high_ref, l, width)
+        solid_rim, rates_rim = rims(pair_ref, cross_ref, l, width)
         current.append(jnp.concatenate([solid_ref[l], solid_rim], axis=0))
         rates.append(jnp.concatenate([rates_ref[l], rates_rim], axis=0))
     for substep in range(SUBCYCLES):
@@ -647,7 +646,7 @@
         out_ref[l] = current[l][:rows]
 
 
-def liner_top(arrived, solid, rates, edge_low, edge_high, rest):
+def liner_top(arrived, solid, rates, edge_pair, edge_cross, rest):
     rows, width = solid.shape[1:]
     depth = 2 * SUBCYCLES
     top = pl.BlockSpec((depth, rows, width), lambda i: (0, 0, 0))
@@ -670,7 +669,7 @@
         compiler_params=params(),
         cost_estimate=cost(60 * cells, 8 * cells),
         name="liner_top",
-    )(arrived, solid, rates, edge_low, edge_high, rest)
+    )(arrived, solid, rates, edge_pair, edge_cross, rest)
 
 
 def body(
@@ -687,34 +686,34 @@
 ):
     layers, rows, width = flow_temp.shape
     devices = lax.axis_size(AXES)
-    up = [(i, (i + 1) % devices) for i in range(devices)]
-    down = [(j, i) for i, j in up]
+    near = [(i, i + 1 if i % 2 == 0 else i - 1) for i in range(devices)]
+    far = [(i, (i - 1 if i % 2 == 0 else i + 1) % devices) for i in range(devices)]
 
     steps = jnp.round(solid_temp[0] * STEPS_PER_UNIT).astype(I16)
     outgoing = jnp.broadcast_to(steps[None], (devices, rows, width))
     faces = lax.all_to_all(outgoing, AXES, split_axis=0, concat_axis=0, tiled=True)
     faces = faces.reshape(devices * rows, width)
 
-    to_up, to_down = edges(flow_temp, solid_temp, conductivity)
-    before = lax.ppermute(to_up, AXES, up)
-    after = lax.ppermute(to_down, AXES, down)
+    to_pair, to_cross = edges(flow_temp, solid_temp, conductivity)
+    pair = lax.ppermute(to_pair, AXES, near)
+    cross = lax.ppermute(to_cross, AXES, far)
 
     solid_device = solid_device.reshape(1, -1)
     solid_patch = solid_patch[None]
     flow_p = flow_patch[None]
     weights = weights_of(block_index[None], interp_table.reshape(NODES * NODES, -1))
 
-    wall, top, top_first, top_last = forward(
-        solid_device, solid_patch, flow_p, weights, faces, before, after, flow_temp, velocity, heat_release
+    wall, top, to_top_pair, to_top_cross = forward(
+        solid_device, solid_patch, flow_p, weights, faces, pair, cross, flow_temp, velocity, heat_release
     )
-    top_low = lax.ppermute(top_last, AXES, up)
-    top_high = lax.ppermute(top_first, AXES, down)
-
-    before, after, wall = lax.optimization_barrier((before, after, wall))
-    mid, mid_first, mid_last = predictor(flow_temp, before, after, velocity, heat_release)
-    mid_low = lax.ppermute(mid_last, AXES, up)
-    mid_high = lax.ppermute(mid_first, AXES, down)
-    top_low, top_high, mid_first = lax.optimization_barrier((top_low, top_high, mid_first))
+    top_pair = lax.ppermute(to_top_pair, AXES, near)
+    top_cross = lax.ppermute(to_top_cross, AXES, far)
+
+    pair, cross, wall = lax.optimization_barrier((pair, cross, wall))
+    mid, to_mid_pair, to_mid_cross = predictor(flow_temp, pair, cross, velocity, heat_release)
+    mid_pair = lax.ppermute(to_mid_pair, AXES, near)
+    mid_cross = lax.ppermute(to_mid_cross, AXES, far)
+    top_pair, top_cross, to_mid_pair = lax.optimization_barrier((top_pair, top_cross, to_mid_pair))
 
     sending = backward(
         solid_device,
@@ -723,20 +722,22 @@
         weights,
         wall,
         top,
-        top_low,
-        top_high,
+        top_pair,
+        top_cross,
         flow_temp,
         velocity,
         heat_release,
         devices,
     )
-    sending, top, before = lax.optimization_barrier((sending, top, before))
+    sending, top, pair, mid_pair, mid_cross = lax.optimization_barrier(
+        (sending, top, pair, mid_pair, mid_cross)
+    )
     arrived = lax.all_to_all(sending, AXES, split_axis=0, concat_axis=0, tiled=True)
     flow_out = corrector(
-        mid, top, wall, top_low, top_high, mid_low, mid_high, flow_temp, velocity, heat_release
+        mid, top, wall, top_pair, top_cross, mid_pair, mid_cross, flow_temp, velocity, heat_release
     )
-    rest = liner(solid_temp, conductivity, before, after)
-    solid_out = liner_top(arrived, solid_temp, conductivity, before, after, rest)
+    rest = liner(solid_temp, conductivity, pair, cross)
+    solid_out = liner_top(arrived, solid_temp, conductivity, pair, cross, rest)
     return (flow_out, solid_out)
 
 

time: 79.7 us -> 75.8 us (0.951)
  starting transfers between devices: 26.2 us -> 24.5 us
  waiting for transfers between devices: 5.13 us -> 3.69 us
    ppermute x6, waiting for transfers between devices: 5.13 us -> 0.02 us  [the longest x1 0.01 us: body(): pair = lax.ppermute(to_pair, AXES, near)]
    all_to_all x1, waiting for transfers between devices: 0.01 us -> 3.67 us  [body(): lax.all_to_all(sending, AXES, split_axis=0, concat_axis=0, tiled=True)]
    ppermute x6, starting transfers between devices: 16.3 us -> 13 us  [the longest x1 3.72 us: body(): cross = lax.ppermute(to_cross, AXES, far)]
    all_to_all x1, starting transfers between devices: 2.59 us -> 4.22 us  [body(): lax.all_to_all(sending, AXES, split_axis=0, concat_axis=0, tiled=True)]
    unnamed x20 -> x16, local copies, waits for them, and re-layouts: 2.71 us -> 2.13 us
  transfers between devices with their start and end apart: 8 -> 8, of which waited for: 2 -> 1; matrix products, arithmetic and copies ran while one was open for 0% -> 0% of each run, Pallas kernels for 33% -> 44%
where the time goes in v3:
time: 75.8 us; the launch traced here: 75.3 us
  Pallas kernels  42.8 us (56%)
  starting transfers between devices  24.5 us (32%)
  waiting for transfers between devices  3.69 us (5%)
  local copies, waits for them, and re-layouts  2.85 us (4%)
    pallas_call x1, Pallas kernels, weights_of(): pl.pallas_call(weights_kernel, grid=(count // WEIGHT_CHUNK,), in_specs=[p...  7.44 us
    all_to_all x1, starting transfers between devices, body(): lax.all_to_all(outgoing, AXES, split_axis=0, concat_axis=0, tiled=True)  7.3 us
    pallas_call x1, Pallas kernels, forward(): pl.pallas_call(forward_kernel, grid=(count // CHUNK,), in_specs=[line, li...  7.2 us
    pallas_call x1, Pallas kernels, backward(): pl.pallas_call(backward_kernel, grid=(count // CHUNK,), in_specs=[line, l...  7.01 us
    pallas_call x1, Pallas kernels, corrector(): pl.pallas_call(corrector_kernel, grid=(layers // BLOCK,), in_specs=[below...  6.4 us
    pallas_call x1, Pallas kernels, predictor(): pl.pallas_call(predictor_kernel, grid=(layers // BLOCK,), in_specs=[below...  6.02 us
    all_to_all x1, starting transfers between devices, body(): lax.all_to_all(sending, AXES, split_axis=0, concat_axis=0, tiled=True)  4.22 us
    pallas_call x1, Pallas kernels, liner(): pl.pallas_call(liner_kernel, grid=(1,), in_specs=[whole, whole, edge, edg...  3.76 us
  transfers between devices with their start and end apart: 8, of which 1 were waited for; matrix products, arithmetic and copies ran while one was open for 0% of the time, Pallas kernels for 44%

profile of v3, /device:TPU:0, one launch (start us, length us, event | category | flops | bytes accessed | tf_op | source)
XLA Modules:
  0.0 75.3 jit_solution(11422242731833947094)
XLA Ops:
  0.6 0.7 fusion
  1.4 0.7 broadcast_in_dim.21
  2.1 7.3 %all-to-all-start = ((s16[32,16,256]{2,1,0:T(8,128)(2,1)}), s16[32,16,256]{2,1,0:T(8,128)(2,1)S(1)}, u32[]{:S(2)}, u32[]{:S(2)}) async-start(s16[32,16,256]{2,1,0:T(8,128)(2,1)} %broadcast_in_dim.21), calls=%async_computation | async-start | bytes 524288 | tf_op jit(solution)/shard_map/all_to_all | solution.py:694
  9.4 2.7 %edges.1 = (bf16[384,256]{1,0:T(8,128)(2,1)}, bf16[384,256]{1,0:T(8,128)(2,1)}) custom-call(f32[128,16,256]{2,1,0:T(8,128)} %flow_ref.7, f32[128,16,256]{2,1,0:T(8,128)} %flow_ref.7, f32[32,16,256]{2,1,0:T(8,128)} %solid_ref.5, f32[32,16,256]{2,1,0:T(8,128)} %rates_ref.5), custom_call_target="tpu_custom_call" | custom-call | flops 786432 | bytes 1179648 | tf_op jit(solution)/shard_map/edges/pallas_call | solution.py:282
  12.1 1.8 %collective-permute-start = (bf16[384,256]{1,0:T(8,128)(2,1)}, bf16[384,256]{1,0:T(8,128)(2,1)S(1)}, u32[]{:S(2)}, u32[]{:S(2)}) collective-permute-start(bf16[384,256]{1,0:T(8,128)(2,1)} %get-tuple-element.21), channel_id=1, source_target_pairs={{0,1},{1,0},{2,3},{3,2},{4,5},{5,4},{6,7},{7,6},{8,9},{9,8},{10,11... | collective-permute-start | bytes 589832 | tf_op jit(solution)/shard_map/ppermute | solution.py:698
  13.9 3.7 %collective-permute-start.1 = (bf16[384,256]{1,0:T(8,128)(2,1)}, bf16[384,256]{1,0:T(8,128)(2,1)S(1)}, u32[]{:S(2)}, u32[]{:S(2)}) collective-permute-start(bf16[384,256]{1,0:T(8,128)(2,1)} %get-tuple-element.22), channel_id=1, source_target_pairs={{0,31},{1,2},{2,1},{3,4},{4,3},{5,6},{6,5},{7,8},{8,7},{9,10},{10,... | collective-permute-start | bytes 589832 | tf_op jit(solution)/shard_map/ppermute | solution.py:699
  17.6 7.4 %weights.1.weights_ref = f32[256,4096]{1,0:T(8,128)} custom-call(s32[1,4096]{1,0:T(1,128)} %bitcast.16, f32[256,1024]{1,0:T(8,128)} %bitcast.15), custom_call_target="tpu_custom_call" | custom-call | flops 4294967296 | bytes 5242880 | tf_op jit(solution)/shard_map/weights/pallas_call | solution.py:89
  25.0 0.0 collective-permute-done.edge_pair_ref.pair_ref
  25.1 0.0 copy-start
  25.1 0.0 collective-permute-done.1.edge_cross_ref.cross_ref
  25.1 0.0 copy-start.1
  25.1 0.0 all-to-all-done
  25.1 0.0 copy-start.3
  25.1 0.6 copy-done
  25.7 0.1 copy-done.1
  25.8 0.1 copy-done.3
  25.9 7.2 %forward.1 = (f32[16,256]{1,0:T(8,128)}, f32[2,16,256]{2,1,0:T(8,128)}, f32[1,256]{1,0:T(1,128)}, f32[1,256]{1,0:T(1,128)}) custom-call(s32[1,4096]{1,0:T(1,128)} %bitcast.9, s32[1,4096]{1,0:T(1,128)} %bitcast.11, s32[1,4096]{1,0:T(1,128)} %bitcast.13, f32[256,4096]{1,0:T(8,128)} %weights.1.weights_ref, s16[512,256]{1,0:T(8,128)(2,1)} %bitcast.8, ...), custom_call_target="tpu_custom_call" | custom-call | flops 3221225472 | bytes 4194304 | tf_op jit(solution)/shard_map/forward/pallas_call | solution.py:215
  33.1 2.1 %collective-permute-start.2 = (f32[1,256]{1,0:T(1,128)}, f32[1,256]{1,0:T(1,128)S(1)}, u32[]{:S(2)}, u32[]{:S(2)}) collective-permute-start(f32[1,256]{1,0:T(1,128)} %get-tuple-element.29), channel_id=1, source_target_pairs={{0,1},{1,0},{2,3},{3,2},{4,5},{5,4},{6,7},{7,6},{8,9},{9,8},{10,11... | collective-permute-start | bytes 3080 | tf_op jit(solution)/shard_map/ppermute | solution.py:709
  35.2 1.8 %collective-permute-start.3 = (f32[1,256]{1,0:T(1,128)}, f32[1,256]{1,0:T(1,128)S(1)}, u32[]{:S(2)}, u32[]{:S(2)}) collective-permute-start(f32[1,256]{1,0:T(1,128)} %get-tuple-element.30), channel_id=1, source_target_pairs={{0,31},{1,2},{2,1},{3,4},{4,3},{5,6},{6,5},{7,8},{8,7},{9,10},{10,... | collective-permute-start | bytes 3080 | tf_op jit(solution)/shard_map/ppermute | solution.py:710
  37.0 6.0 %predictor.1 = (f32[128,16,256]{2,1,0:T(8,128)}, bf16[128,256]{1,0:T(8,128)(2,1)}, bf16[128,256]{1,0:T(8,128)(2,1)}) custom-call(f32[128,16,256]{2,1,0:T(8,128)} %flow_ref.7, f32[128,16,256]{2,1,0:T(8,128)} %flow_ref.7, f32[128,16,256]{2,1,0:T(8,128)} %flow_ref.7, bf16[384,256]{1,0:T(8,128)(2,1)} %copy-done, bf16[384,256]{1,0:T(8,128)(2,1)} %copy-done.1, ...), custom_call_target="tpu_custom_call" | custom-call | flops 20971520 | bytes 8388608 | tf_op jit(solution)/shard_map/predictor/pallas_call | solution.py:370
  43.0 3.6 %collective-permute-start.5 = (bf16[128,256]{1,0:T(8,128)(2,1)}, bf16[128,256]{1,0:T(8,128)(2,1)S(1)}, u32[]{:S(2)}, u32[]{:S(2)}) collective-permute-start(bf16[128,256]{1,0:T(8,128)(2,1)} %get-tuple-element.34), channel_id=1, source_target_pairs={{0,31},{1,2},{2,1},{3,4},{4,3},{5,6},{6,5},{7,8},{8,7},{9,10},{10,... | collective-permute-start | bytes 196616 | tf_op jit(solution)/shard_map/ppermute | solution.py:715
  46.6 0.0 collective-permute-start.4
  46.6 0.0 collective-permute-done.2.pair_ref.top_pair_ref
  46.6 0.0 copy-start.6
  46.6 0.0 collective-permute-done.3.cross_ref.top_cross_ref
  46.6 0.0 copy-start.7
  46.6 0.6 copy-done.6
  47.2 0.0 copy-done.7
  47.2 7.0 %backward.1 = s16[32,24,256]{2,1,0:T(8,128)(2,1)} custom-call(s32[1,4096]{1,0:T(1,128)} %bitcast.10, s32[1,4096]{1,0:T(1,128)} %bitcast.12, s32[1,4096]{1,0:T(1,128)} %bitcast.14, f32[256,4096]{1,0:T(8,128)} %weights.1.weights_ref, f32[16,256]{1,0:T(8,128)} %get-tuple-element.27.wall_ref, f32[2,16,256]{2,1,0:T(8,128)} %get-tuple-element.35.top_ref, ...), custom_call_target="tpu_custom_call" | custom-call | flops 3221225472 | bytes 4194304 | tf_op jit(solution)/shard_map/backward/pallas_call | solution.py:528
  54.2 0.0 collective-permute-done.5.cross_ref
  54.2 0.0 copy-start.4
  54.2 0.0 collective-permute-done.4.pair_ref
  54.2 0.0 copy-start.5
  54.2 4.2 %all-to-all-start.1 = ((s16[32,24,256]{2,1,0:T(8,128)(2,1)}), s16[32,24,256]{2,1,0:T(8,128)(2,1)S(1)}, u32[]{:S(2)}, u32[]{:S(2)}) async-start(s16[32,24,256]{2,1,0:T(8,128)(2,1)} %backward.1), calls=%async_computation.1 | async-start | bytes 786432 | tf_op jit(solution)/shard_map/all_to_all | solution.py:735
  58.5 3.8 %liner.1.rest_ref = f32[32,16,256]{2,1,0:T(8,128)} custom-call(f32[32,16,256]{2,1,0:T(8,128)} %solid_ref.5, f32[32,16,256]{2,1,0:T(8,128)} %rates_ref.5, bf16[384,256]{1,0:T(8,128)(2,1)} %copy-done, bf16[384,256]{1,0:T(8,128)(2,1)} %copy-done.1), custom_call_target="tpu_custom_call" | custom-call | flops 11010048 | bytes 2359296 | tf_op jit(solution)/shard_map/liner/pallas_call | solution.py:616
  62.2 0.0 copy-done.4
  62.2 0.0 copy-done.5
  62.2 6.4 %corrector.1 = f32[128,16,256]{2,1,0:T(8,128)} custom-call(f32[128,16,256]{2,1,0:T(8,128)} %get-tuple-element.26.below_ref.mid_ref.above_ref, f32[128,16,256]{2,1,0:T(8,128)} %get-tuple-element.26.below_ref.mid_ref.above_ref, f32[128,16,256]{2,1,0:T(8,128)} %get-tuple-element.26.below_ref.mid_ref.above_ref, f32[2,16,256]{2,1,0:T(8,128)} %get-tuple-element.35.top_ref, ...), custom_call_target="tpu_custom_call" | custom-call | flops 23068672 | bytes 10485760 | tf_op jit(solution)/shard_map/corrector/pallas_call | solution.py:430
  68.6 3.7 %all-to-all-done.1.arrived_ref = s16[32,24,256]{2,1,0:T(8,128)(2,1)S(1)} async-done(((s16[32,24,256]{2,1,0:T(8,128)(2,1)}), s16[32,24,256]{2,1,0:T(8,128)(2,1)S(1)}, u32[]{:S(2)}, u32[]{:S(2)}) %all-to-all-start.1) | async-done | bytes 393248 | tf_op jit(solution)/shard_map/all_to_all | solution.py:735
  72.3 0.0 copy-start.2
  72.3 0.8 copy-done.2
  73.1 2.2 %liner_top.1 = f32[32,16,256]{2,1,0:T(8,128)} custom-call(s16[32,24,256]{2,1,0:T(8,128)(2,1)} %copy-done.2, f32[32,16,256]{2,1,0:T(8,128)} %solid_ref.5, f32[32,16,256]{2,1,0:T(8,128)} %rates_ref.5, bf16[384,256]{1,0:T(8,128)(2,1)} %copy-done, bf16[384,256]{1,0:T(8,128)(2,1)} %copy-done.1, f32[32,16,256]{2,1,0:T(8,128)} %liner.1.rest_ref), custom_call_target="tpu_custom_call", output_to_operand_aliasing={{}: (5, {})} | custom-call | flops 2949120 | bytes 393216 | tf_op jit(solution)/shard_map/liner_top/pallas_call | solution.py:655
Async XLA Ops:
  2.1 23.0 %all-to-all-start = ((s16[32,16,256]{2,1,0:T(8,128)(2,1)}), s16[32,16,256]{2,1,0:T(8,128)(2,1)S(1)}, u32[]{:S(2)}, u32[]{:S(2)}) async-start(s16[32,16,256]{2,1,0:T(8,128)(2,1)} %broadcast_in_dim.21), calls=%async_computation | async-start | bytes 524288 | tf_op jit(solution)/shard_map/all_to_all | solution.py:694
  12.1 12.9 %collective-permute-start = (bf16[384,256]{1,0:T(8,128)(2,1)}, bf16[384,256]{1,0:T(8,128)(2,1)S(1)}, u32[]{:S(2)}, u32[]{:S(2)}) collective-permute-start(bf16[384,256]{1,0:T(8,128)(2,1)} %get-tuple-element.21), channel_id=1, source_target_pairs={{0,1},{1,0},{2,3},{3,2},{4,5},{5,4},{6,7},{7,6},{8,9},{9,8},{10,11... | collective-permute-start | bytes 589832 | tf_op jit(solution)/shard_map/ppermute | solution.py:698
  13.9 11.2 %collective-permute-start.1 = (bf16[384,256]{1,0:T(8,128)(2,1)}, bf16[384,256]{1,0:T(8,128)(2,1)S(1)}, u32[]{:S(2)}, u32[]{:S(2)}) collective-permute-start(bf16[384,256]{1,0:T(8,128)(2,1)} %get-tuple-element.22), channel_id=1, source_target_pairs={{0,31},{1,2},{2,1},{3,4},{4,3},{5,6},{6,5},{7,8},{8,7},{9,10},{10,... | collective-permute-start | bytes 589832 | tf_op jit(solution)/shard_map/ppermute | solution.py:699
  25.1 0.7 copy-start
  25.1 0.8 %copy-start.1 = (bf16[384,256]{1,0:T(8,128)(2,1)}, bf16[384,256]{1,0:T(8,128)(2,1)S(1)}, u32[]{:S(2)}) copy-start(bf16[384,256]{1,0:T(8,128)(2,1)S(1)} %collective-permute-done.1.edge_cross_ref.cross_ref) | copy-start | bytes 589828
  25.1 0.8 %copy-start.3 = (s16[32,16,256]{2,1,0:T(8,128)(2,1)}, s16[32,16,256]{2,1,0:T(8,128)(2,1)S(1)}, u32[]{:S(2)}) copy-start(s16[32,16,256]{2,1,0:T(8,128)(2,1)S(1)} %all-to-all-done) | copy-start | bytes 786436
  33.1 13.5 %collective-permute-start.2 = (f32[1,256]{1,0:T(1,128)}, f32[1,256]{1,0:T(1,128)S(1)}, u32[]{:S(2)}, u32[]{:S(2)}) collective-permute-start(f32[1,256]{1,0:T(1,128)} %get-tuple-element.29), channel_id=1, source_target_pairs={{0,1},{1,0},{2,3},{3,2},{4,5},{5,4},{6,7},{7,6},{8,9},{9,8},{10,11... | collective-permute-start | bytes 3080 | tf_op jit(solution)/shard_map/ppermute | solution.py:709
  35.2 11.4 %collective-permute-start.3 = (f32[1,256]{1,0:T(1,128)}, f32[1,256]{1,0:T(1,128)S(1)}, u32[]{:S(2)}, u32[]{:S(2)}) collective-permute-start(f32[1,256]{1,0:T(1,128)} %get-tuple-element.30), channel_id=1, source_target_pairs={{0,31},{1,2},{2,1},{3,4},{4,3},{5,6},{6,5},{7,8},{8,7},{9,10},{10,... | collective-permute-start | bytes 3080 | tf_op jit(solution)/shard_map/ppermute | solution.py:710
  43.0 11.2 %collective-permute-start.5 = (bf16[128,256]{1,0:T(8,128)(2,1)}, bf16[128,256]{1,0:T(8,128)(2,1)S(1)}, u32[]{:S(2)}, u32[]{:S(2)}) collective-permute-start(bf16[128,256]{1,0:T(8,128)(2,1)} %get-tuple-element.34), channel_id=1, source_target_pairs={{0,31},{1,2},{2,1},{3,4},{4,3},{5,6},{6,5},{7,8},{8,7},{9,10},{10,... | collective-permute-start | bytes 196616 | tf_op jit(solution)/shard_map/ppermute | solution.py:715
  46.6 7.6 %collective-permute-start.4 = (bf16[128,256]{1,0:T(8,128)(2,1)}, bf16[128,256]{1,0:T(8,128)(2,1)S(1)}, u32[]{:S(2)}, u32[]{:S(2)}) collective-permute-start(bf16[128,256]{1,0:T(8,128)(2,1)} %get-tuple-element.31), channel_id=1, source_target_pairs={{0,1},{1,0},{2,3},{3,2},{4,5},{5,4},{6,7},{7,6},{8,9},{9,8},{10,11... | collective-permute-start | bytes 196616 | tf_op jit(solution)/shard_map/ppermute | solution.py:714
  46.6 0.6 copy-start.6
  46.6 0.6 copy-start.7
  54.2 8.0 %copy-start.4 = (bf16[128,256]{1,0:T(8,128)(2,1)}, bf16[128,256]{1,0:T(8,128)(2,1)S(1)}, u32[]{:S(2)}) copy-start(bf16[128,256]{1,0:T(8,128)(2,1)S(1)} %collective-permute-done.5.cross_ref) | copy-start | bytes 196612
  54.2 8.0 %copy-start.5 = (bf16[128,256]{1,0:T(8,128)(2,1)}, bf16[128,256]{1,0:T(8,128)(2,1)S(1)}, u32[]{:S(2)}) copy-start(bf16[128,256]{1,0:T(8,128)(2,1)S(1)} %collective-permute-done.4.pair_ref) | copy-start | bytes 196612
  54.2 18.1 %all-to-all-start.1 = ((s16[32,24,256]{2,1,0:T(8,128)(2,1)}), s16[32,24,256]{2,1,0:T(8,128)(2,1)S(1)}, u32[]{:S(2)}, u32[]{:S(2)}) async-start(s16[32,24,256]{2,1,0:T(8,128)(2,1)} %backward.1), calls=%async_computation.1 | async-start | bytes 786432 | tf_op jit(solution)/shard_map/all_to_all | solution.py:735
  72.3 0.8 copy-start.2

commit v4 on v3

--- a/solution.py
+++ b/solution.py
@@ -29,8 +29,8 @@
 I16 = jnp.int16
 
 
-def params(**kw):
-    return pltpu.CompilerParams(vmem_limit_bytes=VMEM_LIMIT, **kw)
+def params(limit=VMEM_LIMIT):
+    return pltpu.CompilerParams(vmem_limit_bytes=limit)
 
 
 def cost(flops, nbytes):
@@ -666,7 +666,7 @@
         out_specs=pl.BlockSpec((SUBCYCLES, rows, width), lambda i: (0, 0, 0)),
         out_shape=jax.ShapeDtypeStruct(rest.shape, F32),
         input_output_aliases={5: 0},
-        compiler_params=params(),
+        compiler_params=params(16 * 1024 * 1024),
         cost_estimate=cost(60 * cells, 8 * cells),
         name="liner_top",
     )(arrived, solid, rates, edge_pair, edge_cross, rest)

time: 75.8 us -> 74 us (0.976)
  Pallas kernels: 42.8 us -> 41.7 us
    pallas_call x1, Pallas kernels: 2.23 us -> 1.12 us  [liner_top(): pl.pallas_call(liner_top_kernel, grid=(1,), in_specs=[pl.BlockSpec(arrive...]
    unnamed x16 -> x22, local copies, waits for them, and re-layouts: 2.13 us -> 1.41 us
  transfers between devices with their start and end apart: 8 -> 8, of which waited for: 1 -> 1; matrix products, arithmetic and copies ran while one was open for 0% -> 0% of each run, Pallas kernels for 44% -> 46%
where the time goes in v4:
time: 74 us; the launch traced here: 73.4 us
  Pallas kernels  41.7 us (56%)
  starting transfers between devices  24.5 us (33%)
  waiting for transfers between devices  3.55 us (5%)
  local copies, waits for them, and re-layouts  2.13 us (3%)
  between operations  0.77 us (1%)
    pallas_call x1, Pallas kernels, weights_of(): pl.pallas_call(weights_kernel, grid=(count // WEIGHT_CHUNK,), in_specs=[p...  7.42 us
    all_to_all x1, starting transfers between devices, body(): lax.all_to_all(outgoing, AXES, split_axis=0, concat_axis=0, tiled=True)  7.3 us
    pallas_call x1, Pallas kernels, forward(): pl.pallas_call(forward_kernel, grid=(count // CHUNK,), in_specs=[line, li...  7.21 us
    pallas_call x1, Pallas kernels, backward(): pl.pallas_call(backward_kernel, grid=(count // CHUNK,), in_specs=[line, l...  6.99 us
    pallas_call x1, Pallas kernels, corrector(): pl.pallas_call(corrector_kernel, grid=(layers // BLOCK,), in_specs=[below...  6.5 us
    pallas_call x1, Pallas kernels, predictor(): pl.pallas_call(predictor_kernel, grid=(layers // BLOCK,), in_specs=[below...  6 us
    all_to_all x1, starting transfers between devices, body(): lax.all_to_all(sending, AXES, split_axis=0, concat_axis=0, tiled=True)  4.23 us
    pallas_call x1, Pallas kernels, liner(): pl.pallas_call(liner_kernel, grid=(1,), in_specs=[whole, whole, edge, edg...  3.76 us
  transfers between devices with their start and end apart: 8, of which 1 were waited for; matrix products, arithmetic and copies ran while one was open for 0% of the time, Pallas kernels for 46%

profile of v4, /device:TPU:0, one launch (start us, length us, event | category | flops | bytes accessed | tf_op | source)
XLA Modules:
  0.0 73.4 jit_solution(529032747970114232)
XLA Ops:
  0.6 0.7 fusion
  1.4 0.7 broadcast_in_dim.21
  2.1 7.3 %all-to-all-start = ((s16[32,16,256]{2,1,0:T(8,128)(2,1)}), s16[32,16,256]{2,1,0:T(8,128)(2,1)S(1)}, u32[]{:S(2)}, u32[]{:S(2)}) async-start(s16[32,16,256]{2,1,0:T(8,128)(2,1)} %broadcast_in_dim.21), calls=%async_computation | async-start | bytes 524288 | tf_op jit(solution)/shard_map/all_to_all | solution.py:694
  9.4 2.7 %edges.1 = (bf16[384,256]{1,0:T(8,128)(2,1)}, bf16[384,256]{1,0:T(8,128)(2,1)}) custom-call(f32[128,16,256]{2,1,0:T(8,128)} %flow_ref.7, f32[128,16,256]{2,1,0:T(8,128)} %flow_ref.7, f32[32,16,256]{2,1,0:T(8,128)} %solid_ref.5, f32[32,16,256]{2,1,0:T(8,128)} %rates_ref.5), custom_call_target="tpu_custom_call" | custom-call | flops 786432 | bytes 1179648 | tf_op jit(solution)/shard_map/edges/pallas_call | solution.py:282
  12.1 1.8 %collective-permute-start = (bf16[384,256]{1,0:T(8,128)(2,1)}, bf16[384,256]{1,0:T(8,128)(2,1)S(1)}, u32[]{:S(2)}, u32[]{:S(2)}) collective-permute-start(bf16[384,256]{1,0:T(8,128)(2,1)} %get-tuple-element.21), channel_id=1, source_target_pairs={{0,1},{1,0},{2,3},{3,2},{4,5},{5,4},{6,7},{7,6},{8,9},{9,8},{10,11... | collective-permute-start | bytes 589832 | tf_op jit(solution)/shard_map/ppermute | solution.py:698
  13.9 3.7 %collective-permute-start.1 = (bf16[384,256]{1,0:T(8,128)(2,1)}, bf16[384,256]{1,0:T(8,128)(2,1)S(1)}, u32[]{:S(2)}, u32[]{:S(2)}) collective-permute-start(bf16[384,256]{1,0:T(8,128)(2,1)} %get-tuple-element.22), channel_id=1, source_target_pairs={{0,31},{1,2},{2,1},{3,4},{4,3},{5,6},{6,5},{7,8},{8,7},{9,10},{10,... | collective-permute-start | bytes 589832 | tf_op jit(solution)/shard_map/ppermute | solution.py:699
  17.6 7.4 %weights.1.weights_ref = f32[256,4096]{1,0:T(8,128)} custom-call(s32[1,4096]{1,0:T(1,128)} %bitcast.16, f32[256,1024]{1,0:T(8,128)} %bitcast.15), custom_call_target="tpu_custom_call" | custom-call | flops 4294967296 | bytes 5242880 | tf_op jit(solution)/shard_map/weights/pallas_call | solution.py:89
  25.0 0.0 collective-permute-done.edge_pair_ref.pair_ref
  25.0 0.0 copy-start.2
  25.0 0.0 collective-permute-done.1.edge_cross_ref.cross_ref
  25.0 0.0 copy-start.4
  25.1 0.0 all-to-all-done
  25.1 0.0 copy-start.6
  25.1 0.6 copy-done.2
  25.7 0.1 copy-done.4
  25.8 0.1 copy-done.6
  25.9 7.2 %forward.1 = (f32[16,256]{1,0:T(8,128)}, f32[2,16,256]{2,1,0:T(8,128)}, f32[1,256]{1,0:T(1,128)}, f32[1,256]{1,0:T(1,128)}) custom-call(s32[1,4096]{1,0:T(1,128)} %bitcast.9, s32[1,4096]{1,0:T(1,128)} %bitcast.11, s32[1,4096]{1,0:T(1,128)} %bitcast.13, f32[256,4096]{1,0:T(8,128)} %weights.1.weights_ref, s16[512,256]{1,0:T(8,128)(2,1)} %bitcast.8, ...), custom_call_target="tpu_custom_call" | custom-call | flops 3221225472 | bytes 4194304 | tf_op jit(solution)/shard_map/forward/pallas_call | solution.py:215
  33.1 2.1 %collective-permute-start.2 = (f32[1,256]{1,0:T(1,128)}, f32[1,256]{1,0:T(1,128)S(1)}, u32[]{:S(2)}, u32[]{:S(2)}) collective-permute-start(f32[1,256]{1,0:T(1,128)} %get-tuple-element.29), channel_id=1, source_target_pairs={{0,1},{1,0},{2,3},{3,2},{4,5},{5,4},{6,7},{7,6},{8,9},{9,8},{10,11... | collective-permute-start | bytes 3080 | tf_op jit(solution)/shard_map/ppermute | solution.py:709
  35.2 1.8 %collective-permute-start.3 = (f32[1,256]{1,0:T(1,128)}, f32[1,256]{1,0:T(1,128)S(1)}, u32[]{:S(2)}, u32[]{:S(2)}) collective-permute-start(f32[1,256]{1,0:T(1,128)} %get-tuple-element.30), channel_id=1, source_target_pairs={{0,31},{1,2},{2,1},{3,4},{4,3},{5,6},{6,5},{7,8},{8,7},{9,10},{10,... | collective-permute-start | bytes 3080 | tf_op jit(solution)/shard_map/ppermute | solution.py:710
  37.0 6.0 %predictor.1 = (f32[128,16,256]{2,1,0:T(8,128)}, bf16[128,256]{1,0:T(8,128)(2,1)}, bf16[128,256]{1,0:T(8,128)(2,1)}) custom-call(f32[128,16,256]{2,1,0:T(8,128)} %flow_ref.7, f32[128,16,256]{2,1,0:T(8,128)} %flow_ref.7, f32[128,16,256]{2,1,0:T(8,128)} %flow_ref.7, bf16[384,256]{1,0:T(8,128)(2,1)} %copy-done.2, bf16[384,256]{1,0:T(8,128)(2,1)} %copy-done.4, ...), custom_call_target="tpu_custom_call" | custom-call | flops 20971520 | bytes 8388608 | tf_op jit(solution)/shard_map/predictor/pallas_call | solution.py:370
  43.0 3.6 %collective-permute-start.5 = (bf16[128,256]{1,0:T(8,128)(2,1)}, bf16[128,256]{1,0:T(8,128)(2,1)S(1)}, u32[]{:S(2)}, u32[]{:S(2)}) collective-permute-start(bf16[128,256]{1,0:T(8,128)(2,1)} %get-tuple-element.34), channel_id=1, source_target_pairs={{0,31},{1,2},{2,1},{3,4},{4,3},{5,6},{6,5},{7,8},{8,7},{9,10},{10,... | collective-permute-start | bytes 196616 | tf_op jit(solution)/shard_map/ppermute | solution.py:715
  46.6 0.0 collective-permute-start.4
  46.6 0.0 collective-permute-done.2.pair_ref.top_pair_ref
  46.6 0.0 copy-start.9
  46.6 0.0 collective-permute-done.3.cross_ref.top_cross_ref
  46.6 0.0 copy-start.10
  46.6 0.5 copy-done.9
  47.1 0.1 copy-done.10
  47.2 7.0 %backward.1 = s16[32,24,256]{2,1,0:T(8,128)(2,1)} custom-call(s32[1,4096]{1,0:T(1,128)} %bitcast.10, s32[1,4096]{1,0:T(1,128)} %bitcast.12, s32[1,4096]{1,0:T(1,128)} %bitcast.14, f32[256,4096]{1,0:T(8,128)} %weights.1.weights_ref, f32[16,256]{1,0:T(8,128)} %get-tuple-element.27.wall_ref, f32[2,16,256]{2,1,0:T(8,128)} %get-tuple-element.35.top_ref, ...), custom_call_target="tpu_custom_call" | custom-call | flops 3221225472 | bytes 4194304 | tf_op jit(solution)/shard_map/backward/pallas_call | solution.py:528
  54.2 0.0 collective-permute-done.5.cross_ref
  54.2 0.0 copy-start.7
  54.2 0.0 collective-permute-done.4.pair_ref
  54.2 0.0 copy-start.8
  54.2 4.2 %all-to-all-start.1 = ((s16[32,24,256]{2,1,0:T(8,128)(2,1)}), s16[32,24,256]{2,1,0:T(8,128)(2,1)S(1)}, u32[]{:S(2)}, u32[]{:S(2)}) async-start(s16[32,24,256]{2,1,0:T(8,128)(2,1)} %backward.1), calls=%async_computation.1 | async-start | bytes 786432 | tf_op jit(solution)/shard_map/all_to_all | solution.py:735
  58.4 3.8 %liner.1.rest_ref = f32[32,16,256]{2,1,0:T(8,128)} custom-call(f32[32,16,256]{2,1,0:T(8,128)} %solid_ref.5, f32[32,16,256]{2,1,0:T(8,128)} %rates_ref.5, bf16[384,256]{1,0:T(8,128)(2,1)} %copy-done.2, bf16[384,256]{1,0:T(8,128)(2,1)} %copy-done.4), custom_call_target="tpu_custom_call" | custom-call | flops 11010048 | bytes 2359296 | tf_op jit(solution)/shard_map/liner/pallas_call | solution.py:616
  62.2 0.0 copy-done.7
  62.2 0.0 copy-done.8
  62.2 0.0 copy-start
  62.2 0.0 copy-start.1
  62.2 0.0 copy-start.3
  62.2 0.0 copy-start.5
  62.2 6.5 %corrector.1 = f32[128,16,256]{2,1,0:T(8,128)} custom-call(f32[128,16,256]{2,1,0:T(8,128)} %get-tuple-element.26.below_ref.mid_ref.above_ref, f32[128,16,256]{2,1,0:T(8,128)} %get-tuple-element.26.below_ref.mid_ref.above_ref, f32[128,16,256]{2,1,0:T(8,128)} %get-tuple-element.26.below_ref.mid_ref.above_ref, f32[2,16,256]{2,1,0:T(8,128)} %get-tuple-element.35.top_ref, ...), custom_call_target="tpu_custom_call" | custom-call | flops 23068672 | bytes 10485760 | tf_op jit(solution)/shard_map/corrector/pallas_call | solution.py:430
  68.7 3.5 %all-to-all-done.1.arrived_ref = s16[32,24,256]{2,1,0:T(8,128)(2,1)S(1)} async-done(((s16[32,24,256]{2,1,0:T(8,128)(2,1)}), s16[32,24,256]{2,1,0:T(8,128)(2,1)S(1)}, u32[]{:S(2)}, u32[]{:S(2)}) %all-to-all-start.1) | async-done | bytes 393248 | tf_op jit(solution)/shard_map/all_to_all | solution.py:735
  72.3 0.0 copy-done
  72.3 0.0 copy-done.1
  72.3 0.0 copy-done.3
  72.3 0.0 copy-done.5
  72.3 1.1 %liner_top.1 = f32[32,16,256]{2,1,0:T(8,128)} custom-call(s16[32,24,256]{2,1,0:T(8,128)(2,1)S(1)} %all-to-all-done.1.arrived_ref, f32[32,16,256]{2,1,0:T(8,128)S(1)} %copy-done, f32[32,16,256]{2,1,0:T(8,128)S(1)} %copy-done.1, bf16[384,256]{1,0:T(8,128)(2,1)S(1)} %copy-done.3, bf16[384,256]{1,0:T(8,128)(2,1)S(1)} %copy-done.5, ...), custom_call_target="tpu_custom_call", output_to_operand_aliasing={{}: (5, {})} | custom-call | flops 2949120 | bytes 393216 | tf_op jit(solution)/shard_map/liner_top/pallas_call | solution.py:655
Async XLA Ops:
  2.1 23.0 %all-to-all-start = ((s16[32,16,256]{2,1,0:T(8,128)(2,1)}), s16[32,16,256]{2,1,0:T(8,128)(2,1)S(1)}, u32[]{:S(2)}, u32[]{:S(2)}) async-start(s16[32,16,256]{2,1,0:T(8,128)(2,1)} %broadcast_in_dim.21), calls=%async_computation | async-start | bytes 524288 | tf_op jit(solution)/shard_map/all_to_all | solution.py:694
  12.1 12.9 %collective-permute-start = (bf16[384,256]{1,0:T(8,128)(2,1)}, bf16[384,256]{1,0:T(8,128)(2,1)S(1)}, u32[]{:S(2)}, u32[]{:S(2)}) collective-permute-start(bf16[384,256]{1,0:T(8,128)(2,1)} %get-tuple-element.21), channel_id=1, source_target_pairs={{0,1},{1,0},{2,3},{3,2},{4,5},{5,4},{6,7},{7,6},{8,9},{9,8},{10,11... | collective-permute-start | bytes 589832 | tf_op jit(solution)/shard_map/ppermute | solution.py:698
  13.9 11.1 %collective-permute-start.1 = (bf16[384,256]{1,0:T(8,128)(2,1)}, bf16[384,256]{1,0:T(8,128)(2,1)S(1)}, u32[]{:S(2)}, u32[]{:S(2)}) collective-permute-start(bf16[384,256]{1,0:T(8,128)(2,1)} %get-tuple-element.22), channel_id=1, source_target_pairs={{0,31},{1,2},{2,1},{3,4},{4,3},{5,6},{6,5},{7,8},{8,7},{9,10},{10,... | collective-permute-start | bytes 589832 | tf_op jit(solution)/shard_map/ppermute | solution.py:699
  25.0 0.7 copy-start.2
  25.0 0.7 %copy-start.4 = (bf16[384,256]{1,0:T(8,128)(2,1)}, bf16[384,256]{1,0:T(8,128)(2,1)S(1)}, u32[]{:S(2)}) copy-start(bf16[384,256]{1,0:T(8,128)(2,1)S(1)} %collective-permute-done.1.edge_cross_ref.cross_ref) | copy-start | bytes 589828
  25.1 0.8 %copy-start.6 = (s16[32,16,256]{2,1,0:T(8,128)(2,1)}, s16[32,16,256]{2,1,0:T(8,128)(2,1)S(1)}, u32[]{:S(2)}) copy-start(s16[32,16,256]{2,1,0:T(8,128)(2,1)S(1)} %all-to-all-done) | copy-start | bytes 786436
  33.1 13.5 %collective-permute-start.2 = (f32[1,256]{1,0:T(1,128)}, f32[1,256]{1,0:T(1,128)S(1)}, u32[]{:S(2)}, u32[]{:S(2)}) collective-permute-start(f32[1,256]{1,0:T(1,128)} %get-tuple-element.29), channel_id=1, source_target_pairs={{0,1},{1,0},{2,3},{3,2},{4,5},{5,4},{6,7},{7,6},{8,9},{9,8},{10,11... | collective-permute-start | bytes 3080 | tf_op jit(solution)/shard_map/ppermute | solution.py:709
  35.2 11.4 %collective-permute-start.3 = (f32[1,256]{1,0:T(1,128)}, f32[1,256]{1,0:T(1,128)S(1)}, u32[]{:S(2)}, u32[]{:S(2)}) collective-permute-start(f32[1,256]{1,0:T(1,128)} %get-tuple-element.30), channel_id=1, source_target_pairs={{0,31},{1,2},{2,1},{3,4},{4,3},{5,6},{6,5},{7,8},{8,7},{9,10},{10,... | collective-permute-start | bytes 3080 | tf_op jit(solution)/shard_map/ppermute | solution.py:710
  43.0 11.2 %collective-permute-start.5 = (bf16[128,256]{1,0:T(8,128)(2,1)}, bf16[128,256]{1,0:T(8,128)(2,1)S(1)}, u32[]{:S(2)}, u32[]{:S(2)}) collective-permute-start(bf16[128,256]{1,0:T(8,128)(2,1)} %get-tuple-element.34), channel_id=1, source_target_pairs={{0,31},{1,2},{2,1},{3,4},{4,3},{5,6},{6,5},{7,8},{8,7},{9,10},{10,... | collective-permute-start | bytes 196616 | tf_op jit(solution)/shard_map/ppermute | solution.py:715
  46.6 7.6 %collective-permute-start.4 = (bf16[128,256]{1,0:T(8,128)(2,1)}, bf16[128,256]{1,0:T(8,128)(2,1)S(1)}, u32[]{:S(2)}, u32[]{:S(2)}) collective-permute-start(bf16[128,256]{1,0:T(8,128)(2,1)} %get-tuple-element.31), channel_id=1, source_target_pairs={{0,1},{1,0},{2,3},{3,2},{4,5},{5,4},{6,7},{7,6},{8,9},{9,8},{10,11... | collective-permute-start | bytes 196616 | tf_op jit(solution)/shard_map/ppermute | solution.py:714
  46.6 0.5 copy-start.9
  46.6 0.6 copy-start.10
  54.2 8.0 %copy-start.7 = (bf16[128,256]{1,0:T(8,128)(2,1)}, bf16[128,256]{1,0:T(8,128)(2,1)S(1)}, u32[]{:S(2)}) copy-start(bf16[128,256]{1,0:T(8,128)(2,1)S(1)} %collective-permute-done.5.cross_ref) | copy-start | bytes 196612
  54.2 8.0 %copy-start.8 = (bf16[128,256]{1,0:T(8,128)(2,1)}, bf16[128,256]{1,0:T(8,128)(2,1)S(1)}, u32[]{:S(2)}) copy-start(bf16[128,256]{1,0:T(8,128)(2,1)S(1)} %collective-permute-done.4.pair_ref) | copy-start | bytes 196612
  54.2 18.1 %all-to-all-start.1 = ((s16[32,24,256]{2,1,0:T(8,128)(2,1)}), s16[32,24,256]{2,1,0:T(8,128)(2,1)S(1)}, u32[]{:S(2)}, u32[]{:S(2)}) async-start(s16[32,24,256]{2,1,0:T(8,128)(2,1)} %backward.1), calls=%async_computation.1 | async-start | bytes 786432 | tf_op jit(solution)/shard_map/all_to_all | solution.py:735
  62.2 10.1 %copy-start = (f32[32,16,256]{2,1,0:T(8,128)S(1)}, f32[32,16,256]{2,1,0:T(8,128)}, u32[]{:S(2)}) copy-start(f32[32,16,256]{2,1,0:T(8,128)} %solid_ref.5) | copy-start | bytes 1572868
  62.2 10.1 %copy-start.1 = (f32[32,16,256]{2,1,0:T(8,128)S(1)}, f32[32,16,256]{2,1,0:T(8,128)}, u32[]{:S(2)}) copy-start(f32[32,16,256]{2,1,0:T(8,128)} %rates_ref.5) | copy-start | bytes 1572868
  62.2 10.1 %copy-start.3 = (bf16[384,256]{1,0:T(8,128)(2,1)S(1)}, bf16[384,256]{1,0:T(8,128)(2,1)}, u32[]{:S(2)}) copy-start(bf16[384,256]{1,0:T(8,128)(2,1)} %copy-done.2) | copy-start | bytes 589828
  62.2 10.1 %copy-start.5 = (bf16[384,256]{1,0:T(8,128)(2,1)S(1)}, bf16[384,256]{1,0:T(8,128)(2,1)}, u32[]{:S(2)}) copy-start(bf16[384,256]{1,0:T(8,128)(2,1)} %copy-done.4) | copy-start | bytes 589828

commit v5 on v4

--- a/solution.py
+++ b/solution.py
@@ -729,9 +729,7 @@
         heat_release,
         devices,
     )
-    sending, top, pair, mid_pair, mid_cross = lax.optimization_barrier(
-        (sending, top, pair, mid_pair, mid_cross)
-    )
+    sending, top, pair, mid_cross = lax.optimization_barrier((sending, top, pair, mid_cross))
     arrived = lax.all_to_all(sending, AXES, split_axis=0, concat_axis=0, tiled=True)
     flow_out = corrector(
         mid, top, wall, top_pair, top_cross, mid_pair, mid_cross, flow_temp, velocity, heat_release

time: 74 us -> 73.4 us (level)
  waiting for transfers between devices: 3.55 us -> 1.29 us
  starting transfers between devices: 24.5 us -> 25.5 us
    all_to_all x1, waiting for transfers between devices: 3.54 us -> 0.25 us  [body(): lax.all_to_all(sending, AXES, split_axis=0, concat_axis=0, tiled=True)]
    ppermute x1, starting transfers between devices: 0.01 us -> 1.66 us  [body(): mid_pair = lax.ppermute(to_mid_pair, AXES, near)]
    ppermute x1, waiting for transfers between devices: 0.01 us -> 1.02 us  [body(): mid_pair = lax.ppermute(to_mid_pair, AXES, near)]
    unnamed x22 -> x24, local copies, waits for them, and re-layouts: 1.41 us -> 2.02 us
  transfers between devices with their start and end apart: 8 -> 8, of which waited for: 1 -> 2; matrix products, arithmetic and copies ran while one was open for 0% -> 0% of each run, Pallas kernels for 46% -> 46%
where the time goes in v5:
time: 73.4 us; the launch traced here: 72.9 us
  Pallas kernels  41.9 us (57%)
  starting transfers between devices  25.5 us (35%)
  local copies, waits for them, and re-layouts  2.74 us (4%)
  waiting for transfers between devices  1.29 us (2%)
  between operations  0.74 us (1%)
    pallas_call x1, Pallas kernels, weights_of(): pl.pallas_call(weights_kernel, grid=(count // WEIGHT_CHUNK,), in_specs=[p...  7.49 us
    all_to_all x1, starting transfers between devices, body(): lax.all_to_all(outgoing, AXES, split_axis=0, concat_axis=0, tiled=True)  7.3 us
    pallas_call x1, Pallas kernels, forward(): pl.pallas_call(forward_kernel, grid=(count // CHUNK,), in_specs=[line, li...  7.2 us
    pallas_call x1, Pallas kernels, backward(): pl.pallas_call(backward_kernel, grid=(count // CHUNK,), in_specs=[line, l...  7.05 us
    pallas_call x1, Pallas kernels, corrector(): pl.pallas_call(corrector_kernel, grid=(layers // BLOCK,), in_specs=[below...  6.51 us
    pallas_call x1, Pallas kernels, predictor(): pl.pallas_call(predictor_kernel, grid=(layers // BLOCK,), in_specs=[below...  6 us
    pallas_call x1, Pallas kernels, liner(): pl.pallas_call(liner_kernel, grid=(1,), in_specs=[whole, whole, edge, edg...  3.76 us
    ppermute x1, starting transfers between devices, body(): cross = lax.ppermute(to_cross, AXES, far)  3.72 us
  transfers between devices with their start and end apart: 8, of which 2 were waited for; matrix products, arithmetic and copies ran while one was open for 0% of the time, Pallas kernels for 46%

profile of v5, /device:TPU:0, one launch (start us, length us, event | category | flops | bytes accessed | tf_op | source)
XLA Modules:
  0.0 72.9 jit_solution(15836498566118951577)
XLA Ops:
  0.6 0.7 fusion
  1.4 0.7 broadcast_in_dim.21
  2.1 7.3 %all-to-all-start = ((s16[32,16,256]{2,1,0:T(8,128)(2,1)}), s16[32,16,256]{2,1,0:T(8,128)(2,1)S(1)}, u32[]{:S(2)}, u32[]{:S(2)}) async-start(s16[32,16,256]{2,1,0:T(8,128)(2,1)} %broadcast_in_dim.21), calls=%async_computation | async-start | bytes 524288 | tf_op jit(solution)/shard_map/all_to_all | solution.py:694
  9.4 2.8 %edges.1 = (bf16[384,256]{1,0:T(8,128)(2,1)}, bf16[384,256]{1,0:T(8,128)(2,1)}) custom-call(f32[128,16,256]{2,1,0:T(8,128)} %flow_ref.7, f32[128,16,256]{2,1,0:T(8,128)} %flow_ref.7, f32[32,16,256]{2,1,0:T(8,128)} %solid_ref.5, f32[32,16,256]{2,1,0:T(8,128)} %rates_ref.5), custom_call_target="tpu_custom_call" | custom-call | flops 786432 | bytes 1179648 | tf_op jit(solution)/shard_map/edges/pallas_call | solution.py:282
  12.1 1.8 %collective-permute-start = (bf16[384,256]{1,0:T(8,128)(2,1)}, bf16[384,256]{1,0:T(8,128)(2,1)S(1)}, u32[]{:S(2)}, u32[]{:S(2)}) collective-permute-start(bf16[384,256]{1,0:T(8,128)(2,1)} %get-tuple-element.20), channel_id=1, source_target_pairs={{0,1},{1,0},{2,3},{3,2},{4,5},{5,4},{6,7},{7,6},{8,9},{9,8},{10,11... | collective-permute-start | bytes 589832 | tf_op jit(solution)/shard_map/ppermute | solution.py:698
  13.9 3.7 %collective-permute-start.1 = (bf16[384,256]{1,0:T(8,128)(2,1)}, bf16[384,256]{1,0:T(8,128)(2,1)S(1)}, u32[]{:S(2)}, u32[]{:S(2)}) collective-permute-start(bf16[384,256]{1,0:T(8,128)(2,1)} %get-tuple-element.21), channel_id=1, source_target_pairs={{0,31},{1,2},{2,1},{3,4},{4,3},{5,6},{6,5},{7,8},{8,7},{9,10},{10,... | collective-permute-start | bytes 589832 | tf_op jit(solution)/shard_map/ppermute | solution.py:699
  17.6 7.5 %weights.1.weights_ref = f32[256,4096]{1,0:T(8,128)} custom-call(s32[1,4096]{1,0:T(1,128)} %bitcast.16, f32[256,1024]{1,0:T(8,128)} %bitcast.15), custom_call_target="tpu_custom_call" | custom-call | flops 4294967296 | bytes 5242880 | tf_op jit(solution)/shard_map/weights/pallas_call | solution.py:89
  25.1 0.0 collective-permute-done.edge_pair_ref.pair_ref
  25.1 0.0 copy-start.2
  25.1 0.0 collective-permute-done.1.edge_cross_ref.cross_ref
  25.1 0.0 copy-start.4
  25.1 0.0 all-to-all-done
  25.2 0.0 copy-start.6
  25.2 0.7 copy-done.2
  25.8 0.1 copy-done.4
  25.9 0.1 copy-done.6
  26.0 7.2 %forward.1 = (f32[16,256]{1,0:T(8,128)}, f32[2,16,256]{2,1,0:T(8,128)}, f32[1,256]{1,0:T(1,128)}, f32[1,256]{1,0:T(1,128)}) custom-call(s32[1,4096]{1,0:T(1,128)} %bitcast.9, s32[1,4096]{1,0:T(1,128)} %bitcast.11, s32[1,4096]{1,0:T(1,128)} %bitcast.13, f32[256,4096]{1,0:T(8,128)} %weights.1.weights_ref, s16[512,256]{1,0:T(8,128)(2,1)} %bitcast.8, ...), custom_call_target="tpu_custom_call" | custom-call | flops 3221225472 | bytes 4194304 | tf_op jit(solution)/shard_map/forward/pallas_call | solution.py:215
  33.2 2.0 %collective-permute-start.2 = (f32[1,256]{1,0:T(1,128)}, f32[1,256]{1,0:T(1,128)S(1)}, u32[]{:S(2)}, u32[]{:S(2)}) collective-permute-start(f32[1,256]{1,0:T(1,128)} %get-tuple-element.28), channel_id=1, source_target_pairs={{0,1},{1,0},{2,3},{3,2},{4,5},{5,4},{6,7},{7,6},{8,9},{9,8},{10,11... | collective-permute-start | bytes 3080 | tf_op jit(solution)/shard_map/ppermute | solution.py:709
  35.2 1.8 %collective-permute-start.3 = (f32[1,256]{1,0:T(1,128)}, f32[1,256]{1,0:T(1,128)S(1)}, u32[]{:S(2)}, u32[]{:S(2)}) collective-permute-start(f32[1,256]{1,0:T(1,128)} %get-tuple-element.29), channel_id=1, source_target_pairs={{0,31},{1,2},{2,1},{3,4},{4,3},{5,6},{6,5},{7,8},{8,7},{9,10},{10,... | collective-permute-start | bytes 3080 | tf_op jit(solution)/shard_map/ppermute | solution.py:710
  37.0 6.0 %predictor.1 = (f32[128,16,256]{2,1,0:T(8,128)}, bf16[128,256]{1,0:T(8,128)(2,1)}, bf16[128,256]{1,0:T(8,128)(2,1)}) custom-call(f32[128,16,256]{2,1,0:T(8,128)} %flow_ref.7, f32[128,16,256]{2,1,0:T(8,128)} %flow_ref.7, f32[128,16,256]{2,1,0:T(8,128)} %flow_ref.7, bf16[384,256]{1,0:T(8,128)(2,1)} %copy-done.2, bf16[384,256]{1,0:T(8,128)(2,1)} %copy-done.4, ...), custom_call_target="tpu_custom_call" | custom-call | flops 20971520 | bytes 8388608 | tf_op jit(solution)/shard_map/predictor/pallas_call | solution.py:370
  43.0 3.6 %collective-permute-start.4 = (bf16[128,256]{1,0:T(8,128)(2,1)}, bf16[128,256]{1,0:T(8,128)(2,1)S(1)}, u32[]{:S(2)}, u32[]{:S(2)}) collective-permute-start(bf16[128,256]{1,0:T(8,128)(2,1)} %get-tuple-element.33), channel_id=1, source_target_pairs={{0,31},{1,2},{2,1},{3,4},{4,3},{5,6},{6,5},{7,8},{8,7},{9,10},{10,... | collective-permute-start | bytes 196616 | tf_op jit(solution)/shard_map/ppermute | solution.py:715
  46.6 0.0 collective-permute-done.2.pair_ref.top_pair_ref
  46.6 0.0 copy-start.9
  46.6 0.0 collective-permute-done.3.cross_ref.top_cross_ref
  46.6 0.0 copy-start.10
  46.6 0.6 copy-done.9
  47.2 0.0 copy-done.10
  47.2 0.0 copy-start.11
  47.2 7.0 %backward.1 = s16[32,24,256]{2,1,0:T(8,128)(2,1)} custom-call(s32[1,4096]{1,0:T(1,128)} %bitcast.10, s32[1,4096]{1,0:T(1,128)} %bitcast.12, s32[1,4096]{1,0:T(1,128)} %bitcast.14, f32[256,4096]{1,0:T(8,128)} %weights.1.weights_ref, f32[16,256]{1,0:T(8,128)} %get-tuple-element.26.wall_ref, f32[2,16,256]{2,1,0:T(8,128)} %get-tuple-element.34.top_ref, ...), custom_call_target="tpu_custom_call" | custom-call | flops 3221225472 | bytes 4194304 | tf_op jit(solution)/shard_map/backward/pallas_call | solution.py:528
  54.2 0.0 collective-permute-done.4.cross_ref
  54.2 0.0 copy-start.7
  54.2 3.7 %all-to-all-start.1 = ((s16[32,24,256]{2,1,0:T(8,128)(2,1)}), s16[32,24,256]{2,1,0:T(8,128)(2,1)S(1)}, u32[]{:S(2)}, u32[]{:S(2)}) async-start(s16[32,24,256]{2,1,0:T(8,128)(2,1)} %backward.1), calls=%async_computation.1 | async-start | bytes 786432 | tf_op jit(solution)/shard_map/all_to_all | solution.py:733
  57.9 0.0 copy-done.11
  57.9 1.7 %collective-permute-start.5 = (bf16[128,256]{1,0:T(8,128)(2,1)S(1)}, bf16[128,256]{1,0:T(8,128)(2,1)S(1)}, u32[]{:S(2)}, u32[]{:S(2)}) collective-permute-start(bf16[128,256]{1,0:T(8,128)(2,1)S(1)} %copy-done.11), channel_id=1, source_target_pairs={{0,1},{1,0},{2,3},{3,2},{4,5},{5,4},{6,7},{7,6},{8,9},{9,8},{10,11... | collective-permute-start | bytes 196616 | tf_op jit(solution)/shard_map/ppermute | solution.py:714
  59.6 3.8 %liner.1.rest_ref = f32[32,16,256]{2,1,0:T(8,128)} custom-call(f32[32,16,256]{2,1,0:T(8,128)} %solid_ref.5, f32[32,16,256]{2,1,0:T(8,128)} %rates_ref.5, bf16[384,256]{1,0:T(8,128)(2,1)} %copy-done.2, bf16[384,256]{1,0:T(8,128)(2,1)} %copy-done.4), custom_call_target="tpu_custom_call" | custom-call | flops 11010048 | bytes 2359296 | tf_op jit(solution)/shard_map/liner/pallas_call | solution.py:616
  63.3 1.0 %collective-permute-done.5.pair_ref = bf16[128,256]{1,0:T(8,128)(2,1)S(1)} collective-permute-done((bf16[128,256]{1,0:T(8,128)(2,1)S(1)}, bf16[128,256]{1,0:T(8,128)(2,1)S(1)}, u32[]{:S(2)}, u32[]{:S(2)}) %collective-permute-start.5) | collective-permute-done | bytes 65568 | tf_op jit(solution)/shard_map/ppermute | solution.py:714
  64.4 0.0 copy-start.8
  64.4 0.0 copy-done.7
  64.4 0.6 copy-done.8
  65.0 0.0 copy-start
  65.0 0.0 copy-start.1
  65.0 0.0 copy-start.3
  65.0 0.0 copy-start.5
  65.0 6.5 %corrector.1 = f32[128,16,256]{2,1,0:T(8,128)} custom-call(f32[128,16,256]{2,1,0:T(8,128)} %get-tuple-element.25.below_ref.mid_ref.above_ref, f32[128,16,256]{2,1,0:T(8,128)} %get-tuple-element.25.below_ref.mid_ref.above_ref, f32[128,16,256]{2,1,0:T(8,128)} %get-tuple-element.25.below_ref.mid_ref.above_ref, f32[2,16,256]{2,1,0:T(8,128)} %get-tuple-element.34.top_ref, ...), custom_call_target="tpu_custom_call" | custom-call | flops 23068672 | bytes 10485760 | tf_op jit(solution)/shard_map/corrector/pallas_call | solution.py:430
  71.5 0.2 all-to-all-done.1.arrived_ref
  71.8 0.0 copy-done
  71.8 0.0 copy-done.1
  71.8 0.0 copy-done.3
  71.8 0.0 copy-done.5
  71.8 1.1 %liner_top.1 = f32[32,16,256]{2,1,0:T(8,128)} custom-call(s16[32,24,256]{2,1,0:T(8,128)(2,1)S(1)} %all-to-all-done.1.arrived_ref, f32[32,16,256]{2,1,0:T(8,128)S(1)} %copy-done, f32[32,16,256]{2,1,0:T(8,128)S(1)} %copy-done.1, bf16[384,256]{1,0:T(8,128)(2,1)S(1)} %copy-done.3, bf16[384,256]{1,0:T(8,128)(2,1)S(1)} %copy-done.5, ...), custom_call_target="tpu_custom_call", output_to_operand_aliasing={{}: (5, {})} | custom-call | flops 2949120 | bytes 393216 | tf_op jit(solution)/shard_map/liner_top/pallas_call | solution.py:655
Async XLA Ops:
  2.1 23.1 %all-to-all-start = ((s16[32,16,256]{2,1,0:T(8,128)(2,1)}), s16[32,16,256]{2,1,0:T(8,128)(2,1)S(1)}, u32[]{:S(2)}, u32[]{:S(2)}) async-start(s16[32,16,256]{2,1,0:T(8,128)(2,1)} %broadcast_in_dim.21), calls=%async_computation | async-start | bytes 524288 | tf_op jit(solution)/shard_map/all_to_all | solution.py:694
  12.1 13.0 %collective-permute-start = (bf16[384,256]{1,0:T(8,128)(2,1)}, bf16[384,256]{1,0:T(8,128)(2,1)S(1)}, u32[]{:S(2)}, u32[]{:S(2)}) collective-permute-start(bf16[384,256]{1,0:T(8,128)(2,1)} %get-tuple-element.20), channel_id=1, source_target_pairs={{0,1},{1,0},{2,3},{3,2},{4,5},{5,4},{6,7},{7,6},{8,9},{9,8},{10,11... | collective-permute-start | bytes 589832 | tf_op jit(solution)/shard_map/ppermute | solution.py:698
  13.9 11.2 %collective-permute-start.1 = (bf16[384,256]{1,0:T(8,128)(2,1)}, bf16[384,256]{1,0:T(8,128)(2,1)S(1)}, u32[]{:S(2)}, u32[]{:S(2)}) collective-permute-start(bf16[384,256]{1,0:T(8,128)(2,1)} %get-tuple-element.21), channel_id=1, source_target_pairs={{0,31},{1,2},{2,1},{3,4},{4,3},{5,6},{6,5},{7,8},{8,7},{9,10},{10,... | collective-permute-start | bytes 589832 | tf_op jit(solution)/shard_map/ppermute | solution.py:699
  25.1 0.7 copy-start.2
  25.1 0.8 %copy-start.4 = (bf16[384,256]{1,0:T(8,128)(2,1)}, bf16[384,256]{1,0:T(8,128)(2,1)S(1)}, u32[]{:S(2)}) copy-start(bf16[384,256]{1,0:T(8,128)(2,1)S(1)} %collective-permute-done.1.edge_cross_ref.cross_ref) | copy-start | bytes 589828
  25.2 0.8 %copy-start.6 = (s16[32,16,256]{2,1,0:T(8,128)(2,1)}, s16[32,16,256]{2,1,0:T(8,128)(2,1)S(1)}, u32[]{:S(2)}) copy-start(s16[32,16,256]{2,1,0:T(8,128)(2,1)S(1)} %all-to-all-done) | copy-start | bytes 786436
  33.2 13.4 %collective-permute-start.2 = (f32[1,256]{1,0:T(1,128)}, f32[1,256]{1,0:T(1,128)S(1)}, u32[]{:S(2)}, u32[]{:S(2)}) collective-permute-start(f32[1,256]{1,0:T(1,128)} %get-tuple-element.28), channel_id=1, source_target_pairs={{0,1},{1,0},{2,3},{3,2},{4,5},{5,4},{6,7},{7,6},{8,9},{9,8},{10,11... | collective-permute-start | bytes 3080 | tf_op jit(solution)/shard_map/ppermute | solution.py:709
  35.2 11.4 %collective-permute-start.3 = (f32[1,256]{1,0:T(1,128)}, f32[1,256]{1,0:T(1,128)S(1)}, u32[]{:S(2)}, u32[]{:S(2)}) collective-permute-start(f32[1,256]{1,0:T(1,128)} %get-tuple-element.29), channel_id=1, source_target_pairs={{0,31},{1,2},{2,1},{3,4},{4,3},{5,6},{6,5},{7,8},{8,7},{9,10},{10,... | collective-permute-start | bytes 3080 | tf_op jit(solution)/shard_map/ppermute | solution.py:710
  43.0 11.2 %collective-permute-start.4 = (bf16[128,256]{1,0:T(8,128)(2,1)}, bf16[128,256]{1,0:T(8,128)(2,1)S(1)}, u32[]{:S(2)}, u32[]{:S(2)}) collective-permute-start(bf16[128,256]{1,0:T(8,128)(2,1)} %get-tuple-element.33), channel_id=1, source_target_pairs={{0,31},{1,2},{2,1},{3,4},{4,3},{5,6},{6,5},{7,8},{8,7},{9,10},{10,... | collective-permute-start | bytes 196616 | tf_op jit(solution)/shard_map/ppermute | solution.py:715
  46.6 0.6 copy-start.9
  46.6 0.6 copy-start.10
  47.2 10.7 %copy-start.11 = (bf16[128,256]{1,0:T(8,128)(2,1)S(1)}, bf16[128,256]{1,0:T(8,128)(2,1)}, u32[]{:S(2)}) copy-start(bf16[128,256]{1,0:T(8,128)(2,1)} %get-tuple-element.30) | copy-start | bytes 196612
  54.2 10.1 %copy-start.7 = (bf16[128,256]{1,0:T(8,128)(2,1)}, bf16[128,256]{1,0:T(8,128)(2,1)S(1)}, u32[]{:S(2)}) copy-start(bf16[128,256]{1,0:T(8,128)(2,1)S(1)} %collective-permute-done.4.cross_ref) | copy-start | bytes 196612
  54.2 17.5 %all-to-all-start.1 = ((s16[32,24,256]{2,1,0:T(8,128)(2,1)}), s16[32,24,256]{2,1,0:T(8,128)(2,1)S(1)}, u32[]{:S(2)}, u32[]{:S(2)}) async-start(s16[32,24,256]{2,1,0:T(8,128)(2,1)} %backward.1), calls=%async_computation.1 | async-start | bytes 786432 | tf_op jit(solution)/shard_map/all_to_all | solution.py:733
  57.9 6.4 %collective-permute-start.5 = (bf16[128,256]{1,0:T(8,128)(2,1)S(1)}, bf16[128,256]{1,0:T(8,128)(2,1)S(1)}, u32[]{:S(2)}, u32[]{:S(2)}) collective-permute-start(bf16[128,256]{1,0:T(8,128)(2,1)S(1)} %copy-done.11), channel_id=1, source_target_pairs={{0,1},{1,0},{2,3},{3,2},{4,5},{5,4},{6,7},{7,6},{8,9},{9,8},{10,11... | collective-permute-start | bytes 196616 | tf_op jit(solution)/shard_map/ppermute | solution.py:714
  64.4 0.6 copy-start.8
  65.0 6.8 %copy-start = (f32[32,16,256]{2,1,0:T(8,128)S(1)}, f32[32,16,256]{2,1,0:T(8,128)}, u32[]{:S(2)}) copy-start(f32[32,16,256]{2,1,0:T(8,128)} %solid_ref.5) | copy-start | bytes 1572868
  65.0 6.8 %copy-start.1 = (f32[32,16,256]{2,1,0:T(8,128)S(1)}, f32[32,16,256]{2,1,0:T(8,128)}, u32[]{:S(2)}) copy-start(f32[32,16,256]{2,1,0:T(8,128)} %rates_ref.5) | copy-start | bytes 1572868
  65.0 6.8 %copy-start.3 = (bf16[384,256]{1,0:T(8,128)(2,1)S(1)}, bf16[384,256]{1,0:T(8,128)(2,1)}, u32[]{:S(2)}) copy-start(bf16[384,256]{1,0:T(8,128)(2,1)} %copy-done.2) | copy-start | bytes 589828
  65.0 6.8 %copy-start.5 = (bf16[384,256]{1,0:T(8,128)(2,1)S(1)}, bf16[384,256]{1,0:T(8,128)(2,1)}, u32[]{:S(2)}) copy-start(bf16[384,256]{1,0:T(8,128)(2,1)} %copy-done.4) | copy-start | bytes 589828
